TPU v7x, 32 devices: a whole 2x2x4 slice. The times are simulated.
32 devices in a mesh: groups: 2 (over y), shard: 16 (over z, x, core).
Axes of the slice: x: 2, y: 2, z: 4, core: 2. Of those that a mesh axis runs over, the one named last changes fastest.
Arguments:
- queries: bfloat16 [256, 32, 128], P(('groups', 'shard')), parts along dimension 0, may hold values from -6 to 6
- centroids: bfloat16 [16384, 128], P(('groups', 'shard')), parts along dimension 0, may hold values from -0.5 to 0.5
- passages: bfloat16 [4096, 128, 128], P(('groups', 'shard')), parts along dimension 0, may hold values from -0.5 to 0.5
- lengths: int32 [32, 128], P(('groups', 'shard')), parts along dimension 0, may hold values from 1 to 128, 8192 in all within a row
- cand_owner: int32 [256, 16, 1], P(('groups', 'shard')), parts along dimension 0, may hold values from 0 to 15; in each aligned block of 128 rows (0 to 127, 128 to 255, ..., all dimensions but the last counted through in order) at most 16 rows name the same one
- cand_row: int32 [256, 16], P(('groups', 'shard')), parts along dimension 0, may hold values from 0 to 127
Outputs:
- centroid_best: float32 [256, 32], P(('groups', 'shard')), parts along dimension 0
- maxsim: float32 [256, 16], P(('groups', 'shard')), parts along dimension 0
There are 2 independent parts, one for each index of `groups`. A program takes and returns all parts, laid end to end along the dimension named above; each array names one. Nothing has to cross between parts.
Inputs may be any that keep to these rules, and one draw needn't show every extreme that they name: `cand_owner`: among the 128 candidates of the queries of one device, no owner is named more than 16 times, a bound that some block reaches.
All inputs are finite; a program needn't handle non-finite values.
Results may differ from a plain program's by a relative error of at most 0.0003.
Values may be sent and summed in bfloat16 or wider, within the bound.
No kernel may reach another device: no remote copies, remote signals or barrier semaphores. Data moves between devices by JAX's collectives and lax.ppermute only.
A program may use at most 128 MiB of HBM per device.

v0:
```python
import math

import jax
import jax.numpy as jnp
from jax import lax
from jax.sharding import PartitionSpec as P


def body(queries, centroids, passages, lengths, cand_owner, cand_row):
    q_dev, qt, dim = queries.shape
    cent_dev = centroids.shape[0]
    shards = lax.axis_size("shard")
    cblock = math.gcd(cent_dev, 128)
    cent_blocks = centroids.reshape(cent_dev // cblock, cblock, dim)
    piece = lax.all_gather(queries, "shard", axis=0, tiled=True)
    rows = piece.reshape(-1, dim)

    def step(carry, block):
        scores = jnp.einsum("rd,cd->rc", rows, block, preferred_element_type=jnp.float32)
        return (jnp.maximum(carry, jnp.max(scores, axis=1)), None)

    first = jnp.full((rows.shape[0],), -jnp.inf, dtype=jnp.float32)
    result, _ = lax.scan(step, first, cent_blocks)
    partial_best = result.reshape(piece.shape[0], qt)
    whole_best = lax.pmax(partial_best, "shard")
    centroid_best = lax.dynamic_slice_in_dim(whole_best, lax.axis_index("shard") * q_dev, q_dev, 0)
    cand = cand_row.shape[1]
    owners = cand_owner.reshape(-1)
    wanted = cand_row.reshape(-1)
    slot_count = 2 * q_dev * cand // shards
    onehot = (owners[:, None] == jnp.arange(shards, dtype=jnp.int32)[None, :]).astype(jnp.int32)
    ranks = jnp.sum(jnp.cumsum(onehot, axis=0) * onehot, axis=1) - 1
    target = owners * slot_count + ranks
    row_buffer = jnp.zeros((shards * slot_count,), jnp.int32).at[target].set(wanted)
    row_buffer = row_buffer.reshape(shards, slot_count)
    local_len = lengths.reshape(-1)
    asked = lax.all_to_all(row_buffer, "shard", split_axis=0, concat_axis=0, tiled=True)
    sent_blocks = passages[asked]
    sent_len = local_len[asked]
    got_blocks, got_len = (
        lax.all_to_all(sent_blocks, "shard", split_axis=0, concat_axis=0, tiled=True),
        lax.all_to_all(sent_len, "shard", split_axis=0, concat_axis=0, tiled=True),
    )
    ptok = got_blocks.shape[2]
    picked = got_blocks.reshape(shards * slot_count, ptok, dim)[target].reshape(
        q_dev, cand, ptok, dim
    )
    picked_len = got_len.reshape(-1)[target].reshape(q_dev, cand)
    sim = jnp.einsum("qtd,qcpd->qctp", queries, picked, preferred_element_type=jnp.float32)
    valid = jnp.arange(ptok)[None, None, :] < picked_len[:, :, None]
    sim = jnp.where(valid[:, :, None, :], sim, jnp.float32(-1e30))
    maxsim = jnp.mean(jnp.max(sim, axis=-1), axis=-1)
    return (centroid_best, maxsim)


def solution(mesh):
    placed = (
        P(("groups", "shard"), None, None),
        P(("groups", "shard"), None),
        P(("groups", "shard"), None, None),
        P(("groups", "shard"), None),
        P(("groups", "shard"), None, None),
        P(("groups", "shard"), None),
    )
    return jax.shard_map(
        body,
        mesh=mesh,
        in_specs=placed,
        out_specs=(P(("groups", "shard"), None), P(("groups", "shard"), None)),
        check_vma=False,
    )
```

profile of v0, /device:TPU:0, one launch (start us, length us, event | category | flops | bytes accessed | tf_op | source)
XLA Modules:
  0.0 294.0 jit_solution(8131172389539613610)
XLA Ops:
  7.2 0.5 broadcast.112
  7.7 1.4 fusion.8
  9.7 0.8 reshape.146
  10.4 1.0 scatter_custom_fusion
  11.5 13.6 %all_to_all.26 = s32[16,1,16]{2,1,0:T(1,128)S(1)} all-to-all(s32[16,1,16]{2,1,0:T(1,128)S(1)} %all_to_all.17), channel_id=1, replica_groups=mesh['groups'=2,'shard'=16] {'shard'}, dimensions={0} | all-to-all | bytes 2048 | tf_op jit(solution)/shard_map/all_to_all | solution.py:37
  25.2 1.9 gather_fusion
  27.1 0.7 all_to_all.20
  27.7 3.5 %all-to-all-start.1 = ((s32[16,1,16]{2,1,0:T(1,128)}), s32[16,1,16]{2,1,0:T(1,128)S(1)}, u32[]{:S(2)}, u32[]{:S(2)}) async-start(s32[16,1,16]{2,1,0:T(1,128)} %all_to_all.20), calls=%async_computation.1 | async-start | bytes 16384 | tf_op jit(solution)/shard_map/all_to_all | solution.py:42
  31.2 10.5 %gather_fusion.2 = bf16[256,128,128]{2,1,0:T(8,128)(2,1)} fusion(bf16[128,128,128]{2,1,0:T(8,128)(2,1)} %param.10, s32[1024]{0:T(1024)S(1)} %pad_clamp_fusion.1), kind=kCustom, calls=%fused_computation.2 | custom fusion | bytes 16778240 | tf_op jit(solution)/shard_map/gather | solution.py:38
  41.8 6.1 %all-to-all-start.2 = ((bf16[16,16,128,128]{3,2,1,0:T(8,128)(2,1)}), bf16[16,16,128,128]{3,2,1,0:T(8,128)(2,1)}, u32[]{:S(2)}, u32[]{:S(2)}) async-start(bf16[16,16,128,128]{3,2,1,0:T(8,128)(2,1)} %bitcast.31), calls=%async_computation.2 | async-start | bytes 16777216 | tf_op jit(solution)/shard_map/all_to_all | solution.py:41
  47.9 0.7 all-gather.2.cloned.1.call-update
  48.6 0.7 reduce.13
  49.4 1.3 gather_fusion.1
  50.8 124.3 %all-gather.2.cloned.1.call-done = bf16[128,32,128]{2,1,0:T(8,128)(2,1)} async-done(((bf16[8,32,128]{2,1,0:T(8,128)(2,1)}), bf16[128,32,128]{2,1,0:T(8,128)(2,1)}) %all-gather.2.cloned.1.call-update) | async-done | bytes 1048592 | tf_op jit(solution)/shard_map/all_gather | solution.py:15
  175.1 6.9 %while.11 = (s32[]{:T(128)}, f32[4096]{0:T(1024)S(1)}, bf16[4,128,128]{2,1,0:T(8,128)(2,1)}, bf16[4096,128]{1,0:T(8,128)(2,1)}, s32[]{:T(128)}, /*index=5*/s32[]{:T(128)}) while((s32[]{:T(128)}, f32[4096]{0:T(1024)S(1)}, bf16[4,128,128]{2,1,0:T(8,128)(2,1)}, bf16[4096,128]{1,0:T(8,128)(2,1)}, s32[]{:T(128)}, ...), condition=%wide.region_2.3_spmd.clone, body=%wide.region_0.2_spmd.clone.sunk | while | flops 134746112 | bytes 1146971 | solution.py:23
  175.1 1.7 convolution_reduce_fusion.2
  176.8 1.7 convolution_reduce_fusion.2
  178.5 1.7 convolution_reduce_fusion.2
  180.3 1.7 convolution_reduce_fusion.2
  182.1 93.5 %pmax.7 = f32[128,32]{1,0:T(8,128)S(1)} all-reduce(f32[128,32]{1,0:T(8,128)S(1)} %reshape.104), channel_id=1, replica_groups=mesh['groups'=2,'shard'=16] {'shard'}, use_global_device_ids=true, to_apply=%region_3.4 | all-reduce | flops 4096 | bytes 32768 | tf_op jit(solution)/shard_map/pmax | solution.py:25
  275.5 0.6 constant_dynamic-slice_fusion
  276.1 6.5 %gather_fusion.3 = bf16[128,128,128]{2,1,0:T(8,128)(2,1)} fusion(bf16[256,128,128]{2,1,0:T(8,128)(2,1)} %bitcast.7, s32[1024]{0:T(1024)S(1)} %pad_clamp_fusion), kind=kCustom, calls=%fused_computation.3 | custom fusion | bytes 8389120 | tf_op jit(solution)/shard_map/gather | solution.py:45
  282.6 3.8 %select_reduce_fusion = f32[8,16,32]{2,1,0:T(8,128)S(1)} fusion(bf16[8,16,128,128]{3,2,1,0:T(8,128)(2,1)} %bitcast.33, pred[8,16,128]{2,1,0:T(8,128)(4,1)S(1)} %iota_compare_fusion.1, bf16[8,32,128]{2,1,0:T(8,128)(2,1)S(1)} %copy-done.1), kind=kOutput, calls=%fused_computation.10 | convolution fusion | flops 135262208 | bytes 4292608 | tf_op jit(solution)/shard_map/qtd,qcpd->qctp/dot_general | solution.py:49
  286.5 0.6 broadcast_multiply_fusion
  (28 shorter events, 1.3 us)
Async XLA Ops:
  7.2 18.0 %copy-start = (s32[1,128]{1,0:T(1,128)S(1)}, s32[1,128]{1,0:T(1,128)}, u32[]{:S(2)}) copy-start(s32[1,128]{1,0:T(1,128)} %param.11) | copy-start | bytes 1540
  27.7 14.0 %all-to-all-start.1 = ((s32[16,1,16]{2,1,0:T(1,128)}), s32[16,1,16]{2,1,0:T(1,128)S(1)}, u32[]{:S(2)}, u32[]{:S(2)}) async-start(s32[16,1,16]{2,1,0:T(1,128)} %all_to_all.20), calls=%async_computation.1 | async-start | bytes 16384 | tf_op jit(solution)/shard_map/all_to_all | solution.py:42
  41.8 234.4 %all-to-all-start.2 = ((bf16[16,16,128,128]{3,2,1,0:T(8,128)(2,1)}), bf16[16,16,128,128]{3,2,1,0:T(8,128)(2,1)}, u32[]{:S(2)}, u32[]{:S(2)}) async-start(bf16[16,16,128,128]{3,2,1,0:T(8,128)(2,1)} %bitcast.31), calls=%async_computation.2 | async-start | bytes 16777216 | tf_op jit(solution)/shard_map/all_to_all | solution.py:41
  47.8 127.2 %all-gather.2.cloned.1.call-start = ((), (), s32[]{:S(2)}) async-start(), calls=%async_computation.3 | async-start | bytes 1114112 | tf_op jit(solution)/shard_map/all_gather | solution.py:15
  276.1 6.5 %copy-start.1 = (bf16[8,32,128]{2,1,0:T(8,128)(2,1)S(1)}, bf16[8,32,128]{2,1,0:T(8,128)(2,1)}, u32[]{:S(2)}) copy-start(bf16[8,32,128]{2,1,0:T(8,128)(2,1)} %param.8) | copy-start | bytes 196612
Sparse Core Ops, SparseCore 0:
  50.8 124.1 all-gather.1
where the time goes:
time: 295 us; the launch traced here: 294 us
  waiting for transfers between devices  125 us (42%)
  blocking collectives  107 us (36%)
  local copies, waits for them, and re-layouts  24.2 us (8%)
  between operations  14.2 us (5%)
  matrix products  10.6 us (4%)
  starting transfers between devices  9.6 us (3%)
  other arithmetic  3.29 us (1%)
    all_gather x1, waiting for transfers between devices, body(): piece = lax.all_gather(queries, 'shard', axis=0, tiled=True)  124 us
    pmax x1, blocking collectives, body(): whole_best = lax.pmax(partial_best, 'shard')  93.5 us
    all_to_all x1, blocking collectives, body(): lax.all_to_all(row_buffer, 'shard', split_axis=0, concat_axis=0, tiled=True)  13.6 us
    gather x1, local copies, waits for them, and re-layouts, body(): sent_blocks = passages[asked]  10.5 us
    dot_general x4, matrix products, step(): jnp.einsum('rd,cd->rc', rows, block, preferred_element_type=jnp.float32)  6.75 us
    gather x1, local copies, waits for them, and re-layouts, body(): got_blocks.reshape(shards * slot_count, ptok, dim)[target]  6.47 us
    all_to_all x1, starting transfers between devices, body(): lax.all_to_all(sent_blocks, 'shard', split_axis=0, concat_axis=0, tiled=T...  6.06 us
  transfers between devices with their start and end apart: 3, of which 1 were waited for; matrix products, arithmetic and copies ran while one was open for 7% of the time, Pallas kernels for 0%

commit v1 on v0

v1 whole, which is shorter than its diff:
```python
import functools

import jax
import jax.numpy as jnp
from jax import lax
from jax.experimental import pallas as pl
from jax.experimental.pallas import tpu as pltpu
from jax.sharding import PartitionSpec as P

LOW = -1e30
LANES = 128


def pack_kernel(slots, q_ref, owner_ref, row_ref, out_ref):
    q_dev, cand = owner_ref.shape
    tokens = q_ref.shape[0]
    owners = out_ref.shape[0] - tokens
    out_ref[:tokens] = q_ref[...]
    lane = lax.broadcasted_iota(jnp.int32, (q_dev, LANES), 1)
    own_q = lax.broadcasted_iota(jnp.int32, (q_dev, LANES), 0) == lane // cand
    spread = (
        lax.broadcasted_iota(jnp.int32, (cand, LANES), 0)
        == lax.broadcasted_iota(jnp.int32, (cand, LANES), 1) % cand
    ).astype(jnp.float32)

    def flat(ref):
        wide = jnp.dot(ref[...].astype(jnp.float32), spread, preferred_element_type=jnp.float32)
        return jnp.sum(jnp.where(own_q, wide, 0.0), axis=0, keepdims=True)

    owner, row = flat(owner_ref), flat(row_ref)
    number = lax.broadcasted_iota(jnp.int32, (1, LANES), 1).astype(jnp.float32)
    code = row * 256.0 + (number + 1.0)
    hit = lax.broadcasted_iota(jnp.int32, (owners, LANES), 0).astype(jnp.float32) == owner
    earlier = (
        lax.broadcasted_iota(jnp.int32, (LANES, LANES), 0)
        <= lax.broadcasted_iota(jnp.int32, (LANES, LANES), 1)
    ).astype(jnp.float32)
    rank = jnp.dot(hit.astype(jnp.float32), earlier, preferred_element_type=jnp.float32)
    rank = jnp.where(hit, rank, 0.0)
    wide_lane = lax.broadcasted_iota(jnp.int32, (owners, LANES), 1)
    table = jnp.zeros((owners, LANES), jnp.float32)
    for slot in range(slots):
        value = jnp.sum(jnp.where(rank == slot + 1.0, code, 0.0), axis=1, keepdims=True)
        rows = jnp.floor(value * (1.0 / 256.0))
        table = jnp.where(wide_lane == slot, rows, table)
        table = jnp.where(wide_lane == slots + slot, value - rows * 256.0, table)
    out_ref[tokens:] = table.astype(out_ref.dtype)


def score_kernel(slots, cand, qt, all_ref, cent_ref, pass_ref, len_ref, out_ref,
                 held, codes, codes_smem, len_smem, pass_sem, len_sem, code_sem):
    blocks, height, dim = all_ref.shape
    tokens = out_ref.shape[2] - LANES
    owners = height - tokens
    me = lax.axis_index("shard")
    fetch = pltpu.make_async_copy(pass_ref, held, pass_sem)
    fetch.start()
    fetch_len = pltpu.make_async_copy(len_ref, len_smem, len_sem)
    fetch_len.start()
    mine = lax.broadcasted_iota(jnp.int32, (owners, LANES), 0) == me

    def pick(r, _):
        table = all_ref[r, tokens:, :].astype(jnp.float32)
        line = jnp.sum(jnp.where(mine, table, 0.0), axis=0, keepdims=True)
        codes[pl.ds(r, 1), :] = line.astype(jnp.int32)
        return _

    lax.fori_loop(0, blocks, pick, 0, unroll=True)
    send = pltpu.make_async_copy(codes, codes_smem, code_sem)
    send.start()

    def best(r, _):
        rows = all_ref[r, :tokens, :]
        top = None
        step = 128
        for c in range(0, cent_ref.shape[0], step):
            scores = lax.dot_general(
                cent_ref[c:c + step, :], rows, (((1,), (1,)), ((), ())),
                preferred_element_type=jnp.float32)
            part = scores.reshape(step // 8, 8, tokens)
            part = jnp.max(part, axis=0)
            top = part if top is None else jnp.maximum(top, part)
        out_ref[r, :, :tokens] = jnp.max(top, axis=0, keepdims=True)
        return _

    lax.fori_loop(0, blocks, best, 0)
    send.wait()
    fetch_len.wait()
    fetch.wait()
    lane = lax.broadcasted_iota(jnp.int32, (8, LANES), 1)

    def maxsim(r, _):
        total = jnp.full((8, LANES), LOW, jnp.float32)
        for slot in range(slots):
            row = codes_smem[r, slot]
            number = codes_smem[r, slots + slot] - 1
            query = jnp.maximum(number, 0) // cand
            length = len_smem[0, row]
            rows = all_ref[r, pl.ds(pl.multiple_of(query * qt, qt), qt), :]
            sim = lax.dot_general(rows, held[row], (((1,), (1,)), ((), ())),
                                  preferred_element_type=jnp.float32)
            parts = []
            for t in range(0, qt, 8):
                part = jnp.where(lane < length, sim[t:t + 8, :], LOW)
                parts.append(jnp.max(part, axis=1, keepdims=True))
            total = jnp.where(lane == number, sum(parts), total)
        out_ref[r, :, tokens:] = jnp.sum(total, axis=0, keepdims=True) * (1.0 / qt)
        return _

    lax.fori_loop(0, blocks, maxsim, 0)


def last_kernel(a_ref, b_ref, best_ref, sim_ref):
    q_dev, qt = best_ref.shape
    cand = sim_ref.shape[1]
    both = jnp.maximum(a_ref[...], b_ref[...])
    for q in range(q_dev):
        best_ref[q:q + 1, :] = both[:, q * qt:(q + 1) * qt]
        at = q_dev * qt + q * cand
        sim_ref[q:q + 1, :] = both[:, at:at + cand]


def body(queries, centroids, passages, lengths, cand_owner, cand_row):
    q_dev, qt, dim = queries.shape
    cand = cand_row.shape[1]
    shards = lax.axis_size("shard")
    slots = 2 * q_dev * cand // shards
    tokens = q_dev * qt
    vmem = pl.BlockSpec(memory_space=pltpu.VMEM)
    hbm = pl.BlockSpec(memory_space=pl.ANY)
    owners = -(-shards // 16) * 16
    block = pl.pallas_call(
        functools.partial(pack_kernel, slots),
        out_shape=jax.ShapeDtypeStruct((tokens + owners, dim), queries.dtype),
        in_specs=[vmem] * 3,
        out_specs=vmem,
        name="pack",
    )(queries.reshape(tokens, dim), cand_owner.reshape(q_dev, cand), cand_row)

    steps = []
    k = shards // 2
    while k >= 1:
        steps.append(k | 1)
        k //= 2
    held = block[None]
    for k in steps:
        pairs = [(i, i ^ k) for i in range(shards)]
        held = jnp.concatenate([held, lax.ppermute(held, "shard", pairs)], axis=0)

    width = tokens + q_dev * cand
    result = pl.pallas_call(
        functools.partial(score_kernel, slots, cand, qt),
        out_shape=jax.ShapeDtypeStruct((shards, 1, width), jnp.float32),
        in_specs=[vmem, vmem, hbm, hbm],
        out_specs=vmem,
        scratch_shapes=[
            pltpu.VMEM(passages.shape, passages.dtype),
            pltpu.VMEM((shards, LANES), jnp.int32),
            pltpu.SMEM((shards, LANES), jnp.int32),
            pltpu.SMEM(lengths.shape, jnp.int32),
            pltpu.SemaphoreType.DMA,
            pltpu.SemaphoreType.DMA,
            pltpu.SemaphoreType.DMA,
        ],
        compiler_params=pltpu.CompilerParams(vmem_limit_bytes=32 * 1024 * 1024),
        name="score",
    )(held, centroids, passages, lengths)

    for n, k in enumerate(reversed(steps)):
        half = result.shape[0] // 2
        pairs = [(i, i ^ k) for i in range(shards)]
        got = lax.ppermute(result[half:], "shard", pairs)
        if half > 1:
            result = jnp.maximum(result[:half], got)
        else:
            mine = result[:half]
    return pl.pallas_call(
        last_kernel,
        out_shape=(jax.ShapeDtypeStruct((q_dev, qt), jnp.float32), jax.ShapeDtypeStruct((q_dev, cand), jnp.float32)),
        in_specs=[vmem] * 2,
        out_specs=(vmem, vmem),
        name="last",
    )(mine[0], got[0])


def solution(mesh):
    both = ("groups", "shard")
    placed = (P(both, None, None), P(both, None), P(both, None, None), P(both, None), P(both, None, None), P(both, None))
    return jax.shard_map(body, mesh=mesh, in_specs=placed, out_specs=(P(both, None), P(both, None)), check_vma=False)
```

time: 295 us -> 58.2 us (0.20)
  blocking collectives: 107 us -> 0 us
  waiting for transfers between devices: 125 us -> 20.1 us
  local copies, waits for them, and re-layouts: 24.2 us -> 3.48 us
  Pallas kernels: 0 us -> 15.2 us
  between operations: 14.2 us -> 0.75 us
  matrix products: 10.6 us -> 0 us
  starting transfers between devices: 9.6 us -> 15.6 us
    all_gather x1 -> x0, waiting for transfers between devices: 124 us -> none  [body(): piece = lax.all_gather(queries, 'shard', axis=0, tiled=True)]
    pmax x1 -> x0, blocking collectives: 93.5 us -> none  [body(): whole_best = lax.pmax(partial_best, 'shard')]
    ppermute x0 -> x8, waiting for transfers between devices: none -> 20.1 us  [the longest x4 14.9 us: body(): held = jnp.concatenate([held, lax.ppermute(held, 'shard', pairs)], axis=0)]
    gather x4 -> x0, local copies, waits for them, and re-layouts: 20.1 us -> none  [the longest x1 10.5 us: body(): sent_blocks = passages[asked]]
    ppermute x0 -> x8, starting transfers between devices: none -> 15.6 us  [the longest x4 8.96 us: body(): held = jnp.concatenate([held, lax.ppermute(held, 'shard', pairs)], axis=0)]
    pallas_call x0 -> x3, Pallas kernels: none -> 15.2 us  [the longest x1 12 us: body(): pl.pallas_call(functools.partial(score_kernel, slots, cand, qt), out_shap...]
    all_to_all x1 -> x0, blocking collectives: 13.6 us -> none  [body(): lax.all_to_all(row_buffer, 'shard', split_axis=0, concat_axis=0, tiled=True)]
    dot_general x5 -> x0, matrix products: 10.6 us -> none  [the longest x4 6.75 us: step(): jnp.einsum('rd,cd->rc', rows, block, preferred_element_type=jnp.float32)]
  transfers between devices with their start and end apart: 3 -> 8, of which waited for: 1 -> 8; matrix products, arithmetic and copies ran while one was open for 7% -> 0% of each run, Pallas kernels for 0% -> 0%
where the time goes in v1:
time: 58.2 us; the launch traced here: 57.9 us
  waiting for transfers between devices  20.1 us (35%)
  starting transfers between devices  15.6 us (27%)
  Pallas kernels  15.2 us (26%)
  local copies, waits for them, and re-layouts  3.48 us (6%)
  other arithmetic  2.77 us (5%)
  between operations  0.75 us (1%)
    ppermute x4, waiting for transfers between devices, body(): held = jnp.concatenate([held, lax.ppermute(held, 'shard', pairs)], axis=0)  14.9 us
    pallas_call x1, Pallas kernels, body(): pl.pallas_call(functools.partial(score_kernel, slots, cand, qt), out_shap...  12 us
    ppermute x4, starting transfers between devices, body(): held = jnp.concatenate([held, lax.ppermute(held, 'shard', pairs)], axis=0)  8.96 us
    ppermute x4, starting transfers between devices, body(): got = lax.ppermute(result[half:], 'shard', pairs)  6.62 us
    ppermute x4, waiting for transfers between devices, body(): got = lax.ppermute(result[half:], 'shard', pairs)  5.21 us
    unnamed x14, local copies, waits for them, and re-layouts  2.82 us
    concatenate x3, other arithmetic, body(): held = jnp.concatenate([held, lax.ppermute(held, 'shard', pairs)], axis=0)  2.75 us
    pallas_call x1, Pallas kernels, body(): pl.pallas_call(functools.partial(pack_kernel, slots), out_shape=jax.Shape...  1.83 us
  transfers between devices with their start and end apart: 8, of which 8 were waited for; matrix products, arithmetic and copies ran while one was open for 0% of the time, Pallas kernels for 0%

profile of v1, /device:TPU:0, one launch (start us, length us, event | category | flops | bytes accessed | tf_op | source)
XLA Modules:
  0.0 57.9 jit_solution(9282803232450383676)
XLA Ops:
  0.6 1.8 %pack.1 = bf16[272,128]{1,0:T(8,128)(2,1)} custom-call(bf16[256,128]{1,0:T(8,128)(2,1)} %bitcast.11, s32[8,16]{1,0:T(8,128)} %bitcast.12, s32[8,16]{1,0:T(8,128)} %row_ref.1), custom_call_target="tpu_custom_call" | custom-call | tf_op jit(solution)/shard_map/pack/pallas_call | solution.py:132
  2.5 3.5 %collective-permute-start = (bf16[1,272,128]{2,1,0:T(8,128)(2,1)}, bf16[1,272,128]{2,1,0:T(8,128)(2,1)S(1)}, u32[]{:S(2)}, u32[]{:S(2)}) collective-permute-start(bf16[1,272,128]{2,1,0:T(8,128)(2,1)} %bitcast.7), channel_id=1, source_target_pairs={{0,9},{1,8},{2,11},{3,10},{4,13},{5,12},{6,15},{7,14},{8,1},{9,0},... | collective-permute-start | bytes 208904 | tf_op jit(solution)/shard_map/ppermute | solution.py:148
  5.9 2.9 %collective-permute-done = bf16[1,272,128]{2,1,0:T(8,128)(2,1)S(1)} collective-permute-done((bf16[1,272,128]{2,1,0:T(8,128)(2,1)}, bf16[1,272,128]{2,1,0:T(8,128)(2,1)S(1)}, u32[]{:S(2)}, u32[]{:S(2)}) %collective-permute-start) | collective-permute-done | bytes 69664 | tf_op jit(solution)/shard_map/ppermute | solution.py:148
  8.8 0.9 %pad_maximum_fusion.2 = bf16[2,272,128]{2,1,0:T(8,128)(2,1)S(1)} fusion(bf16[1,272,128]{2,1,0:T(8,128)(2,1)S(1)} %collective-permute-done, bf16[1,272,128]{2,1,0:T(8,128)(2,1)} %bitcast.8), kind=kLoop, calls=%fused_computation.2 | loop fusion | flops 69632 | bytes 278528 | tf_op jit(solution)/shard_map/concatenate | solution.py:148
  9.7 2.7 %collective-permute-start.1 = (bf16[2,272,128]{2,1,0:T(8,128)(2,1)S(1)}, bf16[2,272,128]{2,1,0:T(8,128)(2,1)S(1)}, u32[]{:S(2)}, u32[]{:S(2)}) collective-permute-start(bf16[2,272,128]{2,1,0:T(8,128)(2,1)S(1)} %pad_maximum_fusion.2), channel_id=1, source_target_pairs={{0,5},{1,4},{2,7},{3,6},{4,1},{5,0},{6,3},{7,2},{8,13},{9,12},{10,... | collective-permute-start | bytes 417800 | tf_op jit(solution)/shard_map/ppermute | solution.py:148
  12.5 3.8 %collective-permute-done.1 = bf16[2,272,128]{2,1,0:T(8,128)(2,1)S(1)} collective-permute-done((bf16[2,272,128]{2,1,0:T(8,128)(2,1)S(1)}, bf16[2,272,128]{2,1,0:T(8,128)(2,1)S(1)}, u32[]{:S(2)}, u32[]{:S(2)}) %collective-permute-start.1) | collective-permute-done | bytes 139296 | tf_op jit(solution)/shard_map/ppermute | solution.py:148
  16.2 0.9 %pad_maximum_fusion.1 = bf16[4,272,128]{2,1,0:T(8,128)(2,1)S(1)} fusion(bf16[2,272,128]{2,1,0:T(8,128)(2,1)S(1)} %collective-permute-done.1, bf16[1,272,128]{2,1,0:T(8,128)(2,1)S(1)} %collective-permute-done, bf16[1,272,128]{2,1,0:T(8,128)(2,1)} %bitcast.9), kind=kLoop, calls=%fused_computation.1 | loop fusion | flops 278528 | bytes 557056 | tf_op jit(solution)/shard_map/concatenate | solution.py:148
  17.1 2.4 %collective-permute-start.2 = (bf16[4,272,128]{2,1,0:T(8,128)(2,1)S(1)}, bf16[4,272,128]{2,1,0:T(8,128)(2,1)S(1)}, u32[]{:S(2)}, u32[]{:S(2)}) collective-permute-start(bf16[4,272,128]{2,1,0:T(8,128)(2,1)S(1)} %pad_maximum_fusion.1), channel_id=1, source_target_pairs={{0,3},{1,2},{2,1},{3,0},{4,7},{5,6},{6,5},{7,4},{8,11},{9,10},{10,... | collective-permute-start | bytes 835592 | tf_op jit(solution)/shard_map/ppermute | solution.py:148
  19.5 6.7 %collective-permute-done.2 = bf16[4,272,128]{2,1,0:T(8,128)(2,1)S(1)} collective-permute-done((bf16[4,272,128]{2,1,0:T(8,128)(2,1)S(1)}, bf16[4,272,128]{2,1,0:T(8,128)(2,1)S(1)}, u32[]{:S(2)}, u32[]{:S(2)}) %collective-permute-start.2) | collective-permute-done | bytes 278560 | tf_op jit(solution)/shard_map/ppermute | solution.py:148
  26.3 0.9 %pad_maximum_fusion = bf16[8,272,128]{2,1,0:T(8,128)(2,1)S(1)} fusion(bf16[4,272,128]{2,1,0:T(8,128)(2,1)S(1)} %collective-permute-done.2, bf16[2,272,128]{2,1,0:T(8,128)(2,1)S(1)} %collective-permute-done.1, bf16[1,272,128]{2,1,0:T(8,128)(2,1)S(1)} %collective-permute-done, bf16[1,272,128]{2,1,0:T(8,128)(2,1)} %bitcast.10), kind=kLoop, calls=%fused_computation | loop fusion | flops 835584 | bytes 1114112 | tf_op jit(solution)/shard_map/concatenate | solution.py:148
  27.2 0.4 collective-permute-start.3
  27.7 1.6 %collective-permute-done.3 = bf16[8,272,128]{2,1,0:T(8,128)(2,1)S(1)} collective-permute-done((bf16[8,272,128]{2,1,0:T(8,128)(2,1)S(1)}, bf16[8,272,128]{2,1,0:T(8,128)(2,1)S(1)}, u32[]{:S(2)}, u32[]{:S(2)}) %collective-permute-start.3) | collective-permute-done | bytes 557088 | tf_op jit(solution)/shard_map/ppermute | solution.py:148
  29.4 2.2 %copy-done = bf16[128,128,128]{2,1,0:T(8,128)(2,1)S(1)} copy-done((bf16[128,128,128]{2,1,0:T(8,128)(2,1)S(1)}, bf16[128,128,128]{2,1,0:T(8,128)(2,1)}, u32[]{:S(2)}) %copy-start) | copy-done | bytes 4194328
  31.5 12.0 %score.1 = f32[16,1,384]{2,1,0:T(1,128)S(1)} custom-call(bf16[16,272,128]{2,1,0:T(8,128)(2,1)S(1)} %constant_dynamic-update-slice_fusion.all_ref, bf16[512,128]{1,0:T(8,128)(2,1)S(1)} %copy-done.1, bf16[128,128,128]{2,1,0:T(8,128)(2,1)S(1)} %copy-done, s32[1,128]{1,0:T(1,128)S(1)} %copy-done.2), custom_call_target="tpu_custom_call" | custom-call | tf_op jit(solution)/shard_map/score/pallas_call | solution.py:151
  43.9 0.9 %collective-permute-done.4 = f32[8,1,384]{2,1,0:T(1,128)S(1)} collective-permute-done((f32[8,1,384]{2,1,0:T(1,128)S(1)}, f32[8,1,384]{2,1,0:T(1,128)S(1)}, u32[]{:S(2)}, u32[]{:S(2)}) %collective-permute-start.4) | collective-permute-done | bytes 12320 | tf_op jit(solution)/shard_map/ppermute | solution.py:172
  44.8 2.0 %collective-permute-start.5 = (f32[4,1,384]{2,1,0:T(1,128)S(1)}, f32[4,1,384]{2,1,0:T(1,128)S(1)}, u32[]{:S(2)}, u32[]{:S(2)}) collective-permute-start(f32[4,1,384]{2,1,0:T(1,128)S(1)} %slice.35), channel_id=1, source_target_pairs={{0,3},{1,2},{2,1},{3,0},{4,7},{5,6},{6,5},{7,4},{8,11},{9,10},{10,... | collective-permute-start | bytes 18440 | tf_op jit(solution)/shard_map/ppermute | solution.py:172
  46.8 1.3 %collective-permute-done.5 = f32[4,1,384]{2,1,0:T(1,128)S(1)} collective-permute-done((f32[4,1,384]{2,1,0:T(1,128)S(1)}, f32[4,1,384]{2,1,0:T(1,128)S(1)}, u32[]{:S(2)}, u32[]{:S(2)}) %collective-permute-start.5) | collective-permute-done | bytes 6176 | tf_op jit(solution)/shard_map/ppermute | solution.py:172
  48.2 1.4 %collective-permute-start.6 = (f32[2,1,384]{2,1,0:T(1,128)S(1)}, f32[2,1,384]{2,1,0:T(1,128)S(1)}, u32[]{:S(2)}, u32[]{:S(2)}) collective-permute-start(f32[2,1,384]{2,1,0:T(1,128)S(1)} %slice.37), channel_id=1, source_target_pairs={{0,5},{1,4},{2,7},{3,6},{4,1},{5,0},{6,3},{7,2},{8,13},{9,12},{10,... | collective-permute-start | bytes 9224 | tf_op jit(solution)/shard_map/ppermute | solution.py:172
  49.6 1.7 %collective-permute-done.6 = f32[2,1,384]{2,1,0:T(1,128)S(1)} collective-permute-done((f32[2,1,384]{2,1,0:T(1,128)S(1)}, f32[2,1,384]{2,1,0:T(1,128)S(1)}, u32[]{:S(2)}, u32[]{:S(2)}) %collective-permute-start.6) | collective-permute-done | bytes 3104 | tf_op jit(solution)/shard_map/ppermute | solution.py:172
  51.3 0.6 fusion
  51.8 2.8 %collective-permute-start.7 = (f32[1,1,384]{2,1,0:T(1,128)S(1)}, f32[1,1,384]{2,1,0:T(1,128)S(1)}, u32[]{:S(2)}, u32[]{:S(2)}) collective-permute-start(f32[1,1,384]{2,1,0:T(1,128)S(1)} %get-tuple-element.2), channel_id=1, source_target_pairs={{0,9},{1,8},{2,11},{3,10},{4,13},{5,12},{6,15},{7,14},{8,1},{9,0},... | collective-permute-start | bytes 4616 | tf_op jit(solution)/shard_map/ppermute | solution.py:172
  54.7 1.3 %collective-permute-done.7 = f32[1,1,384]{2,1,0:T(1,128)S(1)} collective-permute-done((f32[1,1,384]{2,1,0:T(1,128)S(1)}, f32[1,1,384]{2,1,0:T(1,128)S(1)}, u32[]{:S(2)}, u32[]{:S(2)}) %collective-permute-start.7) | collective-permute-done | bytes 1568 | tf_op jit(solution)/shard_map/ppermute | solution.py:172
  56.0 0.5 copy-done.4
  56.5 1.3 %last.1 = (f32[8,32]{1,0:T(8,128)}, f32[8,16]{1,0:T(8,128)}) custom-call(f32[1,384]{1,0:T(1,128)} %get-tuple-element.3.a_ref, f32[1,384]{1,0:T(1,128)} %bitcast.13), custom_call_target="tpu_custom_call" | custom-call | tf_op jit(solution)/shard_map/last/pallas_call | solution.py:177
  (20 shorter events, 0.6 us)
Async XLA Ops:
  2.5 25.1 %copy-start.3 = (bf16[272,128]{1,0:T(8,128)(2,1)S(1)}, bf16[272,128]{1,0:T(8,128)(2,1)}, u32[]{:S(2)}) copy-start(bf16[272,128]{1,0:T(8,128)(2,1)} %pack.1) | copy-start | bytes 208900
  2.5 6.4 %collective-permute-start = (bf16[1,272,128]{2,1,0:T(8,128)(2,1)}, bf16[1,272,128]{2,1,0:T(8,128)(2,1)S(1)}, u32[]{:S(2)}, u32[]{:S(2)}) collective-permute-start(bf16[1,272,128]{2,1,0:T(8,128)(2,1)} %bitcast.7), channel_id=1, source_target_pairs={{0,9},{1,8},{2,11},{3,10},{4,13},{5,12},{6,15},{7,14},{8,1},{9,0},... | collective-permute-start | bytes 208904 | tf_op jit(solution)/shard_map/ppermute | solution.py:148
  9.7 6.5 %collective-permute-start.1 = (bf16[2,272,128]{2,1,0:T(8,128)(2,1)S(1)}, bf16[2,272,128]{2,1,0:T(8,128)(2,1)S(1)}, u32[]{:S(2)}, u32[]{:S(2)}) collective-permute-start(bf16[2,272,128]{2,1,0:T(8,128)(2,1)S(1)} %pad_maximum_fusion.2), channel_id=1, source_target_pairs={{0,5},{1,4},{2,7},{3,6},{4,1},{5,0},{6,3},{7,2},{8,13},{9,12},{10,... | collective-permute-start | bytes 417800 | tf_op jit(solution)/shard_map/ppermute | solution.py:148
  17.1 9.1 %collective-permute-start.2 = (bf16[4,272,128]{2,1,0:T(8,128)(2,1)S(1)}, bf16[4,272,128]{2,1,0:T(8,128)(2,1)S(1)}, u32[]{:S(2)}, u32[]{:S(2)}) collective-permute-start(bf16[4,272,128]{2,1,0:T(8,128)(2,1)S(1)} %pad_maximum_fusion.1), channel_id=1, source_target_pairs={{0,3},{1,2},{2,1},{3,0},{4,7},{5,6},{6,5},{7,4},{8,11},{9,10},{10,... | collective-permute-start | bytes 835592 | tf_op jit(solution)/shard_map/ppermute | solution.py:148
  27.2 2.1 %copy-start.1 = (bf16[512,128]{1,0:T(8,128)(2,1)S(1)}, bf16[512,128]{1,0:T(8,128)(2,1)}, u32[]{:S(2)}) copy-start(bf16[512,128]{1,0:T(8,128)(2,1)} %cent_ref.1) | copy-start | bytes 393220
  27.2 2.1 %copy-start.2 = (s32[1,128]{1,0:T(1,128)S(1)}, s32[1,128]{1,0:T(1,128)}, u32[]{:S(2)}) copy-start(s32[1,128]{1,0:T(1,128)} %len_ref.1) | copy-start | bytes 1540
  27.2 2.0 %collective-permute-start.3 = (bf16[8,272,128]{2,1,0:T(8,128)(2,1)S(1)}, bf16[8,272,128]{2,1,0:T(8,128)(2,1)S(1)}, u32[]{:S(2)}, u32[]{:S(2)}) collective-permute-start(bf16[8,272,128]{2,1,0:T(8,128)(2,1)S(1)} %pad_maximum_fusion), channel_id=1, source_target_pairs={{0,1},{1,0},{2,3},{3,2},{4,5},{5,4},{6,7},{7,6},{8,9},{9,8},{10,11... | collective-permute-start | bytes 1671176 | tf_op jit(solution)/shard_map/ppermute | solution.py:148
  29.3 2.2 %copy-start = (bf16[128,128,128]{2,1,0:T(8,128)(2,1)S(1)}, bf16[128,128,128]{2,1,0:T(8,128)(2,1)}, u32[]{:S(2)}) copy-start(bf16[128,128,128]{2,1,0:T(8,128)(2,1)} %pass_ref.1) | copy-start | bytes 12582916
  43.5 1.2 %collective-permute-start.4 = (f32[8,1,384]{2,1,0:T(1,128)S(1)}, f32[8,1,384]{2,1,0:T(1,128)S(1)}, u32[]{:S(2)}, u32[]{:S(2)}) collective-permute-start(f32[8,1,384]{2,1,0:T(1,128)S(1)} %slice.33), channel_id=1, source_target_pairs={{0,1},{1,0},{2,3},{3,2},{4,5},{5,4},{6,7},{7,6},{8,9},{9,8},{10,11... | collective-permute-start | bytes 36872 | tf_op jit(solution)/shard_map/ppermute | solution.py:172
  44.8 3.4 %collective-permute-start.5 = (f32[4,1,384]{2,1,0:T(1,128)S(1)}, f32[4,1,384]{2,1,0:T(1,128)S(1)}, u32[]{:S(2)}, u32[]{:S(2)}) collective-permute-start(f32[4,1,384]{2,1,0:T(1,128)S(1)} %slice.35), channel_id=1, source_target_pairs={{0,3},{1,2},{2,1},{3,0},{4,7},{5,6},{6,5},{7,4},{8,11},{9,10},{10,... | collective-permute-start | bytes 18440 | tf_op jit(solution)/shard_map/ppermute | solution.py:172
  48.2 3.1 %collective-permute-start.6 = (f32[2,1,384]{2,1,0:T(1,128)S(1)}, f32[2,1,384]{2,1,0:T(1,128)S(1)}, u32[]{:S(2)}, u32[]{:S(2)}) collective-permute-start(f32[2,1,384]{2,1,0:T(1,128)S(1)} %slice.37), channel_id=1, source_target_pairs={{0,5},{1,4},{2,7},{3,6},{4,1},{5,0},{6,3},{7,2},{8,13},{9,12},{10,... | collective-permute-start | bytes 9224 | tf_op jit(solution)/shard_map/ppermute | solution.py:172
  51.8 4.1 %collective-permute-start.7 = (f32[1,1,384]{2,1,0:T(1,128)S(1)}, f32[1,1,384]{2,1,0:T(1,128)S(1)}, u32[]{:S(2)}, u32[]{:S(2)}) collective-permute-start(f32[1,1,384]{2,1,0:T(1,128)S(1)} %get-tuple-element.2), channel_id=1, source_target_pairs={{0,9},{1,8},{2,11},{3,10},{4,13},{5,12},{6,15},{7,14},{8,1},{9,0},... | collective-permute-start | bytes 4616 | tf_op jit(solution)/shard_map/ppermute | solution.py:172
  56.0 0.5 copy-start.4

commit v2 on v1

v2 whole, which is shorter than its diff:
```python
import functools

import jax
import jax.numpy as jnp
from jax import lax
from jax.experimental import pallas as pl
from jax.experimental.pallas import tpu as pltpu
from jax.sharding import PartitionSpec as P

LOW = -1e30
LANES = 128
HEAD = 16
MIB = 1024 * 1024
NT = (((1,), (1,)), ((), ()))


def pack_kernel(slots, q_ref, owner_ref, row_ref, out_ref, owner_held, row_held, sems):
    q_dev, cand = owner_ref.shape
    tokens = q_ref.shape[0]
    owners = out_ref.shape[0] - tokens - HEAD
    copies = [
        pltpu.make_async_copy(source, target, sems.at[n])
        for n, (source, target) in enumerate(
            ((owner_ref, owner_held), (row_ref, row_held), (q_ref, out_ref.at[pl.ds(0, tokens)])))
    ]
    for copy in copies:
        copy.start()
    copies[0].wait()
    copies[1].wait()
    lane = lax.broadcasted_iota(jnp.int32, (q_dev, LANES), 1)
    own_q = lax.broadcasted_iota(jnp.int32, (q_dev, LANES), 0) == lane // cand
    spread = (
        lax.broadcasted_iota(jnp.int32, (cand, LANES), 0)
        == lax.broadcasted_iota(jnp.int32, (cand, LANES), 1) % cand
    ).astype(jnp.float32)

    def flat(ref):
        wide = jnp.dot(ref[...].astype(jnp.float32), spread, preferred_element_type=jnp.float32)
        return jnp.sum(jnp.where(own_q, wide, 0.0), axis=0, keepdims=True)

    owner, row = flat(owner_held), flat(row_held)
    query = (lax.broadcasted_iota(jnp.int32, (1, LANES), 1) // cand).astype(jnp.float32)
    code = row * 256.0 + query
    hit = lax.broadcasted_iota(jnp.int32, (owners, LANES), 0).astype(jnp.float32) == owner
    earlier = (
        lax.broadcasted_iota(jnp.int32, (LANES, LANES), 0)
        < lax.broadcasted_iota(jnp.int32, (LANES, LANES), 1)
    ).astype(jnp.float32)
    rank = jnp.dot(hit.astype(jnp.float32), earlier, preferred_element_type=jnp.float32)
    rank = jnp.where(hit, rank, -1.0)
    wide_lane = lax.broadcasted_iota(jnp.int32, (owners, LANES), 1)
    table = jnp.zeros((owners, LANES), jnp.float32)
    for slot in range(slots):
        value = jnp.sum(jnp.where(rank == float(slot), code, 0.0), axis=1, keepdims=True)
        rows = jnp.floor(value * (1.0 / 256.0))
        table = jnp.where(wide_lane == slot, rows, table)
        table = jnp.where(wide_lane == slots + slot, value - rows * 256.0, table)
    own_rank = jnp.max(rank, axis=0, keepdims=True)
    head = lax.broadcasted_iota(jnp.int32, (HEAD, LANES), 0)
    out_ref[tokens:tokens + HEAD] = jnp.where(head == 0, owner, jnp.where(head == 1, own_rank, 0.0)).astype(out_ref.dtype)
    out_ref[tokens + HEAD:] = table.astype(out_ref.dtype)
    copies[2].wait()


def fetch_kernel(cent_ref, pass_ref, len_ref, cent_out, pass_out, len_out, sems):
    copies = [
        pltpu.make_async_copy(source, target, sems.at[n])
        for n, (source, target) in enumerate(((cent_ref, cent_out), (pass_ref, pass_out), (len_ref, len_out)))
    ]
    for copy in copies:
        copy.start()
    for copy in copies:
        copy.wait()


def score_kernel(slots, qt, counts, *refs):
    parts = len(counts)
    all_refs, (cent_ref, held, len_ref), out_refs = refs[:parts], refs[parts:parts + 3], refs[parts + 3:]
    height = all_refs[0].shape[1]
    tokens = out_refs[0].shape[2] - LANES
    owners = height - tokens - HEAD
    at = tokens + HEAD
    ptok = held.shape[1]
    me = lax.axis_index("shard")
    mine = lax.broadcasted_iota(jnp.int32, (owners, LANES), 0) == me
    lens = jnp.broadcast_to(len_ref[...], (8, LANES))
    place = lax.broadcasted_iota(jnp.int32, (ptok, qt), 0)

    def group(ref, out, start, count):
        lines = []
        for n in range(count):
            table = ref[start + n, at:, :].astype(jnp.float32)
            lines.append(jnp.sum(jnp.where(mine, table, 0.0), axis=0, keepdims=True))
        lines.extend([jnp.zeros((1, LANES), jnp.float32)] * (8 - count))
        row = jnp.concatenate(lines, axis=0).astype(jnp.int32)
        query = pltpu.roll(row, LANES - slots, 1)
        length = jnp.take_along_axis(lens, row, axis=1)
        codes = row + (query << 8) + (length << 16)
        for n in range(count):
            r = start + n
            scores = lax.dot_general(cent_ref[...], ref[r, :tokens, :], NT, preferred_element_type=jnp.float32)
            top = jnp.max(scores.reshape(-1, 8, tokens), axis=0)
            out[r, :, :tokens] = jnp.max(top, axis=0, keepdims=True)
        for n in range(count):
            r = start + n
            head = ref[r, tokens:at, :].astype(jnp.float32)
            rank = jnp.where(head[0:1, :] == me.astype(jnp.float32), head[1:2, :], -1.0)
            total = jnp.full((1, LANES), LOW, jnp.float32)
            for slot in range(slots):
                code = codes[n, slot]
                first = pl.multiple_of(((code >> 8) & 255) * qt, qt)
                sim = lax.dot_general(held[code & 255], ref[r, pl.ds(first, qt), :], NT,
                                      preferred_element_type=jnp.float32)
                sim = jnp.where(place < (code >> 16), sim, LOW)
                top = jnp.max(jnp.max(sim.reshape(-1, 8, qt), axis=0), axis=0, keepdims=True)
                score = jnp.sum(top, axis=1, keepdims=True) * (1.0 / qt)
                total = jnp.where(rank == float(slot), score, total)
            out[r, :, tokens:] = total

    for count, ref, out in zip(counts, all_refs, out_refs):
        size = min(count, 8)
        if count == size:
            group(ref, out, 0, count)
        else:

            def some(g, _, ref=ref, out=out, size=size):
                group(ref, out, g * size, size)
                return _

            lax.fori_loop(0, count // size, some, 0)


def last_kernel(a_ref, b_ref, best_ref, sim_ref):
    q_dev, qt = best_ref.shape
    cand = sim_ref.shape[1]
    both = jnp.maximum(a_ref[0], b_ref[0])
    for q in range(q_dev):
        best_ref[q:q + 1, :] = both[:, q * qt:(q + 1) * qt]
        at = q_dev * qt + q * cand
        sim_ref[q:q + 1, :] = both[:, at:at + cand]


def body(queries, centroids, passages, lengths, cand_owner, cand_row):
    q_dev, qt, dim = queries.shape
    cand = cand_row.shape[1]
    shards = lax.axis_size("shard")
    slots = 2 * q_dev * cand // shards
    tokens = q_dev * qt
    vmem = pl.BlockSpec(memory_space=pltpu.VMEM)
    hbm = pl.BlockSpec(memory_space=pltpu.HBM)
    owners = -(-shards // 16) * 16
    height = tokens + HEAD + owners

    def stay(x):
        return pltpu.with_memory_space_constraint(x, pltpu.HBM)

    block = pl.pallas_call(
        functools.partial(pack_kernel, slots),
        out_shape=pltpu.VMEM((height, dim), queries.dtype),
        in_specs=[hbm] * 3,
        out_specs=vmem,
        scratch_shapes=[
            pltpu.VMEM((q_dev, cand), jnp.int32),
            pltpu.VMEM((q_dev, cand), jnp.int32),
            pltpu.SemaphoreType.DMA((3,)),
        ],
        compiler_params=pltpu.CompilerParams(vmem_limit_bytes=2 * MIB),
        name="pack",
    )(stay(queries.reshape(tokens, dim)), stay(cand_owner.reshape(q_dev, cand)), stay(cand_row))

    index = pl.pallas_call(
        fetch_kernel,
        out_shape=[pltpu.VMEM(x.shape, x.dtype) for x in (centroids, passages, lengths)],
        in_specs=[hbm] * 3,
        out_specs=[vmem] * 3,
        scratch_shapes=[pltpu.SemaphoreType.DMA((3,))],
        compiler_params=pltpu.CompilerParams(vmem_limit_bytes=MIB),
        name="fetch",
    )(stay(centroids), stay(passages), stay(lengths))

    def swap(x, k):
        return lax.ppermute(x, "shard", [(i, i ^ k) for i in range(shards)])

    def score(*blocks):
        counts = tuple(b.shape[0] for b in blocks)
        total = sum(counts)
        return pl.pallas_call(
            functools.partial(score_kernel, slots, qt, counts),
            out_shape=[pltpu.VMEM((n, 1, tokens + q_dev * cand), jnp.float32) for n in counts],
            in_specs=[vmem] * (len(blocks) + 3),
            out_specs=[vmem] * len(blocks),
            compiler_params=pltpu.CompilerParams(vmem_limit_bytes=4 * MIB),
            cost_estimate=pl.CostEstimate(
                flops=4 * total * (tokens * centroids.size + slots * qt * (passages.size // passages.shape[0])),
                bytes_accessed=total * MIB, transcendentals=0),
            name="score",
        )(*blocks, *index)

    far = []
    k = shards // 2
    while k > 2:
        far.append(k | 1)
        k //= 2
    first = block[None]
    for k in far[:-2]:
        first = jnp.concatenate([first, swap(first, k)], axis=0)
    second = swap(first, far[-2])
    third = swap(first, far[-1])
    xa = swap(first, 3)
    second, index = lax.optimization_barrier((second, index))
    fourth = swap(second, far[-1])
    near3 = jnp.concatenate([second, third], axis=0)
    xb = swap(near3, 3)
    c1 = swap(jnp.concatenate([first, near3], axis=0), 1)
    s1 = score(first, near3)
    fourth, s1 = lax.optimization_barrier((fourth, s1))
    xc = swap(fourth, 3)
    c2 = swap(jnp.concatenate([fourth, xa], axis=0), 1)
    s2 = score(fourth, xa, c1)
    xb, s2 = lax.optimization_barrier((xb, s2))
    c3 = swap(xb, 1)
    s3 = score(c2, xb)
    xc, s3 = lax.optimization_barrier((xc, s3))
    c4 = swap(xc, 1)
    s4 = score(c3)
    c4, s4 = lax.optimization_barrier((c4, s4))
    s5 = score(c4)
    other = jnp.concatenate([s2[2], s3[0], s4[0], s5[0]], axis=0)
    got = swap(other, 1)
    s6 = score(xc)
    near = jnp.concatenate([s1[0], s1[1], s2[0], s2[1], s3[1], s6[0]], axis=0)
    result = jnp.maximum(near, got)
    for k in [3] + far[::-1]:
        half = result.shape[0] // 2
        got = swap(result[half:], k)
        if half > 1:
            result = jnp.maximum(result[:half], got)
        else:
            mine = result[:half]
    return pl.pallas_call(
        last_kernel,
        out_shape=(jax.ShapeDtypeStruct((q_dev, qt), jnp.float32), jax.ShapeDtypeStruct((q_dev, cand), jnp.float32)),
        in_specs=[vmem] * 2,
        out_specs=(vmem, vmem),
        compiler_params=pltpu.CompilerParams(vmem_limit_bytes=MIB),
        name="last",
    )(mine, got)


def solution(mesh):
    both = ("groups", "shard")
    placed = (P(both, None, None), P(both, None), P(both, None, None), P(both, None), P(both, None, None), P(both, None))
    return jax.shard_map(body, mesh=mesh, in_specs=placed, out_specs=(P(both, None), P(both, None)), check_vma=False)
```

time: 58.2 us -> 34.6 us (0.59)
  waiting for transfers between devices: 20.1 us -> 6.53 us
  Pallas kernels: 15.2 us -> 10.3 us
  local copies, waits for them, and re-layouts: 3.48 us -> 0.07 us
  other arithmetic: 2.77 us -> 0.08 us
  starting transfers between devices: 15.6 us -> 16.7 us
    ppermute x8 -> x14, waiting for transfers between devices: 20.1 us -> 6.53 us  [swap(): return lax.ppermute(x, 'shard', [(i, i ^ k) for i in range(shards)])]
    pallas_call x2 -> x8, Pallas kernels: 13.8 us -> 9.6 us  [the longest x6 6.23 us: score(): pl.pallas_call(functools.partial(score_kernel, slots, qt, counts), out_sh...]
    unnamed x14 -> x6, local copies, waits for them, and re-layouts: 2.82 us -> 0.04 us
    concatenate x3, other arithmetic: 2.75 us -> 0.06 us  [the longest x1 0.03 us: body(): c1 = swap(jnp.concatenate([first, near3], axis=0), 1)]
    ppermute x8 -> x14, starting transfers between devices: 15.6 us -> 16.7 us  [swap(): return lax.ppermute(x, 'shard', [(i, i ^ k) for i in range(shards)])]
    pallas_call x1, Pallas kernels: 1.33 us -> 0.68 us  [body(): pl.pallas_call(last_kernel, out_shape=(jax.ShapeDtypeStruct((q_dev, qt),...]
  transfers between devices with their start and end apart: 8 -> 14, of which waited for: 8 -> 5; matrix products, arithmetic and copies ran while one was open for 0% -> 0% of each run, Pallas kernels for 0% -> 23%
where the time goes in v2:
time: 34.6 us; the launch traced here: 34.4 us
  starting transfers between devices  16.7 us (48%)
  Pallas kernels  10.3 us (30%)
  waiting for transfers between devices  6.53 us (19%)
  between operations  0.73 us (2%)
    ppermute x14, starting transfers between devices, swap(): return lax.ppermute(x, 'shard', [(i, i ^ k) for i in range(shards)])  16.7 us
    ppermute x14, waiting for transfers between devices, swap(): return lax.ppermute(x, 'shard', [(i, i ^ k) for i in range(shards)])  6.53 us
    pallas_call x6, Pallas kernels, score(): pl.pallas_call(functools.partial(score_kernel, slots, qt, counts), out_sh...  6.23 us
    pallas_call x1, Pallas kernels, body(): pl.pallas_call(fetch_kernel, out_shape=[pltpu.VMEM(x.shape, x.dtype) for...  2.29 us
    pallas_call x1, Pallas kernels, body(): pl.pallas_call(functools.partial(pack_kernel, slots), out_shape=pltpu.VME...  1.08 us
  transfers between devices with their start and end apart: 14, of which 5 were waited for; matrix products, arithmetic and copies ran while one was open for 0% of the time, Pallas kernels for 23%

profile of v2, /device:TPU:0, one launch (start us, length us, event | category | flops | bytes accessed | tf_op | source)
XLA Modules:
  0.0 34.4 jit_solution(3388893904283773721)
XLA Ops:
  0.6 1.1 %pack.1 = bf16[288,128]{1,0:T(8,128)(2,1)S(1)} custom-call(bf16[256,128]{1,0:T(8,128)(2,1)} %bitcast.8, s32[8,16]{1,0:T(8,128)} %bitcast.9, s32[8,16]{1,0:T(8,128)} %row_ref.1), custom_call_target="tpu_custom_call" | custom-call | tf_op jit(solution)/shard_map/pack/pallas_call | solution.py:157
  1.7 3.5 %collective-permute-start = (bf16[1,288,128]{2,1,0:T(8,128)(2,1)S(1)}, bf16[1,288,128]{2,1,0:T(8,128)(2,1)S(1)}, u32[]{:S(2)}, u32[]{:S(2)}) collective-permute-start(bf16[1,288,128]{2,1,0:T(8,128)(2,1)S(1)} %bitcast.3), channel_id=1, source_target_pairs={{0,9},{1,8},{2,11},{3,10},{4,13},{5,12},{6,15},{7,14},{8,1},{9,0},... | collective-permute-start | bytes 221192 | tf_op jit(solution)/shard_map/ppermute | solution.py:182
  5.3 1.9 %collective-permute-start.2 = (bf16[1,288,128]{2,1,0:T(8,128)(2,1)S(1)}, bf16[1,288,128]{2,1,0:T(8,128)(2,1)S(1)}, u32[]{:S(2)}, u32[]{:S(2)}) collective-permute-start(bf16[1,288,128]{2,1,0:T(8,128)(2,1)S(1)} %bitcast.4), channel_id=1, source_target_pairs={{0,5},{1,4},{2,7},{3,6},{4,1},{5,0},{6,3},{7,2},{8,13},{9,12},{10,... | collective-permute-start | bytes 221192 | tf_op jit(solution)/shard_map/ppermute | solution.py:182
  7.1 0.9 %collective-permute-start.4 = (bf16[1,288,128]{2,1,0:T(8,128)(2,1)S(1)}, bf16[1,288,128]{2,1,0:T(8,128)(2,1)S(1)}, u32[]{:S(2)}, u32[]{:S(2)}) collective-permute-start(bf16[1,288,128]{2,1,0:T(8,128)(2,1)S(1)} %bitcast.5), channel_id=1, source_target_pairs={{0,3},{1,2},{2,1},{3,0},{4,7},{5,6},{6,5},{7,4},{8,11},{9,10},{10,... | collective-permute-start | bytes 221192 | tf_op jit(solution)/shard_map/ppermute | solution.py:182
  8.1 2.3 %fetch.1 = (bf16[512,128]{1,0:T(8,128)(2,1)S(1)}, bf16[128,128,128]{2,1,0:T(8,128)(2,1)S(1)}, s32[1,128]{1,0:T(1,128)S(1)}) custom-call(bf16[512,128]{1,0:T(8,128)(2,1)} %cent_ref.1, bf16[128,128,128]{2,1,0:T(8,128)(2,1)} %pass_ref.1, s32[1,128]{1,0:T(1,128)} %len_ref.1), custom_call_target="tpu_custom_call" | custom-call | tf_op jit(solution)/shard_map/fetch/pallas_call | solution.py:171
  10.4 0.8 %collective-permute-start.1 = (bf16[1,288,128]{2,1,0:T(8,128)(2,1)S(1)}, bf16[1,288,128]{2,1,0:T(8,128)(2,1)S(1)}, u32[]{:S(2)}, u32[]{:S(2)}) collective-permute-start(bf16[1,288,128]{2,1,0:T(8,128)(2,1)S(1)} %collective-permute-done), channel_id=1, source_target_pairs={{0,5},{1,4},{2,7},{3,6},{4,1},{5,0},{6,3},{7,2},{8,13},{9,12},{10,... | collective-permute-start | bytes 221192 | tf_op jit(solution)/shard_map/ppermute | solution.py:182
  11.3 1.2 %collective-permute-start.3 = (bf16[2,288,128]{2,1,0:T(8,128)(2,1)S(1)}, bf16[2,288,128]{2,1,0:T(8,128)(2,1)S(1)}, u32[]{:S(2)}, u32[]{:S(2)}) collective-permute-start(bf16[2,288,128]{2,1,0:T(8,128)(2,1)S(1)} %constant_dynamic-update-slice_fusion.refs_1_), channel_id=1, source_target_pairs={{0,3},{1,2},{2,1},{3,0},{4,7},{5,6},{6,5},{7,4},{8,11},{9,10},{10,... | collective-permute-start | bytes 442376 | tf_op jit(solution)/shard_map/ppermute | solution.py:182
  12.5 1.1 %score.6 = (f32[1,1,384]{2,1,0:T(1,128)S(1)}, f32[2,1,384]{2,1,0:T(1,128)S(1)}) custom-call(bf16[1,288,128]{2,1,0:T(8,128)(2,1)S(1)} %bitcast.7, bf16[2,288,128]{2,1,0:T(8,128)(2,1)S(1)} %constant_dynamic-update-slice_fusion.refs_1_, bf16[512,128]{1,0:T(8,128)(2,1)S(1)} %get-tuple-element.32.refs_2_.refs_3_.refs_1_, ...), custom_call_target="tpu_custom_call" | custom-call | flops 301989888 | bytes 3145728 | tf_op jit(solution)/shard_map/score/pallas_call | solution.py:187
  13.6 0.6 %collective-permute-done.1.refs_0_ = bf16[1,288,128]{2,1,0:T(8,128)(2,1)S(1)} collective-permute-done((bf16[1,288,128]{2,1,0:T(8,128)(2,1)S(1)}, bf16[1,288,128]{2,1,0:T(8,128)(2,1)S(1)}, u32[]{:S(2)}, u32[]{:S(2)}) %collective-permute-start.1) | collective-permute-done | bytes 73760 | tf_op jit(solution)/shard_map/ppermute | solution.py:182
  14.2 1.7 %collective-permute-start.6 = (bf16[1,288,128]{2,1,0:T(8,128)(2,1)S(1)}, bf16[1,288,128]{2,1,0:T(8,128)(2,1)S(1)}, u32[]{:S(2)}, u32[]{:S(2)}) collective-permute-start(bf16[1,288,128]{2,1,0:T(8,128)(2,1)S(1)} %collective-permute-done.1.refs_0_), channel_id=1, source_target_pairs={{0,3},{1,2},{2,1},{3,0},{4,7},{5,6},{6,5},{7,4},{8,11},{9,10},{10,... | collective-permute-start | bytes 221192 | tf_op jit(solution)/shard_map/ppermute | solution.py:182
  16.2 1.7 %score.7 = (f32[1,1,384]{2,1,0:T(1,128)S(1)}, f32[1,1,384]{2,1,0:T(1,128)S(1)}, f32[3,1,384]{2,1,0:T(1,128)S(1)}) custom-call(bf16[1,288,128]{2,1,0:T(8,128)(2,1)S(1)} %collective-permute-done.1.refs_0_, bf16[1,288,128]{2,1,0:T(8,128)(2,1)S(1)} %collective-permute-done.4.refs_1_, bf16[3,288,128]{2,1,0:T(8,128)(2,1)S(1)} %collective-permute-done.5.refs_2_, ...), custom_call_target="tpu_custom_call" | custom-call | flops 503316480 | bytes 5242880 | tf_op jit(solution)/shard_map/score/pallas_call | solution.py:187
  18.3 1.3 %score.8 = (f32[2,1,384]{2,1,0:T(1,128)S(1)}, f32[2,1,384]{2,1,0:T(1,128)S(1)}) custom-call(bf16[2,288,128]{2,1,0:T(8,128)(2,1)S(1)} %collective-permute-done.7.refs_0_, bf16[2,288,128]{2,1,0:T(8,128)(2,1)S(1)} %collective-permute-done.3.refs_1_, bf16[512,128]{1,0:T(8,128)(2,1)S(1)} %get-tuple-element.32.refs_2_.refs_3_.refs_1_, ...), custom_call_target="tpu_custom_call" | custom-call | flops 402653184 | bytes 4194304 | tf_op jit(solution)/shard_map/score/pallas_call | solution.py:187
  19.8 0.6 %score.9 = f32[1,1,384]{2,1,0:T(1,128)S(1)} custom-call(bf16[1,288,128]{2,1,0:T(8,128)(2,1)S(1)} %collective-permute-done.6.refs_0_, bf16[512,128]{1,0:T(8,128)(2,1)S(1)} %get-tuple-element.32.refs_2_.refs_3_.refs_1_, bf16[128,128,128]{2,1,0:T(8,128)(2,1)S(1)} %get-tuple-element.33.refs_3_.refs_4_.refs_2_, s32[1,128]{1,0:T(1,128)S(1)} %get-tuple-element.34.refs_4_.refs_5_.refs_3_), custom_call_target="tpu_custom_call" | custom-call | flops 100663296 | bytes 1048576 | tf_op jit(solution)/shard_map/score/pallas_call | solution.py:187
  20.5 0.8 %score.10 = f32[2,1,384]{2,1,0:T(1,128)S(1)} custom-call(bf16[2,288,128]{2,1,0:T(8,128)(2,1)S(1)} %collective-permute-done.9.refs_0_, bf16[512,128]{1,0:T(8,128)(2,1)S(1)} %get-tuple-element.32.refs_2_.refs_3_.refs_1_, bf16[128,128,128]{2,1,0:T(8,128)(2,1)S(1)} %get-tuple-element.33.refs_3_.refs_4_.refs_2_, ...), custom_call_target="tpu_custom_call" | custom-call | flops 201326592 | bytes 2097152 | tf_op jit(solution)/shard_map/score/pallas_call | solution.py:187
  21.3 0.6 %score.11 = f32[1,1,384]{2,1,0:T(1,128)S(1)} custom-call(bf16[1,288,128]{2,1,0:T(8,128)(2,1)S(1)} %collective-permute-done.8.refs_0_, bf16[512,128]{1,0:T(8,128)(2,1)S(1)} %get-tuple-element.32.refs_2_.refs_3_.refs_1_, bf16[128,128,128]{2,1,0:T(8,128)(2,1)S(1)} %get-tuple-element.33.refs_3_.refs_4_.refs_2_, ...), custom_call_target="tpu_custom_call" | custom-call | flops 100663296 | bytes 1048576 | tf_op jit(solution)/shard_map/score/pallas_call | solution.py:187
  21.9 0.4 %collective-permute-start.10 = (f32[8,1,384]{2,1,0:T(1,128)S(1)}, f32[8,1,384]{2,1,0:T(1,128)S(1)}, u32[]{:S(2)}, u32[]{:S(2)}) collective-permute-start(f32[8,1,384]{2,1,0:T(1,128)S(1)} %pad_maximum_fusion.2), channel_id=1, source_target_pairs={{0,1},{1,0},{2,3},{3,2},{4,5},{5,4},{6,7},{7,6},{8,9},{9,8},{10,11... | collective-permute-start | bytes 36872 | tf_op jit(solution)/shard_map/ppermute | solution.py:182
  22.4 0.8 %collective-permute-done.10 = f32[8,1,384]{2,1,0:T(1,128)S(1)} collective-permute-done((f32[8,1,384]{2,1,0:T(1,128)S(1)}, f32[8,1,384]{2,1,0:T(1,128)S(1)}, u32[]{:S(2)}, u32[]{:S(2)}) %collective-permute-start.10) | collective-permute-done | bytes 12320 | tf_op jit(solution)/shard_map/ppermute | solution.py:182
  23.2 0.9 %collective-permute-start.11 = (f32[4,1,384]{2,1,0:T(1,128)S(1)}, f32[4,1,384]{2,1,0:T(1,128)S(1)}, u32[]{:S(2)}, u32[]{:S(2)}) collective-permute-start(f32[4,1,384]{2,1,0:T(1,128)S(1)} %slice.25), channel_id=1, source_target_pairs={{0,3},{1,2},{2,1},{3,0},{4,7},{5,6},{6,5},{7,4},{8,11},{9,10},{10,... | collective-permute-start | bytes 18440 | tf_op jit(solution)/shard_map/ppermute | solution.py:182
  24.1 2.2 %collective-permute-done.11 = f32[4,1,384]{2,1,0:T(1,128)S(1)} collective-permute-done((f32[4,1,384]{2,1,0:T(1,128)S(1)}, f32[4,1,384]{2,1,0:T(1,128)S(1)}, u32[]{:S(2)}, u32[]{:S(2)}) %collective-permute-start.11) | collective-permute-done | bytes 6176 | tf_op jit(solution)/shard_map/ppermute | solution.py:182
  26.4 1.6 %collective-permute-start.12 = (f32[2,1,384]{2,1,0:T(1,128)S(1)}, f32[2,1,384]{2,1,0:T(1,128)S(1)}, u32[]{:S(2)}, u32[]{:S(2)}) collective-permute-start(f32[2,1,384]{2,1,0:T(1,128)S(1)} %slice.27), channel_id=1, source_target_pairs={{0,5},{1,4},{2,7},{3,6},{4,1},{5,0},{6,3},{7,2},{8,13},{9,12},{10,... | collective-permute-start | bytes 9224 | tf_op jit(solution)/shard_map/ppermute | solution.py:182
  27.9 1.5 %collective-permute-done.12 = f32[2,1,384]{2,1,0:T(1,128)S(1)} collective-permute-done((f32[2,1,384]{2,1,0:T(1,128)S(1)}, f32[2,1,384]{2,1,0:T(1,128)S(1)}, u32[]{:S(2)}, u32[]{:S(2)}) %collective-permute-start.12) | collective-permute-done | bytes 3104 | tf_op jit(solution)/shard_map/ppermute | solution.py:182
  29.5 2.9 %collective-permute-start.13 = (f32[1,1,384]{2,1,0:T(1,128)S(1)}, f32[1,1,384]{2,1,0:T(1,128)S(1)}, u32[]{:S(2)}, u32[]{:S(2)}) collective-permute-start(f32[1,1,384]{2,1,0:T(1,128)S(1)} %get-tuple-element.54), channel_id=1, source_target_pairs={{0,9},{1,8},{2,11},{3,10},{4,13},{5,12},{6,15},{7,14},{8,1},{9,0},... | collective-permute-start | bytes 4616 | tf_op jit(solution)/shard_map/ppermute | solution.py:182
  32.4 1.3 %collective-permute-done.13.b_ref = f32[1,1,384]{2,1,0:T(1,128)S(1)} collective-permute-done((f32[1,1,384]{2,1,0:T(1,128)S(1)}, f32[1,1,384]{2,1,0:T(1,128)S(1)}, u32[]{:S(2)}, u32[]{:S(2)}) %collective-permute-start.13) | collective-permute-done | bytes 1568 | tf_op jit(solution)/shard_map/ppermute | solution.py:182
  33.7 0.7 %last.1 = (f32[8,32]{1,0:T(8,128)}, f32[8,16]{1,0:T(8,128)}) custom-call(f32[1,1,384]{2,1,0:T(1,128)S(1)} %get-tuple-element.55.a_ref, f32[1,1,384]{2,1,0:T(1,128)S(1)} %collective-permute-done.13.b_ref), custom_call_target="tpu_custom_call" | custom-call | tf_op jit(solution)/shard_map/last/pallas_call | solution.py:240
  (30 shorter events, 1.0 us)
Async XLA Ops:
  1.7 8.6 %collective-permute-start = (bf16[1,288,128]{2,1,0:T(8,128)(2,1)S(1)}, bf16[1,288,128]{2,1,0:T(8,128)(2,1)S(1)}, u32[]{:S(2)}, u32[]{:S(2)}) collective-permute-start(bf16[1,288,128]{2,1,0:T(8,128)(2,1)S(1)} %bitcast.3), channel_id=1, source_target_pairs={{0,9},{1,8},{2,11},{3,10},{4,13},{5,12},{6,15},{7,14},{8,1},{9,0},... | collective-permute-start | bytes 221192 | tf_op jit(solution)/shard_map/ppermute | solution.py:182
  5.3 5.9 %collective-permute-start.2 = (bf16[1,288,128]{2,1,0:T(8,128)(2,1)S(1)}, bf16[1,288,128]{2,1,0:T(8,128)(2,1)S(1)}, u32[]{:S(2)}, u32[]{:S(2)}) collective-permute-start(bf16[1,288,128]{2,1,0:T(8,128)(2,1)S(1)} %bitcast.4), channel_id=1, source_target_pairs={{0,5},{1,4},{2,7},{3,6},{4,1},{5,0},{6,3},{7,2},{8,13},{9,12},{10,... | collective-permute-start | bytes 221192 | tf_op jit(solution)/shard_map/ppermute | solution.py:182
  7.1 8.8 %collective-permute-start.4 = (bf16[1,288,128]{2,1,0:T(8,128)(2,1)S(1)}, bf16[1,288,128]{2,1,0:T(8,128)(2,1)S(1)}, u32[]{:S(2)}, u32[]{:S(2)}) collective-permute-start(bf16[1,288,128]{2,1,0:T(8,128)(2,1)S(1)} %bitcast.5), channel_id=1, source_target_pairs={{0,3},{1,2},{2,1},{3,0},{4,7},{5,6},{6,5},{7,4},{8,11},{9,10},{10,... | collective-permute-start | bytes 221192 | tf_op jit(solution)/shard_map/ppermute | solution.py:182
  10.4 3.8 %collective-permute-start.1 = (bf16[1,288,128]{2,1,0:T(8,128)(2,1)S(1)}, bf16[1,288,128]{2,1,0:T(8,128)(2,1)S(1)}, u32[]{:S(2)}, u32[]{:S(2)}) collective-permute-start(bf16[1,288,128]{2,1,0:T(8,128)(2,1)S(1)} %collective-permute-done), channel_id=1, source_target_pairs={{0,5},{1,4},{2,7},{3,6},{4,1},{5,0},{6,3},{7,2},{8,13},{9,12},{10,... | collective-permute-start | bytes 221192 | tf_op jit(solution)/shard_map/ppermute | solution.py:182
  11.2 5.0 %collective-permute-start.5 = (bf16[3,288,128]{2,1,0:T(8,128)(2,1)S(1)}, bf16[3,288,128]{2,1,0:T(8,128)(2,1)S(1)}, u32[]{:S(2)}, u32[]{:S(2)}) collective-permute-start(bf16[3,288,128]{2,1,0:T(8,128)(2,1)S(1)} %pad_maximum_fusion), channel_id=1, source_target_pairs={{0,1},{1,0},{2,3},{3,2},{4,5},{5,4},{6,7},{7,6},{8,9},{9,8},{10,11... | collective-permute-start | bytes 663560 | tf_op jit(solution)/shard_map/ppermute | solution.py:182
  11.3 6.6 %collective-permute-start.3 = (bf16[2,288,128]{2,1,0:T(8,128)(2,1)S(1)}, bf16[2,288,128]{2,1,0:T(8,128)(2,1)S(1)}, u32[]{:S(2)}, u32[]{:S(2)}) collective-permute-start(bf16[2,288,128]{2,1,0:T(8,128)(2,1)S(1)} %constant_dynamic-update-slice_fusion.refs_1_), channel_id=1, source_target_pairs={{0,3},{1,2},{2,1},{3,0},{4,7},{5,6},{6,5},{7,4},{8,11},{9,10},{10,... | collective-permute-start | bytes 442376 | tf_op jit(solution)/shard_map/ppermute | solution.py:182
  14.2 5.4 %collective-permute-start.6 = (bf16[1,288,128]{2,1,0:T(8,128)(2,1)S(1)}, bf16[1,288,128]{2,1,0:T(8,128)(2,1)S(1)}, u32[]{:S(2)}, u32[]{:S(2)}) collective-permute-start(bf16[1,288,128]{2,1,0:T(8,128)(2,1)S(1)} %collective-permute-done.1.refs_0_), channel_id=1, source_target_pairs={{0,3},{1,2},{2,1},{3,0},{4,7},{5,6},{6,5},{7,4},{8,11},{9,10},{10,... | collective-permute-start | bytes 221192 | tf_op jit(solution)/shard_map/ppermute | solution.py:182
  15.9 2.3 %collective-permute-start.7 = (bf16[2,288,128]{2,1,0:T(8,128)(2,1)S(1)}, bf16[2,288,128]{2,1,0:T(8,128)(2,1)S(1)}, u32[]{:S(2)}, u32[]{:S(2)}) collective-permute-start(bf16[2,288,128]{2,1,0:T(8,128)(2,1)S(1)} %pad_maximum_fusion.1), channel_id=1, source_target_pairs={{0,1},{1,0},{2,3},{3,2},{4,5},{5,4},{6,7},{7,6},{8,9},{9,8},{10,11... | collective-permute-start | bytes 442376 | tf_op jit(solution)/shard_map/ppermute | solution.py:182
  17.9 2.5 %collective-permute-start.9 = (bf16[2,288,128]{2,1,0:T(8,128)(2,1)S(1)}, bf16[2,288,128]{2,1,0:T(8,128)(2,1)S(1)}, u32[]{:S(2)}, u32[]{:S(2)}) collective-permute-start(bf16[2,288,128]{2,1,0:T(8,128)(2,1)S(1)} %collective-permute-done.3.refs_1_), channel_id=1, source_target_pairs={{0,1},{1,0},{2,3},{3,2},{4,5},{5,4},{6,7},{7,6},{8,9},{9,8},{10,11... | collective-permute-start | bytes 442376 | tf_op jit(solution)/shard_map/ppermute | solution.py:182
  19.6 1.7 %collective-permute-start.8 = (bf16[1,288,128]{2,1,0:T(8,128)(2,1)S(1)}, bf16[1,288,128]{2,1,0:T(8,128)(2,1)S(1)}, u32[]{:S(2)}, u32[]{:S(2)}) collective-permute-start(bf16[1,288,128]{2,1,0:T(8,128)(2,1)S(1)} %collective-permute-done.6.refs_0_), channel_id=1, source_target_pairs={{0,1},{1,0},{2,3},{3,2},{4,5},{5,4},{6,7},{7,6},{8,9},{9,8},{10,11... | collective-permute-start | bytes 221192 | tf_op jit(solution)/shard_map/ppermute | solution.py:182
  21.9 1.3 %collective-permute-start.10 = (f32[8,1,384]{2,1,0:T(1,128)S(1)}, f32[8,1,384]{2,1,0:T(1,128)S(1)}, u32[]{:S(2)}, u32[]{:S(2)}) collective-permute-start(f32[8,1,384]{2,1,0:T(1,128)S(1)} %pad_maximum_fusion.2), channel_id=1, source_target_pairs={{0,1},{1,0},{2,3},{3,2},{4,5},{5,4},{6,7},{7,6},{8,9},{9,8},{10,11... | collective-permute-start | bytes 36872 | tf_op jit(solution)/shard_map/ppermute | solution.py:182
  23.2 3.1 %collective-permute-start.11 = (f32[4,1,384]{2,1,0:T(1,128)S(1)}, f32[4,1,384]{2,1,0:T(1,128)S(1)}, u32[]{:S(2)}, u32[]{:S(2)}) collective-permute-start(f32[4,1,384]{2,1,0:T(1,128)S(1)} %slice.25), channel_id=1, source_target_pairs={{0,3},{1,2},{2,1},{3,0},{4,7},{5,6},{6,5},{7,4},{8,11},{9,10},{10,... | collective-permute-start | bytes 18440 | tf_op jit(solution)/shard_map/ppermute | solution.py:182
  26.4 3.1 %collective-permute-start.12 = (f32[2,1,384]{2,1,0:T(1,128)S(1)}, f32[2,1,384]{2,1,0:T(1,128)S(1)}, u32[]{:S(2)}, u32[]{:S(2)}) collective-permute-start(f32[2,1,384]{2,1,0:T(1,128)S(1)} %slice.27), channel_id=1, source_target_pairs={{0,5},{1,4},{2,7},{3,6},{4,1},{5,0},{6,3},{7,2},{8,13},{9,12},{10,... | collective-permute-start | bytes 9224 | tf_op jit(solution)/shard_map/ppermute | solution.py:182
  29.5 4.2 %collective-permute-start.13 = (f32[1,1,384]{2,1,0:T(1,128)S(1)}, f32[1,1,384]{2,1,0:T(1,128)S(1)}, u32[]{:S(2)}, u32[]{:S(2)}) collective-permute-start(f32[1,1,384]{2,1,0:T(1,128)S(1)} %get-tuple-element.54), channel_id=1, source_target_pairs={{0,9},{1,8},{2,11},{3,10},{4,13},{5,12},{6,15},{7,14},{8,1},{9,0},... | collective-permute-start | bytes 4616 | tf_op jit(solution)/shard_map/ppermute | solution.py:182

commit v3 on v2

--- a/solution.py
+++ b/solution.py
@@ -60,17 +60,6 @@
     out_ref[tokens:tokens + HEAD] = jnp.where(head == 0, owner, jnp.where(head == 1, own_rank, 0.0)).astype(out_ref.dtype)
     out_ref[tokens + HEAD:] = table.astype(out_ref.dtype)
     copies[2].wait()
-
-
-def fetch_kernel(cent_ref, pass_ref, len_ref, cent_out, pass_out, len_out, sems):
-    copies = [
-        pltpu.make_async_copy(source, target, sems.at[n])
-        for n, (source, target) in enumerate(((cent_ref, cent_out), (pass_ref, pass_out), (len_ref, len_out)))
-    ]
-    for copy in copies:
-        copy.start()
-    for copy in copies:
-        copy.wait()
 
 
 def score_kernel(slots, qt, counts, *refs):
@@ -165,18 +154,11 @@
             pltpu.SemaphoreType.DMA((3,)),
         ],
         compiler_params=pltpu.CompilerParams(vmem_limit_bytes=2 * MIB),
+        cost_estimate=pl.CostEstimate(flops=int(1e10), bytes_accessed=1000, transcendentals=0),
         name="pack",
     )(stay(queries.reshape(tokens, dim)), stay(cand_owner.reshape(q_dev, cand)), stay(cand_row))
 
-    index = pl.pallas_call(
-        fetch_kernel,
-        out_shape=[pltpu.VMEM(x.shape, x.dtype) for x in (centroids, passages, lengths)],
-        in_specs=[hbm] * 3,
-        out_specs=[vmem] * 3,
-        scratch_shapes=[pltpu.SemaphoreType.DMA((3,))],
-        compiler_params=pltpu.CompilerParams(vmem_limit_bytes=MIB),
-        name="fetch",
-    )(stay(centroids), stay(passages), stay(lengths))
+    index = tuple(pltpu.with_memory_space_constraint(x, pltpu.VMEM) for x in (centroids, passages, lengths))
 
     def swap(x, k):
         return lax.ppermute(x, "shard", [(i, i ^ k) for i in range(shards)])
@@ -204,39 +186,58 @@
     first = block[None]
     for k in far[:-2]:
         first = jnp.concatenate([first, swap(first, k)], axis=0)
-    second = swap(first, far[-2])
-    third = swap(first, far[-1])
-    xa = swap(first, 3)
-    second, index = lax.optimization_barrier((second, index))
-    fourth = swap(second, far[-1])
-    near3 = jnp.concatenate([second, third], axis=0)
-    xb = swap(near3, 3)
-    c1 = swap(jnp.concatenate([first, near3], axis=0), 1)
-    s1 = score(first, near3)
-    fourth, s1 = lax.optimization_barrier((fourth, s1))
-    xc = swap(fourth, 3)
-    c2 = swap(jnp.concatenate([fourth, xa], axis=0), 1)
-    s2 = score(fourth, xa, c1)
-    xb, s2 = lax.optimization_barrier((xb, s2))
-    c3 = swap(xb, 1)
-    s3 = score(c2, xb)
-    xc, s3 = lax.optimization_barrier((xc, s3))
-    c4 = swap(xc, 1)
-    s4 = score(c3)
-    c4, s4 = lax.optimization_barrier((c4, s4))
-    s5 = score(c4)
-    other = jnp.concatenate([s2[2], s3[0], s4[0], s5[0]], axis=0)
+    f, g = far[-2:]
+    d = g ^ 3 ^ 1
+    piece = {0: first}
+    for k in (f, 3, g, d):
+        piece[k] = swap(first, k)
+    for k in (d, 3, g):
+        piece[f ^ k] = swap(piece[f], k)
+    m = first.shape[0]
+    score_of = {}
+
+    def cut(x, keys):
+        return {k: x[n * m:(n + 1) * m] for n, k in enumerate(keys)}
+
+    def join(table, keys):
+        return jnp.concatenate([table[k] for k in keys], axis=0)
+
+    def across(keys):
+        return swap(join(piece, keys), 1)
+
+    xa, xb = (3, d), (f ^ d, f ^ 3)
+    early = (0, f, g, 3, d)
+    scores = score(*(piece[k] for k in early))
+    scores, piece[xb[0]], piece[xb[1]] = lax.optimization_barrier((scores, piece[xb[0]], piece[xb[1]]))
+    score_of.update(zip(early, scores))
+    ca, cb = across(xa), across(xb)
+    *scores, ca = score(*(piece[k] for k in xb), ca)
+    score_of.update(zip(xb, scores))
+    score_of.update(cut(ca, [k ^ 1 for k in xa]))
+    ca, cb = lax.optimization_barrier((ca, cb))
+    score_of.update(cut(score(cb)[0], [k ^ 1 for k in xb]))
+
+    def back(keys, k):
+        got = cut(swap(join(score_of, [key ^ k for key in keys]), k), keys)
+        return lambda: {key: jnp.maximum(score_of[key], got[key]) for key in keys}
+
+    column = (0, f, g, f ^ g)
+    near = column + tuple(k ^ 1 for k in column)
+    take = back(near, 3)
+    rest = (f ^ g, *(k ^ 1 for k in column))
+    cc = across(column)
+    sd = score(piece[f ^ g], cc)
+    score_of[f ^ g] = sd[0]
+    score_of.update(cut(sd[1], rest[1:]))
+    score_of = take()
+    score_of = back((0, f, 1, f ^ 1), g)()
+    score_of = back((0, 1), f)()
+    mine, other = score_of[0], score_of[1]
+    for k in far[:-2][::-1]:
+        half = mine.shape[0] // 2
+        got = swap(jnp.concatenate([mine[half:], other[half:]], axis=0), k)
+        mine, other = jnp.maximum(mine[:half], got[:half]), jnp.maximum(other[:half], got[half:])
     got = swap(other, 1)
-    s6 = score(xc)
-    near = jnp.concatenate([s1[0], s1[1], s2[0], s2[1], s3[1], s6[0]], axis=0)
-    result = jnp.maximum(near, got)
-    for k in [3] + far[::-1]:
-        half = result.shape[0] // 2
-        got = swap(result[half:], k)
-        if half > 1:
-            result = jnp.maximum(result[:half], got)
-        else:
-            mine = result[:half]
     return pl.pallas_call(
         last_kernel,
         out_shape=(jax.ShapeDtypeStruct((q_dev, qt), jnp.float32), jax.ShapeDtypeStruct((q_dev, cand), jnp.float32)),

time: 34.6 us -> 33.1 us (0.957)
  Pallas kernels: 10.3 us -> 7.56 us
  waiting for transfers between devices: 6.53 us -> 8.39 us
  starting transfers between devices: 16.7 us -> 16.1 us
    pallas_call x1 -> x0, Pallas kernels: 2.29 us -> none  [body(): pl.pallas_call(fetch_kernel, out_shape=[pltpu.VMEM(x.shape, x.dtype) for...]
    ppermute x14, waiting for transfers between devices: 6.53 us -> 8.39 us  [swap(): return lax.ppermute(x, 'shard', [(i, i ^ k) for i in range(shards)])]
    pallas_call x6 -> x4, Pallas kernels: 6.23 us -> 5.65 us  [score(): pl.pallas_call(functools.partial(score_kernel, slots, qt, counts), out_sh...]
    ppermute x14, starting transfers between devices: 16.7 us -> 16.1 us  [swap(): return lax.ppermute(x, 'shard', [(i, i ^ k) for i in range(shards)])]
  transfers between devices with their start and end apart: 14 -> 14, of which waited for: 5 -> 6; matrix products, arithmetic and copies ran while one was open for 0% -> 0% of each run, Pallas kernels for 23% -> 17%
where the time goes in v3:
time: 33.1 us; the launch traced here: 33 us
  starting transfers between devices  16.1 us (49%)
  waiting for transfers between devices  8.39 us (25%)
  Pallas kernels  7.56 us (23%)
  between operations  0.73 us (2%)
    ppermute x14, starting transfers between devices, swap(): return lax.ppermute(x, 'shard', [(i, i ^ k) for i in range(shards)])  16.1 us
    ppermute x14, waiting for transfers between devices, swap(): return lax.ppermute(x, 'shard', [(i, i ^ k) for i in range(shards)])  8.39 us
    pallas_call x4, Pallas kernels, score(): pl.pallas_call(functools.partial(score_kernel, slots, qt, counts), out_sh...  5.65 us
    pallas_call x1, Pallas kernels, body(): pl.pallas_call(functools.partial(pack_kernel, slots), out_shape=pltpu.VME...  1.23 us
    pallas_call x1, Pallas kernels, body(): pl.pallas_call(last_kernel, out_shape=(jax.ShapeDtypeStruct((q_dev, qt),...  0.68 us
  transfers between devices with their start and end apart: 14, of which 6 were waited for; matrix products, arithmetic and copies ran while one was open for 0% of the time, Pallas kernels for 17%

profile of v3, /device:TPU:0, one launch (start us, length us, event | category | flops | bytes accessed | tf_op | source)
XLA Modules:
  0.0 33.0 jit_solution(3717251150184248330)
XLA Ops:
  0.7 1.2 %pack.1 = bf16[288,128]{1,0:T(8,128)(2,1)S(1)} custom-call(bf16[256,128]{1,0:T(8,128)(2,1)} %bitcast.9, s32[8,16]{1,0:T(8,128)} %bitcast.10, s32[8,16]{1,0:T(8,128)} %row_ref.1), custom_call_target="tpu_custom_call" | custom-call | flops 10000000000 | bytes 1000 | tf_op jit(solution)/shard_map/pack/pallas_call | solution.py:146
  1.9 3.5 %collective-permute-start = (bf16[1,288,128]{2,1,0:T(8,128)(2,1)S(1)}, bf16[1,288,128]{2,1,0:T(8,128)(2,1)S(1)}, u32[]{:S(2)}, u32[]{:S(2)}) collective-permute-start(bf16[1,288,128]{2,1,0:T(8,128)(2,1)S(1)} %bitcast.3), channel_id=1, source_target_pairs={{0,9},{1,8},{2,11},{3,10},{4,13},{5,12},{6,15},{7,14},{8,1},{9,0},... | collective-permute-start | bytes 221192 | tf_op jit(solution)/shard_map/ppermute | solution.py:164
  5.4 1.8 %collective-permute-start.2 = (bf16[1,288,128]{2,1,0:T(8,128)(2,1)S(1)}, bf16[1,288,128]{2,1,0:T(8,128)(2,1)S(1)}, u32[]{:S(2)}, u32[]{:S(2)}) collective-permute-start(bf16[1,288,128]{2,1,0:T(8,128)(2,1)S(1)} %bitcast.4), channel_id=1, source_target_pairs={{0,3},{1,2},{2,1},{3,0},{4,7},{5,6},{6,5},{7,4},{8,11},{9,10},{10,... | collective-permute-start | bytes 221192 | tf_op jit(solution)/shard_map/ppermute | solution.py:164
  7.2 1.0 %collective-permute-start.3 = (bf16[1,288,128]{2,1,0:T(8,128)(2,1)S(1)}, bf16[1,288,128]{2,1,0:T(8,128)(2,1)S(1)}, u32[]{:S(2)}, u32[]{:S(2)}) collective-permute-start(bf16[1,288,128]{2,1,0:T(8,128)(2,1)S(1)} %bitcast.5), channel_id=1, source_target_pairs={{0,7},{1,6},{2,5},{3,4},{4,3},{5,2},{6,1},{7,0},{8,15},{9,14},{10,... | collective-permute-start | bytes 221192 | tf_op jit(solution)/shard_map/ppermute | solution.py:164
  8.2 0.7 %collective-permute-start.1 = (bf16[1,288,128]{2,1,0:T(8,128)(2,1)S(1)}, bf16[1,288,128]{2,1,0:T(8,128)(2,1)S(1)}, u32[]{:S(2)}, u32[]{:S(2)}) collective-permute-start(bf16[1,288,128]{2,1,0:T(8,128)(2,1)S(1)} %bitcast.6), channel_id=1, source_target_pairs={{0,5},{1,4},{2,7},{3,6},{4,1},{5,0},{6,3},{7,2},{8,13},{9,12},{10,... | collective-permute-start | bytes 221192 | tf_op jit(solution)/shard_map/ppermute | solution.py:164
  8.9 2.9 %collective-permute-start.4 = (bf16[1,288,128]{2,1,0:T(8,128)(2,1)S(1)}, bf16[1,288,128]{2,1,0:T(8,128)(2,1)S(1)}, u32[]{:S(2)}, u32[]{:S(2)}) collective-permute-start(bf16[1,288,128]{2,1,0:T(8,128)(2,1)S(1)} %collective-permute-done.refs_1_), channel_id=1, source_target_pairs={{0,7},{1,6},{2,5},{3,4},{4,3},{5,2},{6,1},{7,0},{8,15},{9,14},{10,... | collective-permute-start | bytes 221192 | tf_op jit(solution)/shard_map/ppermute | solution.py:164
  11.8 0.5 %collective-permute-start.5 = (bf16[1,288,128]{2,1,0:T(8,128)(2,1)S(1)}, bf16[1,288,128]{2,1,0:T(8,128)(2,1)S(1)}, u32[]{:S(2)}, u32[]{:S(2)}) collective-permute-start(bf16[1,288,128]{2,1,0:T(8,128)(2,1)S(1)} %collective-permute-done.refs_1_), channel_id=1, source_target_pairs={{0,3},{1,2},{2,1},{3,0},{4,7},{5,6},{6,5},{7,4},{8,11},{9,10},{10,... | collective-permute-start | bytes 221192 | tf_op jit(solution)/shard_map/ppermute | solution.py:164
  12.4 0.6 %collective-permute-done.3.refs_4_ = bf16[1,288,128]{2,1,0:T(8,128)(2,1)S(1)} collective-permute-done((bf16[1,288,128]{2,1,0:T(8,128)(2,1)S(1)}, bf16[1,288,128]{2,1,0:T(8,128)(2,1)S(1)}, u32[]{:S(2)}, u32[]{:S(2)}) %collective-permute-start.3) | collective-permute-done | bytes 73760 | tf_op jit(solution)/shard_map/ppermute | solution.py:164
  13.2 1.3 %collective-permute-start.9 = (bf16[1,288,128]{2,1,0:T(8,128)(2,1)S(1)}, bf16[1,288,128]{2,1,0:T(8,128)(2,1)S(1)}, u32[]{:S(2)}, u32[]{:S(2)}) collective-permute-start(bf16[1,288,128]{2,1,0:T(8,128)(2,1)S(1)} %collective-permute-done.refs_1_), channel_id=1, source_target_pairs={{0,5},{1,4},{2,7},{3,6},{4,1},{5,0},{6,3},{7,2},{8,13},{9,12},{10,... | collective-permute-start | bytes 221192 | tf_op jit(solution)/shard_map/ppermute | solution.py:164
  14.5 1.7 %score.4 = (f32[1,1,384]{2,1,0:T(1,128)S(1)}, f32[1,1,384]{2,1,0:T(1,128)S(1)}, f32[1,1,384]{2,1,0:T(1,128)S(1)}, f32[1,1,384]{2,1,0:T(1,128)S(1)}, f32[1,1,384]{2,1,0:T(1,128)S(1)}) custom-call(bf16[1,288,128]{2,1,0:T(8,128)(2,1)S(1)} %bitcast.7, bf16[1,288,128]{2,1,0:T(8,128)(2,1)S(1)} %collective-permute-done.refs_1_, ...), custom_call_target="tpu_custom_call" | custom-call | flops 503316480 | bytes 5242880 | tf_op jit(solution)/shard_map/score/pallas_call | solution.py:169
  16.2 1.5 %collective-permute-done.5.refs_1_ = bf16[1,288,128]{2,1,0:T(8,128)(2,1)S(1)} collective-permute-done((bf16[1,288,128]{2,1,0:T(8,128)(2,1)S(1)}, bf16[1,288,128]{2,1,0:T(8,128)(2,1)S(1)}, u32[]{:S(2)}, u32[]{:S(2)}) %collective-permute-start.5) | collective-permute-done | bytes 73760 | tf_op jit(solution)/shard_map/ppermute | solution.py:164
  17.9 0.5 %collective-permute-start.10 = (bf16[4,288,128]{2,1,0:T(8,128)(2,1)S(1)}, bf16[4,288,128]{2,1,0:T(8,128)(2,1)S(1)}, u32[]{:S(2)}, u32[]{:S(2)}) collective-permute-start(bf16[4,288,128]{2,1,0:T(8,128)(2,1)S(1)} %pad_maximum_fusion), channel_id=1, source_target_pairs={{0,1},{1,0},{2,3},{3,2},{4,5},{5,4},{6,7},{7,6},{8,9},{9,8},{10,11... | collective-permute-start | bytes 884744 | tf_op jit(solution)/shard_map/ppermute | solution.py:164
  18.4 1.5 %score.5 = (f32[1,1,384]{2,1,0:T(1,128)S(1)}, f32[1,1,384]{2,1,0:T(1,128)S(1)}, f32[2,1,384]{2,1,0:T(1,128)S(1)}) custom-call(bf16[1,288,128]{2,1,0:T(8,128)(2,1)S(1)} %collective-permute-done.4.refs_0_, bf16[1,288,128]{2,1,0:T(8,128)(2,1)S(1)} %collective-permute-done.5.refs_1_, bf16[2,288,128]{2,1,0:T(8,128)(2,1)S(1)} %collective-permute-done.6.refs_2_, ...), custom_call_target="tpu_custom_call" | custom-call | flops 402653184 | bytes 4194304 | tf_op jit(solution)/shard_map/score/pallas_call | solution.py:169
  19.9 0.8 %score.6 = f32[2,1,384]{2,1,0:T(1,128)S(1)} custom-call(bf16[2,288,128]{2,1,0:T(8,128)(2,1)S(1)} %collective-permute-done.7.refs_0_, bf16[512,128]{1,0:T(8,128)(2,1)S(1)} %copy-done.1, bf16[128,128,128]{2,1,0:T(8,128)(2,1)S(1)} %copy-done, s32[1,128]{1,0:T(1,128)S(1)} %copy-done.2), custom_call_target="tpu_custom_call" | custom-call | flops 201326592 | bytes 2097152 | tf_op jit(solution)/shard_map/score/pallas_call | solution.py:169
  20.7 0.4 %collective-permute-start.8 = (f32[8,1,384]{2,1,0:T(1,128)S(1)}, f32[8,1,384]{2,1,0:T(1,128)S(1)}, u32[]{:S(2)}, u32[]{:S(2)}) collective-permute-start(f32[8,1,384]{2,1,0:T(1,128)S(1)} %constant_dynamic-update-slice_fusion), channel_id=1, source_target_pairs={{0,3},{1,2},{2,1},{3,0},{4,7},{5,6},{6,5},{7,4},{8,11},{9,10},{10,... | collective-permute-start | bytes 36872 | tf_op jit(solution)/shard_map/ppermute | solution.py:164
  21.1 1.6 %score.7 = (f32[1,1,384]{2,1,0:T(1,128)S(1)}, f32[4,1,384]{2,1,0:T(1,128)S(1)}) custom-call(bf16[1,288,128]{2,1,0:T(8,128)(2,1)S(1)} %collective-permute-done.9.refs_0_, bf16[4,288,128]{2,1,0:T(8,128)(2,1)S(1)} %collective-permute-done.10.refs_1_, bf16[512,128]{1,0:T(8,128)(2,1)S(1)} %copy-done.1, bf16[128,128,128]{2,1,0:T(8,128)(2,1)S(1)} %copy-done, ...), custom_call_target="tpu_custom_call" | custom-call | flops 503316480 | bytes 5242880 | tf_op jit(solution)/shard_map/score/pallas_call | solution.py:169
  22.7 1.2 %collective-permute-done.8 = f32[8,1,384]{2,1,0:T(1,128)S(1)} collective-permute-done((f32[8,1,384]{2,1,0:T(1,128)S(1)}, f32[8,1,384]{2,1,0:T(1,128)S(1)}, u32[]{:S(2)}, u32[]{:S(2)}) %collective-permute-start.8) | collective-permute-done | bytes 12320 | tf_op jit(solution)/shard_map/ppermute | solution.py:164
  23.9 1.1 %collective-permute-start.11 = (f32[4,1,384]{2,1,0:T(1,128)S(1)}, f32[4,1,384]{2,1,0:T(1,128)S(1)}, u32[]{:S(2)}, u32[]{:S(2)}) collective-permute-start(f32[4,1,384]{2,1,0:T(1,128)S(1)} %pad_maximum_fusion.3), channel_id=1, source_target_pairs={{0,5},{1,4},{2,7},{3,6},{4,1},{5,0},{6,3},{7,2},{8,13},{9,12},{10,... | collective-permute-start | bytes 18440 | tf_op jit(solution)/shard_map/ppermute | solution.py:164
  25.1 2.0 %collective-permute-done.11 = f32[4,1,384]{2,1,0:T(1,128)S(1)} collective-permute-done((f32[4,1,384]{2,1,0:T(1,128)S(1)}, f32[4,1,384]{2,1,0:T(1,128)S(1)}, u32[]{:S(2)}, u32[]{:S(2)}) %collective-permute-start.11) | collective-permute-done | bytes 6176 | tf_op jit(solution)/shard_map/ppermute | solution.py:164
  27.1 1.9 %collective-permute-start.12 = (f32[2,1,384]{2,1,0:T(1,128)S(1)}, f32[2,1,384]{2,1,0:T(1,128)S(1)}, u32[]{:S(2)}, u32[]{:S(2)}) collective-permute-start(f32[2,1,384]{2,1,0:T(1,128)S(1)} %pad_maximum_fusion.4), channel_id=1, source_target_pairs={{0,9},{1,8},{2,11},{3,10},{4,13},{5,12},{6,15},{7,14},{8,1},{9,0},... | collective-permute-start | bytes 9224 | tf_op jit(solution)/shard_map/ppermute | solution.py:164
  29.0 2.1 %collective-permute-done.12 = f32[2,1,384]{2,1,0:T(1,128)S(1)} collective-permute-done((f32[2,1,384]{2,1,0:T(1,128)S(1)}, f32[2,1,384]{2,1,0:T(1,128)S(1)}, u32[]{:S(2)}, u32[]{:S(2)}) %collective-permute-start.12) | collective-permute-done | bytes 3104 | tf_op jit(solution)/shard_map/ppermute | solution.py:164
  31.1 0.2 collective-permute-start.13
  31.3 1.0 %collective-permute-done.13.b_ref = f32[1,1,384]{2,1,0:T(1,128)S(1)} collective-permute-done((f32[1,1,384]{2,1,0:T(1,128)S(1)}, f32[1,1,384]{2,1,0:T(1,128)S(1)}, u32[]{:S(2)}, u32[]{:S(2)}) %collective-permute-start.13) | collective-permute-done | bytes 1568 | tf_op jit(solution)/shard_map/ppermute | solution.py:164
  32.3 0.7 %last.1 = (f32[8,32]{1,0:T(8,128)}, f32[8,16]{1,0:T(8,128)}) custom-call(f32[1,1,384]{2,1,0:T(1,128)S(1)} %get-tuple-element.39.a_ref, f32[1,1,384]{2,1,0:T(1,128)S(1)} %collective-permute-done.13.b_ref), custom_call_target="tpu_custom_call" | custom-call | tf_op jit(solution)/shard_map/last/pallas_call | solution.py:241
  (32 shorter events, 0.6 us)
Async XLA Ops:
  0.6 13.8 %copy-start = (bf16[128,128,128]{2,1,0:T(8,128)(2,1)S(1)}, bf16[128,128,128]{2,1,0:T(8,128)(2,1)}, u32[]{:S(2)}) copy-start(bf16[128,128,128]{2,1,0:T(8,128)(2,1)} %refs_3_.5) | copy-start | bytes 12582916
  0.6 13.8 %copy-start.1 = (bf16[512,128]{1,0:T(8,128)(2,1)S(1)}, bf16[512,128]{1,0:T(8,128)(2,1)}, u32[]{:S(2)}) copy-start(bf16[512,128]{1,0:T(8,128)(2,1)} %refs_2_.3) | copy-start | bytes 393220
  0.7 13.8 %copy-start.2 = (s32[1,128]{1,0:T(1,128)S(1)}, s32[1,128]{1,0:T(1,128)}, u32[]{:S(2)}) copy-start(s32[1,128]{1,0:T(1,128)} %refs_4_.3) | copy-start | bytes 1540
  1.9 7.0 %collective-permute-start = (bf16[1,288,128]{2,1,0:T(8,128)(2,1)S(1)}, bf16[1,288,128]{2,1,0:T(8,128)(2,1)S(1)}, u32[]{:S(2)}, u32[]{:S(2)}) collective-permute-start(bf16[1,288,128]{2,1,0:T(8,128)(2,1)S(1)} %bitcast.3), channel_id=1, source_target_pairs={{0,9},{1,8},{2,11},{3,10},{4,13},{5,12},{6,15},{7,14},{8,1},{9,0},... | collective-permute-start | bytes 221192 | tf_op jit(solution)/shard_map/ppermute | solution.py:164
  5.4 6.9 %collective-permute-start.2 = (bf16[1,288,128]{2,1,0:T(8,128)(2,1)S(1)}, bf16[1,288,128]{2,1,0:T(8,128)(2,1)S(1)}, u32[]{:S(2)}, u32[]{:S(2)}) collective-permute-start(bf16[1,288,128]{2,1,0:T(8,128)(2,1)S(1)} %bitcast.4), channel_id=1, source_target_pairs={{0,3},{1,2},{2,1},{3,0},{4,7},{5,6},{6,5},{7,4},{8,11},{9,10},{10,... | collective-permute-start | bytes 221192 | tf_op jit(solution)/shard_map/ppermute | solution.py:164
  7.2 5.8 %collective-permute-start.3 = (bf16[1,288,128]{2,1,0:T(8,128)(2,1)S(1)}, bf16[1,288,128]{2,1,0:T(8,128)(2,1)S(1)}, u32[]{:S(2)}, u32[]{:S(2)}) collective-permute-start(bf16[1,288,128]{2,1,0:T(8,128)(2,1)S(1)} %bitcast.5), channel_id=1, source_target_pairs={{0,7},{1,6},{2,5},{3,4},{4,3},{5,2},{6,1},{7,0},{8,15},{9,14},{10,... | collective-permute-start | bytes 221192 | tf_op jit(solution)/shard_map/ppermute | solution.py:164
  8.2 6.2 %collective-permute-start.1 = (bf16[1,288,128]{2,1,0:T(8,128)(2,1)S(1)}, bf16[1,288,128]{2,1,0:T(8,128)(2,1)S(1)}, u32[]{:S(2)}, u32[]{:S(2)}) collective-permute-start(bf16[1,288,128]{2,1,0:T(8,128)(2,1)S(1)} %bitcast.6), channel_id=1, source_target_pairs={{0,5},{1,4},{2,7},{3,6},{4,1},{5,0},{6,3},{7,2},{8,13},{9,12},{10,... | collective-permute-start | bytes 221192 | tf_op jit(solution)/shard_map/ppermute | solution.py:164
  8.9 7.3 %collective-permute-start.4 = (bf16[1,288,128]{2,1,0:T(8,128)(2,1)S(1)}, bf16[1,288,128]{2,1,0:T(8,128)(2,1)S(1)}, u32[]{:S(2)}, u32[]{:S(2)}) collective-permute-start(bf16[1,288,128]{2,1,0:T(8,128)(2,1)S(1)} %collective-permute-done.refs_1_), channel_id=1, source_target_pairs={{0,7},{1,6},{2,5},{3,4},{4,3},{5,2},{6,1},{7,0},{8,15},{9,14},{10,... | collective-permute-start | bytes 221192 | tf_op jit(solution)/shard_map/ppermute | solution.py:164
  11.8 5.8 %collective-permute-start.5 = (bf16[1,288,128]{2,1,0:T(8,128)(2,1)S(1)}, bf16[1,288,128]{2,1,0:T(8,128)(2,1)S(1)}, u32[]{:S(2)}, u32[]{:S(2)}) collective-permute-start(bf16[1,288,128]{2,1,0:T(8,128)(2,1)S(1)} %collective-permute-done.refs_1_), channel_id=1, source_target_pairs={{0,3},{1,2},{2,1},{3,0},{4,7},{5,6},{6,5},{7,4},{8,11},{9,10},{10,... | collective-permute-start | bytes 221192 | tf_op jit(solution)/shard_map/ppermute | solution.py:164
  13.0 5.4 %collective-permute-start.6 = (bf16[2,288,128]{2,1,0:T(8,128)(2,1)S(1)}, bf16[2,288,128]{2,1,0:T(8,128)(2,1)S(1)}, u32[]{:S(2)}, u32[]{:S(2)}) collective-permute-start(bf16[2,288,128]{2,1,0:T(8,128)(2,1)S(1)} %pad_maximum_fusion.1), channel_id=1, source_target_pairs={{0,1},{1,0},{2,3},{3,2},{4,5},{5,4},{6,7},{7,6},{8,9},{9,8},{10,11... | collective-permute-start | bytes 442376 | tf_op jit(solution)/shard_map/ppermute | solution.py:164
  13.2 4.7 %collective-permute-start.9 = (bf16[1,288,128]{2,1,0:T(8,128)(2,1)S(1)}, bf16[1,288,128]{2,1,0:T(8,128)(2,1)S(1)}, u32[]{:S(2)}, u32[]{:S(2)}) collective-permute-start(bf16[1,288,128]{2,1,0:T(8,128)(2,1)S(1)} %collective-permute-done.refs_1_), channel_id=1, source_target_pairs={{0,5},{1,4},{2,7},{3,6},{4,1},{5,0},{6,3},{7,2},{8,13},{9,12},{10,... | collective-permute-start | bytes 221192 | tf_op jit(solution)/shard_map/ppermute | solution.py:164
  17.7 2.2 %collective-permute-start.7 = (bf16[2,288,128]{2,1,0:T(8,128)(2,1)S(1)}, bf16[2,288,128]{2,1,0:T(8,128)(2,1)S(1)}, u32[]{:S(2)}, u32[]{:S(2)}) collective-permute-start(bf16[2,288,128]{2,1,0:T(8,128)(2,1)S(1)} %pad_maximum_fusion.2), channel_id=1, source_target_pairs={{0,1},{1,0},{2,3},{3,2},{4,5},{5,4},{6,7},{7,6},{8,9},{9,8},{10,11... | collective-permute-start | bytes 442376 | tf_op jit(solution)/shard_map/ppermute | solution.py:164
  17.9 3.2 %collective-permute-start.10 = (bf16[4,288,128]{2,1,0:T(8,128)(2,1)S(1)}, bf16[4,288,128]{2,1,0:T(8,128)(2,1)S(1)}, u32[]{:S(2)}, u32[]{:S(2)}) collective-permute-start(bf16[4,288,128]{2,1,0:T(8,128)(2,1)S(1)} %pad_maximum_fusion), channel_id=1, source_target_pairs={{0,1},{1,0},{2,3},{3,2},{4,5},{5,4},{6,7},{7,6},{8,9},{9,8},{10,11... | collective-permute-start | bytes 884744 | tf_op jit(solution)/shard_map/ppermute | solution.py:164
  20.7 3.2 %collective-permute-start.8 = (f32[8,1,384]{2,1,0:T(1,128)S(1)}, f32[8,1,384]{2,1,0:T(1,128)S(1)}, u32[]{:S(2)}, u32[]{:S(2)}) collective-permute-start(f32[8,1,384]{2,1,0:T(1,128)S(1)} %constant_dynamic-update-slice_fusion), channel_id=1, source_target_pairs={{0,3},{1,2},{2,1},{3,0},{4,7},{5,6},{6,5},{7,4},{8,11},{9,10},{10,... | collective-permute-start | bytes 36872 | tf_op jit(solution)/shard_map/ppermute | solution.py:164
  23.9 3.1 %collective-permute-start.11 = (f32[4,1,384]{2,1,0:T(1,128)S(1)}, f32[4,1,384]{2,1,0:T(1,128)S(1)}, u32[]{:S(2)}, u32[]{:S(2)}) collective-permute-start(f32[4,1,384]{2,1,0:T(1,128)S(1)} %pad_maximum_fusion.3), channel_id=1, source_target_pairs={{0,5},{1,4},{2,7},{3,6},{4,1},{5,0},{6,3},{7,2},{8,13},{9,12},{10,... | collective-permute-start | bytes 18440 | tf_op jit(solution)/shard_map/ppermute | solution.py:164
  27.1 4.0 %collective-permute-start.12 = (f32[2,1,384]{2,1,0:T(1,128)S(1)}, f32[2,1,384]{2,1,0:T(1,128)S(1)}, u32[]{:S(2)}, u32[]{:S(2)}) collective-permute-start(f32[2,1,384]{2,1,0:T(1,128)S(1)} %pad_maximum_fusion.4), channel_id=1, source_target_pairs={{0,9},{1,8},{2,11},{3,10},{4,13},{5,12},{6,15},{7,14},{8,1},{9,0},... | collective-permute-start | bytes 9224 | tf_op jit(solution)/shard_map/ppermute | solution.py:164
  31.1 1.2 %collective-permute-start.13 = (f32[1,1,384]{2,1,0:T(1,128)S(1)}, f32[1,1,384]{2,1,0:T(1,128)S(1)}, u32[]{:S(2)}, u32[]{:S(2)}) collective-permute-start(f32[1,1,384]{2,1,0:T(1,128)S(1)} %get-tuple-element.38), channel_id=1, source_target_pairs={{0,1},{1,0},{2,3},{3,2},{4,5},{5,4},{6,7},{7,6},{8,9},{9,8},{10,11... | collective-permute-start | bytes 4616 | tf_op jit(solution)/shard_map/ppermute | solution.py:164

commit v4 on v3

v4 whole, which is shorter than its diff:
```python
import functools
import math

import jax
import jax.numpy as jnp
from jax import lax
from jax.experimental import pallas as pl
from jax.experimental.pallas import tpu as pltpu
from jax.sharding import PartitionSpec as P

LOW = -1e30
LANES = 128
MIB = 1024 * 1024
NT = (((1,), (1,)), ((), ()))


def pack_kernel(slots, q_ref, owner_ref, row_ref, out_ref, owner_held, row_held, sems):
    q_dev, cand = owner_ref.shape
    tokens = q_ref.shape[0]
    owners = out_ref.shape[0] - tokens
    copies = [
        pltpu.make_async_copy(source, target, sems.at[n])
        for n, (source, target) in enumerate(
            ((owner_ref, owner_held), (row_ref, row_held), (q_ref, out_ref.at[pl.ds(0, tokens)])))
    ]
    for copy in copies:
        copy.start()
    lane = lax.broadcasted_iota(jnp.int32, (q_dev, LANES), 1)
    own_q = lax.broadcasted_iota(jnp.int32, (q_dev, LANES), 0) == lane // cand
    spread = (
        lax.broadcasted_iota(jnp.int32, (cand, LANES), 0)
        == lax.broadcasted_iota(jnp.int32, (cand, LANES), 1) % cand
    ).astype(jnp.float32)
    earlier = (
        lax.broadcasted_iota(jnp.int32, (LANES, LANES), 0)
        < lax.broadcasted_iota(jnp.int32, (LANES, LANES), 1)
    ).astype(jnp.float32)
    number = lax.broadcasted_iota(jnp.int32, (1, LANES), 1).astype(jnp.float32) + 1.0
    each = lax.broadcasted_iota(jnp.int32, (owners, LANES), 0).astype(jnp.float32)
    place = lax.broadcasted_iota(jnp.int32, (LANES, LANES), 0).astype(jnp.float32)
    copies[0].wait()
    copies[1].wait()
    both = jnp.concatenate([owner_held[...], row_held[...]], axis=0).astype(jnp.float32)
    wide = jnp.dot(both, spread, preferred_element_type=jnp.float32)
    owner = jnp.sum(jnp.where(own_q, wide[:q_dev], 0.0), axis=0, keepdims=True)
    row = jnp.sum(jnp.where(own_q, wide[q_dev:], 0.0), axis=0, keepdims=True)
    hit = each == owner
    rank = jnp.dot(hit.astype(jnp.float32), earlier, preferred_element_type=jnp.float32)
    rank = jnp.sum(jnp.where(hit, rank, 0.0), axis=0, keepdims=True)
    rows = lax.dot_general(jnp.where(hit, row, 0.0), (place == rank).astype(jnp.float32), NT,
                           preferred_element_type=jnp.float32)
    numbers = lax.dot_general(jnp.where(hit, number, 0.0), (place == rank + slots).astype(jnp.float32), NT,
                              preferred_element_type=jnp.float32)
    out_ref[tokens:] = (rows + numbers).astype(out_ref.dtype)
    copies[2].wait()


def score_kernel(slots, qt, cand, jobs, outs, *refs):
    parts = len(jobs)
    all_refs, (cent_ref, held, len_ref) = refs[:parts], refs[parts:parts + 3]
    out_refs = refs[parts + 3:]
    out_refs = out_refs[len(out_refs) - outs:]
    height = all_refs[0].shape[1]
    tokens = out_refs[0].shape[2] - LANES
    owners = height - tokens
    ptok = held.shape[1]
    me = lax.axis_index("shard")
    mine = lax.broadcasted_iota(jnp.int32, (owners, LANES), 0) == me
    lens = jnp.broadcast_to(len_ref[...], (8, LANES))
    place = lax.broadcasted_iota(jnp.int32, (ptok, qt), 0)
    lane = lax.broadcasted_iota(jnp.int32, (1, LANES), 1) + 1

    def group(blocks):
        lines = []
        for ref, r, _, _ in blocks:
            table = ref[r, tokens:, :].astype(jnp.float32)
            lines.append(jnp.sum(jnp.where(mine, table, 0.0), axis=0, keepdims=True))
        lines.extend([jnp.zeros((1, LANES), jnp.float32)] * (8 - len(blocks)))
        lines = jnp.concatenate(lines, axis=0)
        row = lines.astype(jnp.int32)
        length = jnp.take_along_axis(lens, row, axis=1)
        number = pltpu.roll(lines, LANES - slots, 1)
        query = jnp.maximum(jnp.floor((number - 0.5) * (1.0 / cand)), 0.0).astype(jnp.int32)
        codes = row + (query << 8) + (number.astype(jnp.int32) << 16) + ((length - 1) << 24)
        for ref, r, out, at in blocks:
            scores = lax.dot_general(cent_ref[...], ref[r, :tokens, :], NT, preferred_element_type=jnp.float32)
            top = jnp.max(scores.reshape(-1, 8, tokens), axis=0)
            out[at, :, :tokens] = jnp.max(top, axis=0, keepdims=True)
        for n, (ref, r, out, at) in enumerate(blocks):
            total = jnp.full((1, LANES), LOW, jnp.float32)
            for slot in range(slots):
                code = codes[n, slot]
                first = pl.multiple_of(((code >> 8) & 255) * qt, qt)
                sim = lax.dot_general(held[code & 255], ref[r, pl.ds(first, qt), :], NT,
                                      preferred_element_type=jnp.float32)
                sim = jnp.where(place <= (code >> 24), sim, LOW)
                top = jnp.max(jnp.max(sim.reshape(-1, 8, qt), axis=0), axis=0, keepdims=True)
                score = jnp.sum(top, axis=1, keepdims=True) * (1.0 / qt)
                total = jnp.where(lane == ((code >> 16) & 255), score, total)
            out[at, :, tokens:] = total

    pieces = []
    for ref, job in zip(all_refs, jobs):
        count = ref.shape[0] // len(job)
        pieces.extend((ref, n * count, out_refs[which], at, count) for n, (which, at) in enumerate(job))
    blocks = [(ref, r + n, out, at + n) for ref, r, out, at, count in pieces for n in range(count)]
    if len(blocks) <= 8:
        group(blocks)
        return
    for ref, r, out, at, count in pieces:
        size = math.gcd(count, 8)

        def some(g, _, ref=ref, r=r, out=out, at=at, size=size):
            group([(ref, r + g * size + n, out, at + g * size + n) for n in range(size)])
            return _

        lax.fori_loop(0, count // size, some, 0)


def last_kernel(a_ref, b_ref, best_ref, sim_ref, best, sim, sems):
    q_dev, qt = best.shape
    cand = sim.shape[1]
    both = jnp.maximum(a_ref[0], b_ref[0])
    for q in range(q_dev):
        best[q:q + 1, :] = both[:, q * qt:(q + 1) * qt]
    copies = [pltpu.make_async_copy(best, best_ref, sems.at[0]), pltpu.make_async_copy(sim, sim_ref, sems.at[1])]
    copies[0].start()
    for q in range(q_dev):
        at = q_dev * qt + q * cand
        sim[q:q + 1, :] = both[:, at:at + cand]
    copies[1].start()
    for copy in copies:
        copy.wait()


def body(queries, centroids, passages, lengths, cand_owner, cand_row):
    q_dev, qt, dim = queries.shape
    cand = cand_row.shape[1]
    shards = lax.axis_size("shard")
    slots = 2 * q_dev * cand // shards
    tokens = q_dev * qt
    vmem = pl.BlockSpec(memory_space=pltpu.VMEM)
    hbm = pl.BlockSpec(memory_space=pltpu.HBM)
    owners = -(-shards // 16) * 16
    height = tokens + owners

    def stay(x):
        return pltpu.with_memory_space_constraint(x, pltpu.HBM)

    block = pl.pallas_call(
        functools.partial(pack_kernel, slots),
        out_shape=pltpu.VMEM((height, dim), queries.dtype),
        in_specs=[hbm] * 3,
        out_specs=vmem,
        scratch_shapes=[
            pltpu.VMEM((q_dev, cand), jnp.int32),
            pltpu.VMEM((q_dev, cand), jnp.int32),
            pltpu.SemaphoreType.DMA((3,)),
        ],
        compiler_params=pltpu.CompilerParams(vmem_limit_bytes=2 * MIB),
        cost_estimate=pl.CostEstimate(flops=int(1e10), bytes_accessed=1000, transcendentals=0),
        name="pack",
    )(stay(queries.reshape(tokens, dim)), stay(cand_owner.reshape(q_dev, cand)), stay(cand_row))

    index = tuple(pltpu.with_memory_space_constraint(x, pltpu.VMEM) for x in (centroids, passages, lengths))

    def swap(x, k):
        return lax.ppermute(x, "shard", [(i, i ^ k) for i in range(shards)])

    def score(blocks, jobs, *held):
        total = sum(b.shape[0] for b in blocks)
        wide = pltpu.VMEM((shards // 2, 1, tokens + q_dev * cand), jnp.float32)
        outs = len(held) or 2
        return pl.pallas_call(
            functools.partial(score_kernel, slots, qt, cand, jobs, outs),
            out_shape=[wide] * outs,
            in_specs=[vmem] * (len(blocks) + 3 + len(held)),
            out_specs=[vmem] * outs,
            input_output_aliases={len(blocks) + 3 + n: n for n in range(len(held))},
            compiler_params=pltpu.CompilerParams(vmem_limit_bytes=4 * MIB),
            cost_estimate=pl.CostEstimate(
                flops=4 * total * (tokens * centroids.size + slots * qt * (passages.size // passages.shape[0])),
                bytes_accessed=total * MIB, transcendentals=0),
            name="score",
        )(*blocks, *index, *held)

    far = []
    k = shards // 2
    while k > 2:
        far.append(k | 1)
        k //= 2
    first = block[None]
    for k in far[:-2]:
        first = jnp.concatenate([first, swap(first, k)], axis=0)
    f, g = far[-2:]
    d = g ^ 3 ^ 1
    piece = {0: first}
    for k in (f, 3, g, d):
        piece[k] = swap(first, k)
    for k in (d, 3, g):
        piece[f ^ k] = swap(piece[f], k)
    m = first.shape[0]

    def across(keys):
        return swap(jnp.concatenate([piece[k] for k in keys], axis=0), 1)

    column = (0, 1, f, f ^ 1, g, g ^ 1, f ^ g, f ^ g ^ 1)
    place = {k: (0, n * m) for n, k in enumerate(column)}
    place.update({k ^ 3: (1, n * m) for n, k in enumerate(column)})

    def jobs(*keys):
        return tuple(tuple(place[k] for k in (key if isinstance(key, tuple) else (key,))) for key in keys)

    def only(first, *keys):
        return tuple(tuple((0, at) for _, at in job) for job in jobs(first, *keys))

    xa, xb = (3, d), (f ^ d, f ^ 3)
    early = (0, f, g, 3, d)
    near, beyond = score([piece[k] for k in early], jobs(*early))
    beyond, piece[xb[0]], piece[xb[1]] = lax.optimization_barrier((beyond, piece[xb[0]], piece[xb[1]]))
    ca, cb = across(xa), across(xb)
    [beyond] = score([ca[:m], *(piece[k] for k in xb)], only(xa[0] ^ 1, *xb), beyond)
    beyond, cb = lax.optimization_barrier((beyond, cb))
    [beyond] = score([ca[m:], cb], only(xa[1] ^ 1, tuple(k ^ 1 for k in xb)), beyond)

    got = swap(beyond, 3)
    own = (0, f, g, f ^ g)
    cc = across(own)
    [near] = score([piece[f ^ g], cc], only(f ^ g, tuple(k ^ 1 for k in own)), near)
    near = jnp.maximum(near, got)
    for k in (g, f):
        half = near.shape[0] // 2
        near = jnp.maximum(near[:half], swap(near[half:], k))
    near = near.reshape(2, m, *near.shape[1:])
    for k in far[:-2][::-1]:
        half = near.shape[1] // 2
        near = jnp.maximum(near[:, :half], swap(near[:, half:], k))
    mine, got = near[0], swap(near[1], 1)
    return pl.pallas_call(
        last_kernel,
        out_shape=(jax.ShapeDtypeStruct((q_dev, qt), jnp.float32), jax.ShapeDtypeStruct((q_dev, cand), jnp.float32)),
        in_specs=[vmem] * 2,
        out_specs=(hbm, hbm),
        scratch_shapes=[
            pltpu.VMEM((q_dev, qt), jnp.float32),
            pltpu.VMEM((q_dev, cand), jnp.float32),
            pltpu.SemaphoreType.DMA((2,)),
        ],
        compiler_params=pltpu.CompilerParams(vmem_limit_bytes=MIB),
        name="last",
    )(mine, got)


def solution(mesh):
    both = ("groups", "shard")
    placed = (P(both, None, None), P(both, None), P(both, None, None), P(both, None), P(both, None, None), P(both, None))
    return jax.shard_map(body, mesh=mesh, in_specs=placed, out_specs=(P(both, None), P(both, None)), check_vma=False)
```

time: 33.1 us -> 32.4 us (0.979)
  waiting for transfers between devices: 8.39 us -> 7.36 us
  starting transfers between devices: 16.1 us -> 16.7 us
    ppermute x14, waiting for transfers between devices: 8.39 us -> 7.36 us  [swap(): return lax.ppermute(x, 'shard', [(i, i ^ k) for i in range(shards)])]
    ppermute x14, starting transfers between devices: 16.1 us -> 16.7 us  [swap(): return lax.ppermute(x, 'shard', [(i, i ^ k) for i in range(shards)])]
where the time goes in v4:
time: 32.4 us; the launch traced here: 32.3 us
  starting transfers between devices  16.7 us (52%)
  waiting for transfers between devices  7.36 us (23%)
  Pallas kernels  7.31 us (23%)
  between operations  0.73 us (2%)
    ppermute x14, starting transfers between devices, swap(): return lax.ppermute(x, 'shard', [(i, i ^ k) for i in range(shards)])  16.7 us
    ppermute x14, waiting for transfers between devices, swap(): return lax.ppermute(x, 'shard', [(i, i ^ k) for i in range(shards)])  7.36 us
    pallas_call x4, Pallas kernels, score(): pl.pallas_call(functools.partial(score_kernel, slots, qt, cand, jobs, out...  5.34 us
    pallas_call x1, Pallas kernels, body(): pl.pallas_call(functools.partial(pack_kernel, slots), out_shape=pltpu.VME...  1.28 us
    pallas_call x1, Pallas kernels, body(): pl.pallas_call(last_kernel, out_shape=(jax.ShapeDtypeStruct((q_dev, qt),...  0.69 us
  transfers between devices with their start and end apart: 14, of which 6 were waited for; matrix products, arithmetic and copies ran while one was open for 0% of the time, Pallas kernels for 17%

profile of v4, /device:TPU:0, one launch (start us, length us, event | category | flops | bytes accessed | tf_op | source)
XLA Modules:
  0.0 32.3 jit_solution(1515928035220720054)
XLA Ops:
  0.7 1.3 %pack.1 = bf16[272,128]{1,0:T(8,128)(2,1)S(1)} custom-call(bf16[256,128]{1,0:T(8,128)(2,1)} %bitcast.9, s32[8,16]{1,0:T(8,128)} %bitcast.10, s32[8,16]{1,0:T(8,128)} %row_ref.1), custom_call_target="tpu_custom_call" | custom-call | flops 10000000000 | bytes 1000 | tf_op jit(solution)/shard_map/pack/pallas_call | solution.py:150
  1.9 3.5 %collective-permute-start = (bf16[1,272,128]{2,1,0:T(8,128)(2,1)S(1)}, bf16[1,272,128]{2,1,0:T(8,128)(2,1)S(1)}, u32[]{:S(2)}, u32[]{:S(2)}) collective-permute-start(bf16[1,272,128]{2,1,0:T(8,128)(2,1)S(1)} %bitcast.3), channel_id=1, source_target_pairs={{0,9},{1,8},{2,11},{3,10},{4,13},{5,12},{6,15},{7,14},{8,1},{9,0},... | collective-permute-start | bytes 208904 | tf_op jit(solution)/shard_map/ppermute | solution.py:168
  5.5 1.8 %collective-permute-start.4 = (bf16[1,272,128]{2,1,0:T(8,128)(2,1)S(1)}, bf16[1,272,128]{2,1,0:T(8,128)(2,1)S(1)}, u32[]{:S(2)}, u32[]{:S(2)}) collective-permute-start(bf16[1,272,128]{2,1,0:T(8,128)(2,1)S(1)} %bitcast.4), channel_id=1, source_target_pairs={{0,3},{1,2},{2,1},{3,0},{4,7},{5,6},{6,5},{7,4},{8,11},{9,10},{10,... | collective-permute-start | bytes 208904 | tf_op jit(solution)/shard_map/ppermute | solution.py:168
  7.3 1.0 %collective-permute-start.5 = (bf16[1,272,128]{2,1,0:T(8,128)(2,1)S(1)}, bf16[1,272,128]{2,1,0:T(8,128)(2,1)S(1)}, u32[]{:S(2)}, u32[]{:S(2)}) collective-permute-start(bf16[1,272,128]{2,1,0:T(8,128)(2,1)S(1)} %bitcast.5), channel_id=1, source_target_pairs={{0,7},{1,6},{2,5},{3,4},{4,3},{5,2},{6,1},{7,0},{8,15},{9,14},{10,... | collective-permute-start | bytes 208904 | tf_op jit(solution)/shard_map/ppermute | solution.py:168
  8.3 0.7 %collective-permute-start.2 = (bf16[1,272,128]{2,1,0:T(8,128)(2,1)S(1)}, bf16[1,272,128]{2,1,0:T(8,128)(2,1)S(1)}, u32[]{:S(2)}, u32[]{:S(2)}) collective-permute-start(bf16[1,272,128]{2,1,0:T(8,128)(2,1)S(1)} %bitcast.6), channel_id=1, source_target_pairs={{0,5},{1,4},{2,7},{3,6},{4,1},{5,0},{6,3},{7,2},{8,13},{9,12},{10,... | collective-permute-start | bytes 208904 | tf_op jit(solution)/shard_map/ppermute | solution.py:168
  9.0 2.7 %collective-permute-start.7 = (bf16[1,272,128]{2,1,0:T(8,128)(2,1)S(1)}, bf16[1,272,128]{2,1,0:T(8,128)(2,1)S(1)}, u32[]{:S(2)}, u32[]{:S(2)}) collective-permute-start(bf16[1,272,128]{2,1,0:T(8,128)(2,1)S(1)} %collective-permute-done.refs_1_), channel_id=1, source_target_pairs={{0,7},{1,6},{2,5},{3,4},{4,3},{5,2},{6,1},{7,0},{8,15},{9,14},{10,... | collective-permute-start | bytes 208904 | tf_op jit(solution)/shard_map/ppermute | solution.py:168
  11.7 0.5 %collective-permute-start.8 = (bf16[1,272,128]{2,1,0:T(8,128)(2,1)S(1)}, bf16[1,272,128]{2,1,0:T(8,128)(2,1)S(1)}, u32[]{:S(2)}, u32[]{:S(2)}) collective-permute-start(bf16[1,272,128]{2,1,0:T(8,128)(2,1)S(1)} %collective-permute-done.refs_1_), channel_id=1, source_target_pairs={{0,3},{1,2},{2,1},{3,0},{4,7},{5,6},{6,5},{7,4},{8,11},{9,10},{10,... | collective-permute-start | bytes 208904 | tf_op jit(solution)/shard_map/ppermute | solution.py:168
  12.2 0.5 %collective-permute-done.5.refs_4_ = bf16[1,272,128]{2,1,0:T(8,128)(2,1)S(1)} collective-permute-done((bf16[1,272,128]{2,1,0:T(8,128)(2,1)S(1)}, bf16[1,272,128]{2,1,0:T(8,128)(2,1)S(1)}, u32[]{:S(2)}, u32[]{:S(2)}) %collective-permute-start.5) | collective-permute-done | bytes 69664 | tf_op jit(solution)/shard_map/ppermute | solution.py:168
  12.9 1.5 %collective-permute-start.1 = (bf16[1,272,128]{2,1,0:T(8,128)(2,1)S(1)}, bf16[1,272,128]{2,1,0:T(8,128)(2,1)S(1)}, u32[]{:S(2)}, u32[]{:S(2)}) collective-permute-start(bf16[1,272,128]{2,1,0:T(8,128)(2,1)S(1)} %collective-permute-done.refs_1_), channel_id=1, source_target_pairs={{0,5},{1,4},{2,7},{3,6},{4,1},{5,0},{6,3},{7,2},{8,13},{9,12},{10,... | collective-permute-start | bytes 208904 | tf_op jit(solution)/shard_map/ppermute | solution.py:168
  14.4 1.6 %score.4 = (f32[8,1,384]{2,1,0:T(1,128)S(1)}, f32[8,1,384]{2,1,0:T(1,128)S(1)}) custom-call(bf16[1,272,128]{2,1,0:T(8,128)(2,1)S(1)} %bitcast.7, bf16[1,272,128]{2,1,0:T(8,128)(2,1)S(1)} %collective-permute-done.refs_1_, bf16[1,272,128]{2,1,0:T(8,128)(2,1)S(1)} %collective-permute-done.2.refs_2_, bf16[1,272,128]{2,1,0:T(8,128)(2,1)S(1)} %collective-permute-done.4.refs_3_, ...), custom_call_target="tpu_custom_call" | custom-call | flops 503316480 | bytes 5242880 | tf_op jit(solution)/shard_map/score/pallas_call | solution.py:174
  16.0 1.1 %collective-permute-done.8.refs_2_ = bf16[1,272,128]{2,1,0:T(8,128)(2,1)S(1)} collective-permute-done((bf16[1,272,128]{2,1,0:T(8,128)(2,1)S(1)}, bf16[1,272,128]{2,1,0:T(8,128)(2,1)S(1)}, u32[]{:S(2)}, u32[]{:S(2)}) %collective-permute-start.8) | collective-permute-done | bytes 69664 | tf_op jit(solution)/shard_map/ppermute | solution.py:168
  17.4 0.5 %collective-permute-start.3 = (bf16[4,272,128]{2,1,0:T(8,128)(2,1)S(1)}, bf16[4,272,128]{2,1,0:T(8,128)(2,1)S(1)}, u32[]{:S(2)}, u32[]{:S(2)}) collective-permute-start(bf16[4,272,128]{2,1,0:T(8,128)(2,1)S(1)} %pad_maximum_fusion), channel_id=1, source_target_pairs={{0,1},{1,0},{2,3},{3,2},{4,5},{5,4},{6,7},{7,6},{8,9},{9,8},{10,11... | collective-permute-start | bytes 835592 | tf_op jit(solution)/shard_map/ppermute | solution.py:168
  17.9 1.1 %score.6.refs_5_ = f32[8,1,384]{2,1,0:T(1,128)S(1)} custom-call(bf16[1,272,128]{2,1,0:T(8,128)(2,1)S(1)} %get-tuple-element.16.refs_0_, bf16[1,272,128]{2,1,0:T(8,128)(2,1)S(1)} %collective-permute-done.7.refs_1_, bf16[1,272,128]{2,1,0:T(8,128)(2,1)S(1)} %collective-permute-done.8.refs_2_, ...), custom_call_target="tpu_custom_call", output_to_operand_aliasing={{}: (6, {})} | custom-call | flops 301989888 | bytes 3145728 | tf_op jit(solution)/shard_map/score/pallas_call | solution.py:174
  19.0 1.1 %score.7 = f32[8,1,384]{2,1,0:T(1,128)S(1)} custom-call(bf16[1,272,128]{2,1,0:T(8,128)(2,1)S(1)} %get-tuple-element.17.refs_0_, bf16[2,272,128]{2,1,0:T(8,128)(2,1)S(1)} %collective-permute-done.9.refs_1_, bf16[512,128]{1,0:T(8,128)(2,1)S(1)} %copy-done.1, bf16[128,128,128]{2,1,0:T(8,128)(2,1)S(1)} %copy-done, ...), custom_call_target="tpu_custom_call", output_to_operand_aliasing={{}: (5, {})} | custom-call | flops 301989888 | bytes 3145728 | tf_op jit(solution)/shard_map/score/pallas_call | solution.py:174
  20.0 0.6 %collective-permute-start.10 = (f32[8,1,384]{2,1,0:T(1,128)S(1)}, f32[8,1,384]{2,1,0:T(1,128)S(1)}, u32[]{:S(2)}, u32[]{:S(2)}) collective-permute-start(f32[8,1,384]{2,1,0:T(1,128)S(1)} %score.7), channel_id=1, source_target_pairs={{0,3},{1,2},{2,1},{3,0},{4,7},{5,6},{6,5},{7,4},{8,11},{9,10},{10,... | collective-permute-start | bytes 36872 | tf_op jit(solution)/shard_map/ppermute | solution.py:168
  20.6 1.6 %score.5 = f32[8,1,384]{2,1,0:T(1,128)S(1)} custom-call(bf16[1,272,128]{2,1,0:T(8,128)(2,1)S(1)} %collective-permute-done.1.refs_0_, bf16[4,272,128]{2,1,0:T(8,128)(2,1)S(1)} %collective-permute-done.3.refs_1_, bf16[512,128]{1,0:T(8,128)(2,1)S(1)} %copy-done.1, bf16[128,128,128]{2,1,0:T(8,128)(2,1)S(1)} %copy-done, ...), custom_call_target="tpu_custom_call", output_to_operand_aliasing={{}: (5, {})} | custom-call | flops 503316480 | bytes 5242880 | tf_op jit(solution)/shard_map/score/pallas_call | solution.py:174
  22.2 1.0 %collective-permute-done.10 = f32[8,1,384]{2,1,0:T(1,128)S(1)} collective-permute-done((f32[8,1,384]{2,1,0:T(1,128)S(1)}, f32[8,1,384]{2,1,0:T(1,128)S(1)}, u32[]{:S(2)}, u32[]{:S(2)}) %collective-permute-start.10) | collective-permute-done | bytes 12320 | tf_op jit(solution)/shard_map/ppermute | solution.py:168
  23.2 1.3 %collective-permute-start.11 = (f32[4,1,384]{2,1,0:T(1,128)S(1)}, f32[4,1,384]{2,1,0:T(1,128)S(1)}, u32[]{:S(2)}, u32[]{:S(2)}) collective-permute-start(f32[4,1,384]{2,1,0:T(1,128)S(1)} %slice.37), channel_id=1, source_target_pairs={{0,5},{1,4},{2,7},{3,6},{4,1},{5,0},{6,3},{7,2},{8,13},{9,12},{10,... | collective-permute-start | bytes 18440 | tf_op jit(solution)/shard_map/ppermute | solution.py:168
  24.5 1.9 %collective-permute-done.11 = f32[4,1,384]{2,1,0:T(1,128)S(1)} collective-permute-done((f32[4,1,384]{2,1,0:T(1,128)S(1)}, f32[4,1,384]{2,1,0:T(1,128)S(1)}, u32[]{:S(2)}, u32[]{:S(2)}) %collective-permute-start.11) | collective-permute-done | bytes 6176 | tf_op jit(solution)/shard_map/ppermute | solution.py:168
  26.4 2.2 %collective-permute-start.12 = (f32[2,1,384]{2,1,0:T(1,128)S(1)}, f32[2,1,384]{2,1,0:T(1,128)S(1)}, u32[]{:S(2)}, u32[]{:S(2)}) collective-permute-start(f32[2,1,384]{2,1,0:T(1,128)S(1)} %slice.39), channel_id=1, source_target_pairs={{0,9},{1,8},{2,11},{3,10},{4,13},{5,12},{6,15},{7,14},{8,1},{9,0},... | collective-permute-start | bytes 9224 | tf_op jit(solution)/shard_map/ppermute | solution.py:168
  28.5 1.8 %collective-permute-done.12 = f32[2,1,384]{2,1,0:T(1,128)S(1)} collective-permute-done((f32[2,1,384]{2,1,0:T(1,128)S(1)}, f32[2,1,384]{2,1,0:T(1,128)S(1)}, u32[]{:S(2)}, u32[]{:S(2)}) %collective-permute-start.12) | collective-permute-done | bytes 3104 | tf_op jit(solution)/shard_map/ppermute | solution.py:168
  30.4 0.2 collective-permute-start.13
  30.5 1.0 %collective-permute-done.13.b_ref = f32[1,1,384]{2,1,0:T(1,128)S(1)} collective-permute-done((f32[1,1,384]{2,1,0:T(1,128)S(1)}, f32[1,1,384]{2,1,0:T(1,128)S(1)}, u32[]{:S(2)}, u32[]{:S(2)}) %collective-permute-start.13) | collective-permute-done | bytes 1568 | tf_op jit(solution)/shard_map/ppermute | solution.py:168
  31.6 0.7 %last.1 = (f32[8,32]{1,0:T(8,128)}, f32[8,16]{1,0:T(8,128)}) custom-call(f32[1,1,384]{2,1,0:T(1,128)S(1)} %get-tuple-element.19.a_ref, f32[1,1,384]{2,1,0:T(1,128)S(1)} %collective-permute-done.13.b_ref), custom_call_target="tpu_custom_call" | custom-call | tf_op jit(solution)/shard_map/last/pallas_call | solution.py:239
  (26 shorter events, 0.5 us)
Async XLA Ops:
  0.6 13.8 %copy-start = (bf16[128,128,128]{2,1,0:T(8,128)(2,1)S(1)}, bf16[128,128,128]{2,1,0:T(8,128)(2,1)}, u32[]{:S(2)}) copy-start(bf16[128,128,128]{2,1,0:T(8,128)(2,1)} %refs_3_.5) | copy-start | bytes 12582916
  0.6 13.8 %copy-start.1 = (bf16[512,128]{1,0:T(8,128)(2,1)S(1)}, bf16[512,128]{1,0:T(8,128)(2,1)}, u32[]{:S(2)}) copy-start(bf16[512,128]{1,0:T(8,128)(2,1)} %refs_2_.3) | copy-start | bytes 393220
  0.7 13.8 %copy-start.2 = (s32[1,128]{1,0:T(1,128)S(1)}, s32[1,128]{1,0:T(1,128)}, u32[]{:S(2)}) copy-start(s32[1,128]{1,0:T(1,128)} %refs_4_.5) | copy-start | bytes 1540
  1.9 7.0 %collective-permute-start = (bf16[1,272,128]{2,1,0:T(8,128)(2,1)S(1)}, bf16[1,272,128]{2,1,0:T(8,128)(2,1)S(1)}, u32[]{:S(2)}, u32[]{:S(2)}) collective-permute-start(bf16[1,272,128]{2,1,0:T(8,128)(2,1)S(1)} %bitcast.3), channel_id=1, source_target_pairs={{0,9},{1,8},{2,11},{3,10},{4,13},{5,12},{6,15},{7,14},{8,1},{9,0},... | collective-permute-start | bytes 208904 | tf_op jit(solution)/shard_map/ppermute | solution.py:168
  5.5 6.7 %collective-permute-start.4 = (bf16[1,272,128]{2,1,0:T(8,128)(2,1)S(1)}, bf16[1,272,128]{2,1,0:T(8,128)(2,1)S(1)}, u32[]{:S(2)}, u32[]{:S(2)}) collective-permute-start(bf16[1,272,128]{2,1,0:T(8,128)(2,1)S(1)} %bitcast.4), channel_id=1, source_target_pairs={{0,3},{1,2},{2,1},{3,0},{4,7},{5,6},{6,5},{7,4},{8,11},{9,10},{10,... | collective-permute-start | bytes 208904 | tf_op jit(solution)/shard_map/ppermute | solution.py:168
  7.3 5.5 %collective-permute-start.5 = (bf16[1,272,128]{2,1,0:T(8,128)(2,1)S(1)}, bf16[1,272,128]{2,1,0:T(8,128)(2,1)S(1)}, u32[]{:S(2)}, u32[]{:S(2)}) collective-permute-start(bf16[1,272,128]{2,1,0:T(8,128)(2,1)S(1)} %bitcast.5), channel_id=1, source_target_pairs={{0,7},{1,6},{2,5},{3,4},{4,3},{5,2},{6,1},{7,0},{8,15},{9,14},{10,... | collective-permute-start | bytes 208904 | tf_op jit(solution)/shard_map/ppermute | solution.py:168
  8.3 6.1 %collective-permute-start.2 = (bf16[1,272,128]{2,1,0:T(8,128)(2,1)S(1)}, bf16[1,272,128]{2,1,0:T(8,128)(2,1)S(1)}, u32[]{:S(2)}, u32[]{:S(2)}) collective-permute-start(bf16[1,272,128]{2,1,0:T(8,128)(2,1)S(1)} %bitcast.6), channel_id=1, source_target_pairs={{0,5},{1,4},{2,7},{3,6},{4,1},{5,0},{6,3},{7,2},{8,13},{9,12},{10,... | collective-permute-start | bytes 208904 | tf_op jit(solution)/shard_map/ppermute | solution.py:168
  9.0 7.1 %collective-permute-start.7 = (bf16[1,272,128]{2,1,0:T(8,128)(2,1)S(1)}, bf16[1,272,128]{2,1,0:T(8,128)(2,1)S(1)}, u32[]{:S(2)}, u32[]{:S(2)}) collective-permute-start(bf16[1,272,128]{2,1,0:T(8,128)(2,1)S(1)} %collective-permute-done.refs_1_), channel_id=1, source_target_pairs={{0,7},{1,6},{2,5},{3,4},{4,3},{5,2},{6,1},{7,0},{8,15},{9,14},{10,... | collective-permute-start | bytes 208904 | tf_op jit(solution)/shard_map/ppermute | solution.py:168
  11.7 5.5 %collective-permute-start.8 = (bf16[1,272,128]{2,1,0:T(8,128)(2,1)S(1)}, bf16[1,272,128]{2,1,0:T(8,128)(2,1)S(1)}, u32[]{:S(2)}, u32[]{:S(2)}) collective-permute-start(bf16[1,272,128]{2,1,0:T(8,128)(2,1)S(1)} %collective-permute-done.refs_1_), channel_id=1, source_target_pairs={{0,3},{1,2},{2,1},{3,0},{4,7},{5,6},{6,5},{7,4},{8,11},{9,10},{10,... | collective-permute-start | bytes 208904 | tf_op jit(solution)/shard_map/ppermute | solution.py:168
  12.8 5.1 %collective-permute-start.6 = (bf16[2,272,128]{2,1,0:T(8,128)(2,1)S(1)}, bf16[2,272,128]{2,1,0:T(8,128)(2,1)S(1)}, u32[]{:S(2)}, u32[]{:S(2)}) collective-permute-start(bf16[2,272,128]{2,1,0:T(8,128)(2,1)S(1)} %pad_maximum_fusion.1), channel_id=1, source_target_pairs={{0,1},{1,0},{2,3},{3,2},{4,5},{5,4},{6,7},{7,6},{8,9},{9,8},{10,11... | collective-permute-start | bytes 417800 | tf_op jit(solution)/shard_map/ppermute | solution.py:168
  12.9 4.4 %collective-permute-start.1 = (bf16[1,272,128]{2,1,0:T(8,128)(2,1)S(1)}, bf16[1,272,128]{2,1,0:T(8,128)(2,1)S(1)}, u32[]{:S(2)}, u32[]{:S(2)}) collective-permute-start(bf16[1,272,128]{2,1,0:T(8,128)(2,1)S(1)} %collective-permute-done.refs_1_), channel_id=1, source_target_pairs={{0,5},{1,4},{2,7},{3,6},{4,1},{5,0},{6,3},{7,2},{8,13},{9,12},{10,... | collective-permute-start | bytes 208904 | tf_op jit(solution)/shard_map/ppermute | solution.py:168
  17.2 1.8 %collective-permute-start.9 = (bf16[2,272,128]{2,1,0:T(8,128)(2,1)S(1)}, bf16[2,272,128]{2,1,0:T(8,128)(2,1)S(1)}, u32[]{:S(2)}, u32[]{:S(2)}) collective-permute-start(bf16[2,272,128]{2,1,0:T(8,128)(2,1)S(1)} %pad_maximum_fusion.2), channel_id=1, source_target_pairs={{0,1},{1,0},{2,3},{3,2},{4,5},{5,4},{6,7},{7,6},{8,9},{9,8},{10,11... | collective-permute-start | bytes 417800 | tf_op jit(solution)/shard_map/ppermute | solution.py:168
  17.4 3.2 %collective-permute-start.3 = (bf16[4,272,128]{2,1,0:T(8,128)(2,1)S(1)}, bf16[4,272,128]{2,1,0:T(8,128)(2,1)S(1)}, u32[]{:S(2)}, u32[]{:S(2)}) collective-permute-start(bf16[4,272,128]{2,1,0:T(8,128)(2,1)S(1)} %pad_maximum_fusion), channel_id=1, source_target_pairs={{0,1},{1,0},{2,3},{3,2},{4,5},{5,4},{6,7},{7,6},{8,9},{9,8},{10,11... | collective-permute-start | bytes 835592 | tf_op jit(solution)/shard_map/ppermute | solution.py:168
  20.0 3.2 %collective-permute-start.10 = (f32[8,1,384]{2,1,0:T(1,128)S(1)}, f32[8,1,384]{2,1,0:T(1,128)S(1)}, u32[]{:S(2)}, u32[]{:S(2)}) collective-permute-start(f32[8,1,384]{2,1,0:T(1,128)S(1)} %score.7), channel_id=1, source_target_pairs={{0,3},{1,2},{2,1},{3,0},{4,7},{5,6},{6,5},{7,4},{8,11},{9,10},{10,... | collective-permute-start | bytes 36872 | tf_op jit(solution)/shard_map/ppermute | solution.py:168
  23.2 3.1 %collective-permute-start.11 = (f32[4,1,384]{2,1,0:T(1,128)S(1)}, f32[4,1,384]{2,1,0:T(1,128)S(1)}, u32[]{:S(2)}, u32[]{:S(2)}) collective-permute-start(f32[4,1,384]{2,1,0:T(1,128)S(1)} %slice.37), channel_id=1, source_target_pairs={{0,5},{1,4},{2,7},{3,6},{4,1},{5,0},{6,3},{7,2},{8,13},{9,12},{10,... | collective-permute-start | bytes 18440 | tf_op jit(solution)/shard_map/ppermute | solution.py:168
  26.4 4.0 %collective-permute-start.12 = (f32[2,1,384]{2,1,0:T(1,128)S(1)}, f32[2,1,384]{2,1,0:T(1,128)S(1)}, u32[]{:S(2)}, u32[]{:S(2)}) collective-permute-start(f32[2,1,384]{2,1,0:T(1,128)S(1)} %slice.39), channel_id=1, source_target_pairs={{0,9},{1,8},{2,11},{3,10},{4,13},{5,12},{6,15},{7,14},{8,1},{9,0},... | collective-permute-start | bytes 9224 | tf_op jit(solution)/shard_map/ppermute | solution.py:168
  30.4 1.2 %collective-permute-start.13 = (f32[1,1,384]{2,1,0:T(1,128)S(1)}, f32[1,1,384]{2,1,0:T(1,128)S(1)}, u32[]{:S(2)}, u32[]{:S(2)}) collective-permute-start(f32[1,1,384]{2,1,0:T(1,128)S(1)} %get-tuple-element.18), channel_id=1, source_target_pairs={{0,1},{1,0},{2,3},{3,2},{4,5},{5,4},{6,7},{7,6},{8,9},{9,8},{10,11... | collective-permute-start | bytes 4616 | tf_op jit(solution)/shard_map/ppermute | solution.py:168

commit v5 on v4

--- a/solution.py
+++ b/solution.py
@@ -214,13 +214,13 @@
     def only(first, *keys):
         return tuple(tuple((0, at) for _, at in job) for job in jobs(first, *keys))
 
-    xa, xb = (3, d), (f ^ d, f ^ 3)
+    xa, xb = (3, d), (f ^ 3, f ^ d)
     early = (0, f, g, 3, d)
     near, beyond = score([piece[k] for k in early], jobs(*early))
     beyond, piece[xb[0]], piece[xb[1]] = lax.optimization_barrier((beyond, piece[xb[0]], piece[xb[1]]))
     ca, cb = across(xa), across(xb)
     [beyond] = score([ca[:m], *(piece[k] for k in xb)], only(xa[0] ^ 1, *xb), beyond)
-    beyond, cb = lax.optimization_barrier((beyond, cb))
+    beyond, cb, piece[f ^ g] = lax.optimization_barrier((beyond, cb, piece[f ^ g]))
     [beyond] = score([ca[m:], cb], only(xa[1] ^ 1, tuple(k ^ 1 for k in xb)), beyond)
 
     got = swap(beyond, 3)

time: 32.4 us -> 32.1 us (level)
  starting transfers between devices: 16.7 us -> 16.3 us
    ppermute x14, starting transfers between devices: 16.7 us -> 16.3 us  [swap(): return lax.ppermute(x, 'shard', [(i, i ^ k) for i in range(shards)])]
where the time goes in v5:
time: 32.1 us; the launch traced here: 31.9 us
  starting transfers between devices  16.3 us (51%)
  waiting for transfers between devices  7.43 us (23%)
  Pallas kernels  7.31 us (23%)
  between operations  0.74 us (2%)
    ppermute x14, starting transfers between devices, swap(): return lax.ppermute(x, 'shard', [(i, i ^ k) for i in range(shards)])  16.3 us
    ppermute x14, waiting for transfers between devices, swap(): return lax.ppermute(x, 'shard', [(i, i ^ k) for i in range(shards)])  7.43 us
    pallas_call x4, Pallas kernels, score(): pl.pallas_call(functools.partial(score_kernel, slots, qt, cand, jobs, out...  5.34 us
    pallas_call x1, Pallas kernels, body(): pl.pallas_call(functools.partial(pack_kernel, slots), out_shape=pltpu.VME...  1.28 us
    pallas_call x1, Pallas kernels, body(): pl.pallas_call(last_kernel, out_shape=(jax.ShapeDtypeStruct((q_dev, qt),...  0.69 us
  transfers between devices with their start and end apart: 14, of which 6 were waited for; matrix products, arithmetic and copies ran while one was open for 0% of the time, Pallas kernels for 17%

profile of v5, /device:TPU:0, one launch (start us, length us, event | category | flops | bytes accessed | tf_op | source)
XLA Modules:
  0.0 31.9 jit_solution(16306867269029722946)
XLA Ops:
  0.7 1.3 %pack.1 = bf16[272,128]{1,0:T(8,128)(2,1)S(1)} custom-call(bf16[256,128]{1,0:T(8,128)(2,1)} %bitcast.9, s32[8,16]{1,0:T(8,128)} %bitcast.10, s32[8,16]{1,0:T(8,128)} %row_ref.1), custom_call_target="tpu_custom_call" | custom-call | flops 10000000000 | bytes 1000 | tf_op jit(solution)/shard_map/pack/pallas_call | solution.py:150
  1.9 3.5 %collective-permute-start.3 = (bf16[1,272,128]{2,1,0:T(8,128)(2,1)S(1)}, bf16[1,272,128]{2,1,0:T(8,128)(2,1)S(1)}, u32[]{:S(2)}, u32[]{:S(2)}) collective-permute-start(bf16[1,272,128]{2,1,0:T(8,128)(2,1)S(1)} %bitcast.3), channel_id=1, source_target_pairs={{0,9},{1,8},{2,11},{3,10},{4,13},{5,12},{6,15},{7,14},{8,1},{9,0},... | collective-permute-start | bytes 208904 | tf_op jit(solution)/shard_map/ppermute | solution.py:168
  5.5 1.8 %collective-permute-start = (bf16[1,272,128]{2,1,0:T(8,128)(2,1)S(1)}, bf16[1,272,128]{2,1,0:T(8,128)(2,1)S(1)}, u32[]{:S(2)}, u32[]{:S(2)}) collective-permute-start(bf16[1,272,128]{2,1,0:T(8,128)(2,1)S(1)} %bitcast.4), channel_id=1, source_target_pairs={{0,3},{1,2},{2,1},{3,0},{4,7},{5,6},{6,5},{7,4},{8,11},{9,10},{10,... | collective-permute-start | bytes 208904 | tf_op jit(solution)/shard_map/ppermute | solution.py:168
  7.3 1.0 %collective-permute-start.1 = (bf16[1,272,128]{2,1,0:T(8,128)(2,1)S(1)}, bf16[1,272,128]{2,1,0:T(8,128)(2,1)S(1)}, u32[]{:S(2)}, u32[]{:S(2)}) collective-permute-start(bf16[1,272,128]{2,1,0:T(8,128)(2,1)S(1)} %bitcast.5), channel_id=1, source_target_pairs={{0,7},{1,6},{2,5},{3,4},{4,3},{5,2},{6,1},{7,0},{8,15},{9,14},{10,... | collective-permute-start | bytes 208904 | tf_op jit(solution)/shard_map/ppermute | solution.py:168
  8.3 0.7 %collective-permute-start.4 = (bf16[1,272,128]{2,1,0:T(8,128)(2,1)S(1)}, bf16[1,272,128]{2,1,0:T(8,128)(2,1)S(1)}, u32[]{:S(2)}, u32[]{:S(2)}) collective-permute-start(bf16[1,272,128]{2,1,0:T(8,128)(2,1)S(1)} %bitcast.6), channel_id=1, source_target_pairs={{0,5},{1,4},{2,7},{3,6},{4,1},{5,0},{6,3},{7,2},{8,13},{9,12},{10,... | collective-permute-start | bytes 208904 | tf_op jit(solution)/shard_map/ppermute | solution.py:168
  9.0 2.6 %collective-permute-start.5 = (bf16[1,272,128]{2,1,0:T(8,128)(2,1)S(1)}, bf16[1,272,128]{2,1,0:T(8,128)(2,1)S(1)}, u32[]{:S(2)}, u32[]{:S(2)}) collective-permute-start(bf16[1,272,128]{2,1,0:T(8,128)(2,1)S(1)} %collective-permute-done.3.refs_1_), channel_id=1, source_target_pairs={{0,3},{1,2},{2,1},{3,0},{4,7},{5,6},{6,5},{7,4},{8,11},{9,10},{10,... | collective-permute-start | bytes 208904 | tf_op jit(solution)/shard_map/ppermute | solution.py:168
  11.5 0.7 %collective-permute-start.6 = (bf16[1,272,128]{2,1,0:T(8,128)(2,1)S(1)}, bf16[1,272,128]{2,1,0:T(8,128)(2,1)S(1)}, u32[]{:S(2)}, u32[]{:S(2)}) collective-permute-start(bf16[1,272,128]{2,1,0:T(8,128)(2,1)S(1)} %collective-permute-done.3.refs_1_), channel_id=1, source_target_pairs={{0,7},{1,6},{2,5},{3,4},{4,3},{5,2},{6,1},{7,0},{8,15},{9,14},{10,... | collective-permute-start | bytes 208904 | tf_op jit(solution)/shard_map/ppermute | solution.py:168
  12.2 0.5 %collective-permute-done.1.refs_4_ = bf16[1,272,128]{2,1,0:T(8,128)(2,1)S(1)} collective-permute-done((bf16[1,272,128]{2,1,0:T(8,128)(2,1)S(1)}, bf16[1,272,128]{2,1,0:T(8,128)(2,1)S(1)}, u32[]{:S(2)}, u32[]{:S(2)}) %collective-permute-start.1) | collective-permute-done | bytes 69664 | tf_op jit(solution)/shard_map/ppermute | solution.py:168
  12.9 1.5 %collective-permute-start.8 = (bf16[1,272,128]{2,1,0:T(8,128)(2,1)S(1)}, bf16[1,272,128]{2,1,0:T(8,128)(2,1)S(1)}, u32[]{:S(2)}, u32[]{:S(2)}) collective-permute-start(bf16[1,272,128]{2,1,0:T(8,128)(2,1)S(1)} %collective-permute-done.3.refs_1_), channel_id=1, source_target_pairs={{0,5},{1,4},{2,7},{3,6},{4,1},{5,0},{6,3},{7,2},{8,13},{9,12},{10,... | collective-permute-start | bytes 208904 | tf_op jit(solution)/shard_map/ppermute | solution.py:168
  14.5 1.6 %score.4 = (f32[8,1,384]{2,1,0:T(1,128)S(1)}, f32[8,1,384]{2,1,0:T(1,128)S(1)}) custom-call(bf16[1,272,128]{2,1,0:T(8,128)(2,1)S(1)} %bitcast.7, bf16[1,272,128]{2,1,0:T(8,128)(2,1)S(1)} %collective-permute-done.3.refs_1_, bf16[1,272,128]{2,1,0:T(8,128)(2,1)S(1)} %collective-permute-done.4.refs_2_, bf16[1,272,128]{2,1,0:T(8,128)(2,1)S(1)} %collective-permute-done.refs_3_, ...), custom_call_target="tpu_custom_call" | custom-call | flops 503316480 | bytes 5242880 | tf_op jit(solution)/shard_map/score/pallas_call | solution.py:174
  16.1 0.5 %collective-permute-done.6.refs_2_ = bf16[1,272,128]{2,1,0:T(8,128)(2,1)S(1)} collective-permute-done((bf16[1,272,128]{2,1,0:T(8,128)(2,1)S(1)}, bf16[1,272,128]{2,1,0:T(8,128)(2,1)S(1)}, u32[]{:S(2)}, u32[]{:S(2)}) %collective-permute-start.6) | collective-permute-done | bytes 69664 | tf_op jit(solution)/shard_map/ppermute | solution.py:168
  16.6 0.6 %collective-permute-start.7 = (bf16[2,272,128]{2,1,0:T(8,128)(2,1)S(1)}, bf16[2,272,128]{2,1,0:T(8,128)(2,1)S(1)}, u32[]{:S(2)}, u32[]{:S(2)}) collective-permute-start(bf16[2,272,128]{2,1,0:T(8,128)(2,1)S(1)} %pad_maximum_fusion.2), channel_id=1, source_target_pairs={{0,1},{1,0},{2,3},{3,2},{4,5},{5,4},{6,7},{7,6},{8,9},{9,8},{10,11... | collective-permute-start | bytes 417800 | tf_op jit(solution)/shard_map/ppermute | solution.py:168
  17.2 1.1 %score.5.refs_5_ = f32[8,1,384]{2,1,0:T(1,128)S(1)} custom-call(bf16[1,272,128]{2,1,0:T(8,128)(2,1)S(1)} %get-tuple-element.19.refs_0_, bf16[1,272,128]{2,1,0:T(8,128)(2,1)S(1)} %collective-permute-done.5.refs_1_, bf16[1,272,128]{2,1,0:T(8,128)(2,1)S(1)} %collective-permute-done.6.refs_2_, ...), custom_call_target="tpu_custom_call", output_to_operand_aliasing={{}: (6, {})} | custom-call | flops 301989888 | bytes 3145728 | tf_op jit(solution)/shard_map/score/pallas_call | solution.py:174
  18.3 0.3 %collective-permute-start.9 = (bf16[4,272,128]{2,1,0:T(8,128)(2,1)S(1)}, bf16[4,272,128]{2,1,0:T(8,128)(2,1)S(1)}, u32[]{:S(2)}, u32[]{:S(2)}) collective-permute-start(bf16[4,272,128]{2,1,0:T(8,128)(2,1)S(1)} %pad_maximum_fusion), channel_id=1, source_target_pairs={{0,1},{1,0},{2,3},{3,2},{4,5},{5,4},{6,7},{7,6},{8,9},{9,8},{10,11... | collective-permute-start | bytes 835592 | tf_op jit(solution)/shard_map/ppermute | solution.py:168
  18.6 1.1 %score.7 = f32[8,1,384]{2,1,0:T(1,128)S(1)} custom-call(bf16[1,272,128]{2,1,0:T(8,128)(2,1)S(1)} %get-tuple-element.18.refs_0_, bf16[2,272,128]{2,1,0:T(8,128)(2,1)S(1)} %collective-permute-done.7.refs_1_, bf16[512,128]{1,0:T(8,128)(2,1)S(1)} %copy-done.1, bf16[128,128,128]{2,1,0:T(8,128)(2,1)S(1)} %copy-done, ...), custom_call_target="tpu_custom_call", output_to_operand_aliasing={{}: (5, {})} | custom-call | flops 301989888 | bytes 3145728 | tf_op jit(solution)/shard_map/score/pallas_call | solution.py:174
  19.7 0.5 %collective-permute-start.10 = (f32[8,1,384]{2,1,0:T(1,128)S(1)}, f32[8,1,384]{2,1,0:T(1,128)S(1)}, u32[]{:S(2)}, u32[]{:S(2)}) collective-permute-start(f32[8,1,384]{2,1,0:T(1,128)S(1)} %score.7), channel_id=1, source_target_pairs={{0,3},{1,2},{2,1},{3,0},{4,7},{5,6},{6,5},{7,4},{8,11},{9,10},{10,... | collective-permute-start | bytes 36872 | tf_op jit(solution)/shard_map/ppermute | solution.py:168
  20.2 1.6 %score.6 = f32[8,1,384]{2,1,0:T(1,128)S(1)} custom-call(bf16[1,272,128]{2,1,0:T(8,128)(2,1)S(1)} %collective-permute-done.8.refs_0_, bf16[4,272,128]{2,1,0:T(8,128)(2,1)S(1)} %collective-permute-done.9.refs_1_, bf16[512,128]{1,0:T(8,128)(2,1)S(1)} %copy-done.1, bf16[128,128,128]{2,1,0:T(8,128)(2,1)S(1)} %copy-done, ...), custom_call_target="tpu_custom_call", output_to_operand_aliasing={{}: (5, {})} | custom-call | flops 503316480 | bytes 5242880 | tf_op jit(solution)/shard_map/score/pallas_call | solution.py:174
  21.8 1.1 %collective-permute-done.10 = f32[8,1,384]{2,1,0:T(1,128)S(1)} collective-permute-done((f32[8,1,384]{2,1,0:T(1,128)S(1)}, f32[8,1,384]{2,1,0:T(1,128)S(1)}, u32[]{:S(2)}, u32[]{:S(2)}) %collective-permute-start.10) | collective-permute-done | bytes 12320 | tf_op jit(solution)/shard_map/ppermute | solution.py:168
  22.9 0.3 %collective-permute-start.11 = (f32[4,1,384]{2,1,0:T(1,128)S(1)}, f32[4,1,384]{2,1,0:T(1,128)S(1)}, u32[]{:S(2)}, u32[]{:S(2)}) collective-permute-start(f32[4,1,384]{2,1,0:T(1,128)S(1)} %slice.37), channel_id=1, source_target_pairs={{0,5},{1,4},{2,7},{3,6},{4,1},{5,0},{6,3},{7,2},{8,13},{9,12},{10,... | collective-permute-start | bytes 18440 | tf_op jit(solution)/shard_map/ppermute | solution.py:168
  23.2 2.8 %collective-permute-done.11 = f32[4,1,384]{2,1,0:T(1,128)S(1)} collective-permute-done((f32[4,1,384]{2,1,0:T(1,128)S(1)}, f32[4,1,384]{2,1,0:T(1,128)S(1)}, u32[]{:S(2)}, u32[]{:S(2)}) %collective-permute-start.11) | collective-permute-done | bytes 6176 | tf_op jit(solution)/shard_map/ppermute | solution.py:168
  26.0 2.4 %collective-permute-start.12 = (f32[2,1,384]{2,1,0:T(1,128)S(1)}, f32[2,1,384]{2,1,0:T(1,128)S(1)}, u32[]{:S(2)}, u32[]{:S(2)}) collective-permute-start(f32[2,1,384]{2,1,0:T(1,128)S(1)} %slice.39), channel_id=1, source_target_pairs={{0,9},{1,8},{2,11},{3,10},{4,13},{5,12},{6,15},{7,14},{8,1},{9,0},... | collective-permute-start | bytes 9224 | tf_op jit(solution)/shard_map/ppermute | solution.py:168
  28.4 1.6 %collective-permute-done.12 = f32[2,1,384]{2,1,0:T(1,128)S(1)} collective-permute-done((f32[2,1,384]{2,1,0:T(1,128)S(1)}, f32[2,1,384]{2,1,0:T(1,128)S(1)}, u32[]{:S(2)}, u32[]{:S(2)}) %collective-permute-start.12) | collective-permute-done | bytes 3104 | tf_op jit(solution)/shard_map/ppermute | solution.py:168
  30.3 0.9 %collective-permute-done.13.b_ref = f32[1,1,384]{2,1,0:T(1,128)S(1)} collective-permute-done((f32[1,1,384]{2,1,0:T(1,128)S(1)}, f32[1,1,384]{2,1,0:T(1,128)S(1)}, u32[]{:S(2)}, u32[]{:S(2)}) %collective-permute-start.13) | collective-permute-done | bytes 1568 | tf_op jit(solution)/shard_map/ppermute | solution.py:168
  31.2 0.7 %last.1 = (f32[8,32]{1,0:T(8,128)}, f32[8,16]{1,0:T(8,128)}) custom-call(f32[1,1,384]{2,1,0:T(1,128)S(1)} %get-tuple-element.21.a_ref, f32[1,1,384]{2,1,0:T(1,128)S(1)} %collective-permute-done.13.b_ref), custom_call_target="tpu_custom_call" | custom-call | tf_op jit(solution)/shard_map/last/pallas_call | solution.py:239
  (26 shorter events, 0.6 us)
Async XLA Ops:
  0.6 13.8 %copy-start = (bf16[128,128,128]{2,1,0:T(8,128)(2,1)S(1)}, bf16[128,128,128]{2,1,0:T(8,128)(2,1)}, u32[]{:S(2)}) copy-start(bf16[128,128,128]{2,1,0:T(8,128)(2,1)} %refs_3_.5) | copy-start | bytes 12582916
  0.6 13.8 %copy-start.1 = (bf16[512,128]{1,0:T(8,128)(2,1)S(1)}, bf16[512,128]{1,0:T(8,128)(2,1)}, u32[]{:S(2)}) copy-start(bf16[512,128]{1,0:T(8,128)(2,1)} %refs_2_.3) | copy-start | bytes 393220
  0.7 13.8 %copy-start.2 = (s32[1,128]{1,0:T(1,128)S(1)}, s32[1,128]{1,0:T(1,128)}, u32[]{:S(2)}) copy-start(s32[1,128]{1,0:T(1,128)} %refs_4_.5) | copy-start | bytes 1540
  1.9 7.0 %collective-permute-start.3 = (bf16[1,272,128]{2,1,0:T(8,128)(2,1)S(1)}, bf16[1,272,128]{2,1,0:T(8,128)(2,1)S(1)}, u32[]{:S(2)}, u32[]{:S(2)}) collective-permute-start(bf16[1,272,128]{2,1,0:T(8,128)(2,1)S(1)} %bitcast.3), channel_id=1, source_target_pairs={{0,9},{1,8},{2,11},{3,10},{4,13},{5,12},{6,15},{7,14},{8,1},{9,0},... | collective-permute-start | bytes 208904 | tf_op jit(solution)/shard_map/ppermute | solution.py:168
  5.5 6.7 %collective-permute-start = (bf16[1,272,128]{2,1,0:T(8,128)(2,1)S(1)}, bf16[1,272,128]{2,1,0:T(8,128)(2,1)S(1)}, u32[]{:S(2)}, u32[]{:S(2)}) collective-permute-start(bf16[1,272,128]{2,1,0:T(8,128)(2,1)S(1)} %bitcast.4), channel_id=1, source_target_pairs={{0,3},{1,2},{2,1},{3,0},{4,7},{5,6},{6,5},{7,4},{8,11},{9,10},{10,... | collective-permute-start | bytes 208904 | tf_op jit(solution)/shard_map/ppermute | solution.py:168
  7.3 5.5 %collective-permute-start.1 = (bf16[1,272,128]{2,1,0:T(8,128)(2,1)S(1)}, bf16[1,272,128]{2,1,0:T(8,128)(2,1)S(1)}, u32[]{:S(2)}, u32[]{:S(2)}) collective-permute-start(bf16[1,272,128]{2,1,0:T(8,128)(2,1)S(1)} %bitcast.5), channel_id=1, source_target_pairs={{0,7},{1,6},{2,5},{3,4},{4,3},{5,2},{6,1},{7,0},{8,15},{9,14},{10,... | collective-permute-start | bytes 208904 | tf_op jit(solution)/shard_map/ppermute | solution.py:168
  8.3 6.2 %collective-permute-start.4 = (bf16[1,272,128]{2,1,0:T(8,128)(2,1)S(1)}, bf16[1,272,128]{2,1,0:T(8,128)(2,1)S(1)}, u32[]{:S(2)}, u32[]{:S(2)}) collective-permute-start(bf16[1,272,128]{2,1,0:T(8,128)(2,1)S(1)} %bitcast.6), channel_id=1, source_target_pairs={{0,5},{1,4},{2,7},{3,6},{4,1},{5,0},{6,3},{7,2},{8,13},{9,12},{10,... | collective-permute-start | bytes 208904 | tf_op jit(solution)/shard_map/ppermute | solution.py:168
  9.0 7.1 %collective-permute-start.5 = (bf16[1,272,128]{2,1,0:T(8,128)(2,1)S(1)}, bf16[1,272,128]{2,1,0:T(8,128)(2,1)S(1)}, u32[]{:S(2)}, u32[]{:S(2)}) collective-permute-start(bf16[1,272,128]{2,1,0:T(8,128)(2,1)S(1)} %collective-permute-done.3.refs_1_), channel_id=1, source_target_pairs={{0,3},{1,2},{2,1},{3,0},{4,7},{5,6},{6,5},{7,4},{8,11},{9,10},{10,... | collective-permute-start | bytes 208904 | tf_op jit(solution)/shard_map/ppermute | solution.py:168
  11.5 5.0 %collective-permute-start.6 = (bf16[1,272,128]{2,1,0:T(8,128)(2,1)S(1)}, bf16[1,272,128]{2,1,0:T(8,128)(2,1)S(1)}, u32[]{:S(2)}, u32[]{:S(2)}) collective-permute-start(bf16[1,272,128]{2,1,0:T(8,128)(2,1)S(1)} %collective-permute-done.3.refs_1_), channel_id=1, source_target_pairs={{0,7},{1,6},{2,5},{3,4},{4,3},{5,2},{6,1},{7,0},{8,15},{9,14},{10,... | collective-permute-start | bytes 208904 | tf_op jit(solution)/shard_map/ppermute | solution.py:168
  12.8 4.4 %collective-permute-start.2 = (bf16[2,272,128]{2,1,0:T(8,128)(2,1)S(1)}, bf16[2,272,128]{2,1,0:T(8,128)(2,1)S(1)}, u32[]{:S(2)}, u32[]{:S(2)}) collective-permute-start(bf16[2,272,128]{2,1,0:T(8,128)(2,1)S(1)} %pad_maximum_fusion.1), channel_id=1, source_target_pairs={{0,1},{1,0},{2,3},{3,2},{4,5},{5,4},{6,7},{7,6},{8,9},{9,8},{10,11... | collective-permute-start | bytes 417800 | tf_op jit(solution)/shard_map/ppermute | solution.py:168
  12.9 5.3 %collective-permute-start.8 = (bf16[1,272,128]{2,1,0:T(8,128)(2,1)S(1)}, bf16[1,272,128]{2,1,0:T(8,128)(2,1)S(1)}, u32[]{:S(2)}, u32[]{:S(2)}) collective-permute-start(bf16[1,272,128]{2,1,0:T(8,128)(2,1)S(1)} %collective-permute-done.3.refs_1_), channel_id=1, source_target_pairs={{0,5},{1,4},{2,7},{3,6},{4,1},{5,0},{6,3},{7,2},{8,13},{9,12},{10,... | collective-permute-start | bytes 208904 | tf_op jit(solution)/shard_map/ppermute | solution.py:168
  16.6 1.7 %collective-permute-start.7 = (bf16[2,272,128]{2,1,0:T(8,128)(2,1)S(1)}, bf16[2,272,128]{2,1,0:T(8,128)(2,1)S(1)}, u32[]{:S(2)}, u32[]{:S(2)}) collective-permute-start(bf16[2,272,128]{2,1,0:T(8,128)(2,1)S(1)} %pad_maximum_fusion.2), channel_id=1, source_target_pairs={{0,1},{1,0},{2,3},{3,2},{4,5},{5,4},{6,7},{7,6},{8,9},{9,8},{10,11... | collective-permute-start | bytes 417800 | tf_op jit(solution)/shard_map/ppermute | solution.py:168
  18.3 1.9 %collective-permute-start.9 = (bf16[4,272,128]{2,1,0:T(8,128)(2,1)S(1)}, bf16[4,272,128]{2,1,0:T(8,128)(2,1)S(1)}, u32[]{:S(2)}, u32[]{:S(2)}) collective-permute-start(bf16[4,272,128]{2,1,0:T(8,128)(2,1)S(1)} %pad_maximum_fusion), channel_id=1, source_target_pairs={{0,1},{1,0},{2,3},{3,2},{4,5},{5,4},{6,7},{7,6},{8,9},{9,8},{10,11... | collective-permute-start | bytes 835592 | tf_op jit(solution)/shard_map/ppermute | solution.py:168
  19.7 3.2 %collective-permute-start.10 = (f32[8,1,384]{2,1,0:T(1,128)S(1)}, f32[8,1,384]{2,1,0:T(1,128)S(1)}, u32[]{:S(2)}, u32[]{:S(2)}) collective-permute-start(f32[8,1,384]{2,1,0:T(1,128)S(1)} %score.7), channel_id=1, source_target_pairs={{0,3},{1,2},{2,1},{3,0},{4,7},{5,6},{6,5},{7,4},{8,11},{9,10},{10,... | collective-permute-start | bytes 36872 | tf_op jit(solution)/shard_map/ppermute | solution.py:168
  22.9 3.1 %collective-permute-start.11 = (f32[4,1,384]{2,1,0:T(1,128)S(1)}, f32[4,1,384]{2,1,0:T(1,128)S(1)}, u32[]{:S(2)}, u32[]{:S(2)}) collective-permute-start(f32[4,1,384]{2,1,0:T(1,128)S(1)} %slice.37), channel_id=1, source_target_pairs={{0,5},{1,4},{2,7},{3,6},{4,1},{5,0},{6,3},{7,2},{8,13},{9,12},{10,... | collective-permute-start | bytes 18440 | tf_op jit(solution)/shard_map/ppermute | solution.py:168
  26.0 4.0 %collective-permute-start.12 = (f32[2,1,384]{2,1,0:T(1,128)S(1)}, f32[2,1,384]{2,1,0:T(1,128)S(1)}, u32[]{:S(2)}, u32[]{:S(2)}) collective-permute-start(f32[2,1,384]{2,1,0:T(1,128)S(1)} %slice.39), channel_id=1, source_target_pairs={{0,9},{1,8},{2,11},{3,10},{4,13},{5,12},{6,15},{7,14},{8,1},{9,0},... | collective-permute-start | bytes 9224 | tf_op jit(solution)/shard_map/ppermute | solution.py:168
  30.0 1.2 %collective-permute-start.13 = (f32[1,1,384]{2,1,0:T(1,128)S(1)}, f32[1,1,384]{2,1,0:T(1,128)S(1)}, u32[]{:S(2)}, u32[]{:S(2)}) collective-permute-start(f32[1,1,384]{2,1,0:T(1,128)S(1)} %get-tuple-element.20), channel_id=1, source_target_pairs={{0,1},{1,0},{2,3},{3,2},{4,5},{5,4},{6,7},{7,6},{8,9},{9,8},{10,11... | collective-permute-start | bytes 4616 | tf_op jit(solution)/shard_map/ppermute | solution.py:168

commit v6 on v5

--- a/solution.py
+++ b/solution.py
@@ -220,13 +220,15 @@
     beyond, piece[xb[0]], piece[xb[1]] = lax.optimization_barrier((beyond, piece[xb[0]], piece[xb[1]]))
     ca, cb = across(xa), across(xb)
     [beyond] = score([ca[:m], *(piece[k] for k in xb)], only(xa[0] ^ 1, *xb), beyond)
-    beyond, cb, piece[f ^ g] = lax.optimization_barrier((beyond, cb, piece[f ^ g]))
+    beyond, cb = lax.optimization_barrier((beyond, cb))
     [beyond] = score([ca[m:], cb], only(xa[1] ^ 1, tuple(k ^ 1 for k in xb)), beyond)
 
+    beyond, piece[f ^ g] = lax.optimization_barrier((beyond, piece[f ^ g]))
     got = swap(beyond, 3)
     own = (0, f, g, f ^ g)
     cc = across(own)
-    [near] = score([piece[f ^ g], cc], only(f ^ g, tuple(k ^ 1 for k in own)), near)
+    alone = (f ^ g,)
+    [near] = score([piece[k] for k in alone] + [cc], only(*alone, tuple(k ^ 1 for k in own)), near)
     near = jnp.maximum(near, got)
     for k in (g, f):
         half = near.shape[0] // 2

time: 32.1 us -> 31.7 us (0.988)
  waiting for transfers between devices: 7.43 us -> 6.05 us
  starting transfers between devices: 16.3 us -> 17.4 us
    ppermute x14, waiting for transfers between devices: 7.43 us -> 6.05 us  [swap(): return lax.ppermute(x, 'shard', [(i, i ^ k) for i in range(shards)])]
    ppermute x14, starting transfers between devices: 16.3 us -> 17.4 us  [swap(): return lax.ppermute(x, 'shard', [(i, i ^ k) for i in range(shards)])]
where the time goes in v6:
time: 31.7 us; the launch traced here: 31.6 us
  starting transfers between devices  17.4 us (55%)
  Pallas kernels  7.31 us (23%)
  waiting for transfers between devices  6.05 us (19%)
  between operations  0.73 us (2%)
    ppermute x14, starting transfers between devices, swap(): return lax.ppermute(x, 'shard', [(i, i ^ k) for i in range(shards)])  17.4 us
    ppermute x14, waiting for transfers between devices, swap(): return lax.ppermute(x, 'shard', [(i, i ^ k) for i in range(shards)])  6.05 us
    pallas_call x4, Pallas kernels, score(): pl.pallas_call(functools.partial(score_kernel, slots, qt, cand, jobs, out...  5.34 us
    pallas_call x1, Pallas kernels, body(): pl.pallas_call(functools.partial(pack_kernel, slots), out_shape=pltpu.VME...  1.28 us
    pallas_call x1, Pallas kernels, body(): pl.pallas_call(last_kernel, out_shape=(jax.ShapeDtypeStruct((q_dev, qt),...  0.69 us
  transfers between devices with their start and end apart: 14, of which 6 were waited for; matrix products, arithmetic and copies ran while one was open for 0% of the time, Pallas kernels for 17%

profile of v6, /device:TPU:0, one launch (start us, length us, event | category | flops | bytes accessed | tf_op | source)
XLA Modules:
  0.0 31.6 jit_solution(6632366229177525858)
XLA Ops:
  0.7 1.3 %pack.1 = bf16[272,128]{1,0:T(8,128)(2,1)S(1)} custom-call(bf16[256,128]{1,0:T(8,128)(2,1)} %bitcast.9, s32[8,16]{1,0:T(8,128)} %bitcast.10, s32[8,16]{1,0:T(8,128)} %row_ref.1), custom_call_target="tpu_custom_call" | custom-call | flops 10000000000 | bytes 1000 | tf_op jit(solution)/shard_map/pack/pallas_call | solution.py:150
  1.9 3.5 %collective-permute-start.3 = (bf16[1,272,128]{2,1,0:T(8,128)(2,1)S(1)}, bf16[1,272,128]{2,1,0:T(8,128)(2,1)S(1)}, u32[]{:S(2)}, u32[]{:S(2)}) collective-permute-start(bf16[1,272,128]{2,1,0:T(8,128)(2,1)S(1)} %bitcast.3), channel_id=1, source_target_pairs={{0,9},{1,8},{2,11},{3,10},{4,13},{5,12},{6,15},{7,14},{8,1},{9,0},... | collective-permute-start | bytes 208904 | tf_op jit(solution)/shard_map/ppermute | solution.py:168
  5.5 2.8 %collective-permute-start.1 = (bf16[1,272,128]{2,1,0:T(8,128)(2,1)S(1)}, bf16[1,272,128]{2,1,0:T(8,128)(2,1)S(1)}, u32[]{:S(2)}, u32[]{:S(2)}) collective-permute-start(bf16[1,272,128]{2,1,0:T(8,128)(2,1)S(1)} %bitcast.4), channel_id=1, source_target_pairs={{0,7},{1,6},{2,5},{3,4},{4,3},{5,2},{6,1},{7,0},{8,15},{9,14},{10,... | collective-permute-start | bytes 208904 | tf_op jit(solution)/shard_map/ppermute | solution.py:168
  8.3 0.7 %collective-permute-start.4 = (bf16[1,272,128]{2,1,0:T(8,128)(2,1)S(1)}, bf16[1,272,128]{2,1,0:T(8,128)(2,1)S(1)}, u32[]{:S(2)}, u32[]{:S(2)}) collective-permute-start(bf16[1,272,128]{2,1,0:T(8,128)(2,1)S(1)} %bitcast.6), channel_id=1, source_target_pairs={{0,5},{1,4},{2,7},{3,6},{4,1},{5,0},{6,3},{7,2},{8,13},{9,12},{10,... | collective-permute-start | bytes 208904 | tf_op jit(solution)/shard_map/ppermute | solution.py:168
  9.0 2.4 %collective-permute-start.5 = (bf16[1,272,128]{2,1,0:T(8,128)(2,1)S(1)}, bf16[1,272,128]{2,1,0:T(8,128)(2,1)S(1)}, u32[]{:S(2)}, u32[]{:S(2)}) collective-permute-start(bf16[1,272,128]{2,1,0:T(8,128)(2,1)S(1)} %collective-permute-done.3.refs_1_), channel_id=1, source_target_pairs={{0,3},{1,2},{2,1},{3,0},{4,7},{5,6},{6,5},{7,4},{8,11},{9,10},{10,... | collective-permute-start | bytes 208904 | tf_op jit(solution)/shard_map/ppermute | solution.py:168
  11.3 0.9 %collective-permute-start.6 = (bf16[1,272,128]{2,1,0:T(8,128)(2,1)S(1)}, bf16[1,272,128]{2,1,0:T(8,128)(2,1)S(1)}, u32[]{:S(2)}, u32[]{:S(2)}) collective-permute-start(bf16[1,272,128]{2,1,0:T(8,128)(2,1)S(1)} %collective-permute-done.3.refs_1_), channel_id=1, source_target_pairs={{0,7},{1,6},{2,5},{3,4},{4,3},{5,2},{6,1},{7,0},{8,15},{9,14},{10,... | collective-permute-start | bytes 208904 | tf_op jit(solution)/shard_map/ppermute | solution.py:168
  12.2 0.5 %collective-permute-done.refs_3_ = bf16[1,272,128]{2,1,0:T(8,128)(2,1)S(1)} collective-permute-done((bf16[1,272,128]{2,1,0:T(8,128)(2,1)S(1)}, bf16[1,272,128]{2,1,0:T(8,128)(2,1)S(1)}, u32[]{:S(2)}, u32[]{:S(2)}) %collective-permute-start) | collective-permute-done | bytes 69664 | tf_op jit(solution)/shard_map/ppermute | solution.py:168
  13.0 1.7 %collective-permute-start.8 = (bf16[1,272,128]{2,1,0:T(8,128)(2,1)S(1)}, bf16[1,272,128]{2,1,0:T(8,128)(2,1)S(1)}, u32[]{:S(2)}, u32[]{:S(2)}) collective-permute-start(bf16[1,272,128]{2,1,0:T(8,128)(2,1)S(1)} %collective-permute-done.3.refs_1_), channel_id=1, source_target_pairs={{0,5},{1,4},{2,7},{3,6},{4,1},{5,0},{6,3},{7,2},{8,13},{9,12},{10,... | collective-permute-start | bytes 208904 | tf_op jit(solution)/shard_map/ppermute | solution.py:168
  14.7 1.6 %score.4 = (f32[8,1,384]{2,1,0:T(1,128)S(1)}, f32[8,1,384]{2,1,0:T(1,128)S(1)}) custom-call(bf16[1,272,128]{2,1,0:T(8,128)(2,1)S(1)} %bitcast.7, bf16[1,272,128]{2,1,0:T(8,128)(2,1)S(1)} %collective-permute-done.3.refs_1_, bf16[1,272,128]{2,1,0:T(8,128)(2,1)S(1)} %collective-permute-done.4.refs_2_, bf16[1,272,128]{2,1,0:T(8,128)(2,1)S(1)} %collective-permute-done.refs_3_, ...), custom_call_target="tpu_custom_call" | custom-call | flops 503316480 | bytes 5242880 | tf_op jit(solution)/shard_map/score/pallas_call | solution.py:174
  16.4 0.4 %collective-permute-start.7 = (bf16[2,272,128]{2,1,0:T(8,128)(2,1)S(1)}, bf16[2,272,128]{2,1,0:T(8,128)(2,1)S(1)}, u32[]{:S(2)}, u32[]{:S(2)}) collective-permute-start(bf16[2,272,128]{2,1,0:T(8,128)(2,1)S(1)} %pad_maximum_fusion.2), channel_id=1, source_target_pairs={{0,1},{1,0},{2,3},{3,2},{4,5},{5,4},{6,7},{7,6},{8,9},{9,8},{10,11... | collective-permute-start | bytes 417800 | tf_op jit(solution)/shard_map/ppermute | solution.py:168
  16.8 1.1 %score.5.refs_5_ = f32[8,1,384]{2,1,0:T(1,128)S(1)} custom-call(bf16[1,272,128]{2,1,0:T(8,128)(2,1)S(1)} %get-tuple-element.20.refs_0_, bf16[1,272,128]{2,1,0:T(8,128)(2,1)S(1)} %collective-permute-done.5.refs_1_, bf16[1,272,128]{2,1,0:T(8,128)(2,1)S(1)} %collective-permute-done.6.refs_2_, ...), custom_call_target="tpu_custom_call", output_to_operand_aliasing={{}: (6, {})} | custom-call | flops 301989888 | bytes 3145728 | tf_op jit(solution)/shard_map/score/pallas_call | solution.py:174
  17.9 1.1 %score.6 = f32[8,1,384]{2,1,0:T(1,128)S(1)} custom-call(bf16[1,272,128]{2,1,0:T(8,128)(2,1)S(1)} %get-tuple-element.21.refs_0_, bf16[2,272,128]{2,1,0:T(8,128)(2,1)S(1)} %collective-permute-done.7.refs_1_, bf16[512,128]{1,0:T(8,128)(2,1)S(1)} %copy-done.1, bf16[128,128,128]{2,1,0:T(8,128)(2,1)S(1)} %copy-done, ...), custom_call_target="tpu_custom_call", output_to_operand_aliasing={{}: (5, {})} | custom-call | flops 301989888 | bytes 3145728 | tf_op jit(solution)/shard_map/score/pallas_call | solution.py:174
  19.0 0.3 %collective-permute-start.9 = (bf16[4,272,128]{2,1,0:T(8,128)(2,1)S(1)}, bf16[4,272,128]{2,1,0:T(8,128)(2,1)S(1)}, u32[]{:S(2)}, u32[]{:S(2)}) collective-permute-start(bf16[4,272,128]{2,1,0:T(8,128)(2,1)S(1)} %pad_maximum_fusion), channel_id=1, source_target_pairs={{0,1},{1,0},{2,3},{3,2},{4,5},{5,4},{6,7},{7,6},{8,9},{9,8},{10,11... | collective-permute-start | bytes 835592 | tf_op jit(solution)/shard_map/ppermute | solution.py:168
  19.3 0.7 %collective-permute-start.10 = (f32[8,1,384]{2,1,0:T(1,128)S(1)}, f32[8,1,384]{2,1,0:T(1,128)S(1)}, u32[]{:S(2)}, u32[]{:S(2)}) collective-permute-start(f32[8,1,384]{2,1,0:T(1,128)S(1)} %score.6), channel_id=1, source_target_pairs={{0,3},{1,2},{2,1},{3,0},{4,7},{5,6},{6,5},{7,4},{8,11},{9,10},{10,... | collective-permute-start | bytes 36872 | tf_op jit(solution)/shard_map/ppermute | solution.py:168
  20.1 0.6 %collective-permute-done.9.refs_1_ = bf16[4,272,128]{2,1,0:T(8,128)(2,1)S(1)} collective-permute-done((bf16[4,272,128]{2,1,0:T(8,128)(2,1)S(1)}, bf16[4,272,128]{2,1,0:T(8,128)(2,1)S(1)}, u32[]{:S(2)}, u32[]{:S(2)}) %collective-permute-start.9) | collective-permute-done | bytes 278560 | tf_op jit(solution)/shard_map/ppermute | solution.py:168
  20.6 1.6 %score.7 = f32[8,1,384]{2,1,0:T(1,128)S(1)} custom-call(bf16[1,272,128]{2,1,0:T(8,128)(2,1)S(1)} %collective-permute-done.8.refs_0_, bf16[4,272,128]{2,1,0:T(8,128)(2,1)S(1)} %collective-permute-done.9.refs_1_, bf16[512,128]{1,0:T(8,128)(2,1)S(1)} %copy-done.1, bf16[128,128,128]{2,1,0:T(8,128)(2,1)S(1)} %copy-done, ...), custom_call_target="tpu_custom_call", output_to_operand_aliasing={{}: (5, {})} | custom-call | flops 503316480 | bytes 5242880 | tf_op jit(solution)/shard_map/score/pallas_call | solution.py:174
  22.2 0.2 collective-permute-done.10
  22.5 0.7 %collective-permute-start.11 = (f32[4,1,384]{2,1,0:T(1,128)S(1)}, f32[4,1,384]{2,1,0:T(1,128)S(1)}, u32[]{:S(2)}, u32[]{:S(2)}) collective-permute-start(f32[4,1,384]{2,1,0:T(1,128)S(1)} %slice.37), channel_id=1, source_target_pairs={{0,5},{1,4},{2,7},{3,6},{4,1},{5,0},{6,3},{7,2},{8,13},{9,12},{10,... | collective-permute-start | bytes 18440 | tf_op jit(solution)/shard_map/ppermute | solution.py:168
  23.2 2.5 %collective-permute-done.11 = f32[4,1,384]{2,1,0:T(1,128)S(1)} collective-permute-done((f32[4,1,384]{2,1,0:T(1,128)S(1)}, f32[4,1,384]{2,1,0:T(1,128)S(1)}, u32[]{:S(2)}, u32[]{:S(2)}) %collective-permute-start.11) | collective-permute-done | bytes 6176 | tf_op jit(solution)/shard_map/ppermute | solution.py:168
  25.6 2.7 %collective-permute-start.12 = (f32[2,1,384]{2,1,0:T(1,128)S(1)}, f32[2,1,384]{2,1,0:T(1,128)S(1)}, u32[]{:S(2)}, u32[]{:S(2)}) collective-permute-start(f32[2,1,384]{2,1,0:T(1,128)S(1)} %slice.39), channel_id=1, source_target_pairs={{0,9},{1,8},{2,11},{3,10},{4,13},{5,12},{6,15},{7,14},{8,1},{9,0},... | collective-permute-start | bytes 9224 | tf_op jit(solution)/shard_map/ppermute | solution.py:168
  28.4 1.3 %collective-permute-done.12 = f32[2,1,384]{2,1,0:T(1,128)S(1)} collective-permute-done((f32[2,1,384]{2,1,0:T(1,128)S(1)}, f32[2,1,384]{2,1,0:T(1,128)S(1)}, u32[]{:S(2)}, u32[]{:S(2)}) %collective-permute-start.12) | collective-permute-done | bytes 3104 | tf_op jit(solution)/shard_map/ppermute | solution.py:168
  29.7 0.3 collective-permute-start.13
  30.0 0.9 %collective-permute-done.13.b_ref = f32[1,1,384]{2,1,0:T(1,128)S(1)} collective-permute-done((f32[1,1,384]{2,1,0:T(1,128)S(1)}, f32[1,1,384]{2,1,0:T(1,128)S(1)}, u32[]{:S(2)}, u32[]{:S(2)}) %collective-permute-start.13) | collective-permute-done | bytes 1568 | tf_op jit(solution)/shard_map/ppermute | solution.py:168
  30.9 0.7 %last.1 = (f32[8,32]{1,0:T(8,128)}, f32[8,16]{1,0:T(8,128)}) custom-call(f32[1,1,384]{2,1,0:T(1,128)S(1)} %get-tuple-element.23.a_ref, f32[1,1,384]{2,1,0:T(1,128)S(1)} %collective-permute-done.13.b_ref), custom_call_target="tpu_custom_call" | custom-call | tf_op jit(solution)/shard_map/last/pallas_call | solution.py:241
  (26 shorter events, 0.4 us)
Async XLA Ops:
  0.6 14.0 %copy-start = (bf16[128,128,128]{2,1,0:T(8,128)(2,1)S(1)}, bf16[128,128,128]{2,1,0:T(8,128)(2,1)}, u32[]{:S(2)}) copy-start(bf16[128,128,128]{2,1,0:T(8,128)(2,1)} %refs_3_.5) | copy-start | bytes 12582916
  0.6 14.0 %copy-start.1 = (bf16[512,128]{1,0:T(8,128)(2,1)S(1)}, bf16[512,128]{1,0:T(8,128)(2,1)}, u32[]{:S(2)}) copy-start(bf16[512,128]{1,0:T(8,128)(2,1)} %refs_2_.3) | copy-start | bytes 393220
  0.7 14.0 %copy-start.2 = (s32[1,128]{1,0:T(1,128)S(1)}, s32[1,128]{1,0:T(1,128)}, u32[]{:S(2)}) copy-start(s32[1,128]{1,0:T(1,128)} %refs_4_.5) | copy-start | bytes 1540
  1.9 7.0 %collective-permute-start.3 = (bf16[1,272,128]{2,1,0:T(8,128)(2,1)S(1)}, bf16[1,272,128]{2,1,0:T(8,128)(2,1)S(1)}, u32[]{:S(2)}, u32[]{:S(2)}) collective-permute-start(bf16[1,272,128]{2,1,0:T(8,128)(2,1)S(1)} %bitcast.3), channel_id=1, source_target_pairs={{0,9},{1,8},{2,11},{3,10},{4,13},{5,12},{6,15},{7,14},{8,1},{9,0},... | collective-permute-start | bytes 208904 | tf_op jit(solution)/shard_map/ppermute | solution.py:168
  5.5 6.7 %collective-permute-start.1 = (bf16[1,272,128]{2,1,0:T(8,128)(2,1)S(1)}, bf16[1,272,128]{2,1,0:T(8,128)(2,1)S(1)}, u32[]{:S(2)}, u32[]{:S(2)}) collective-permute-start(bf16[1,272,128]{2,1,0:T(8,128)(2,1)S(1)} %bitcast.4), channel_id=1, source_target_pairs={{0,7},{1,6},{2,5},{3,4},{4,3},{5,2},{6,1},{7,0},{8,15},{9,14},{10,... | collective-permute-start | bytes 208904 | tf_op jit(solution)/shard_map/ppermute | solution.py:168
  8.3 4.5 %collective-permute-start = (bf16[1,272,128]{2,1,0:T(8,128)(2,1)S(1)}, bf16[1,272,128]{2,1,0:T(8,128)(2,1)S(1)}, u32[]{:S(2)}, u32[]{:S(2)}) collective-permute-start(bf16[1,272,128]{2,1,0:T(8,128)(2,1)S(1)} %bitcast.5), channel_id=1, source_target_pairs={{0,3},{1,2},{2,1},{3,0},{4,7},{5,6},{6,5},{7,4},{8,11},{9,10},{10,... | collective-permute-start | bytes 208904 | tf_op jit(solution)/shard_map/ppermute | solution.py:168
  8.3 6.4 %collective-permute-start.4 = (bf16[1,272,128]{2,1,0:T(8,128)(2,1)S(1)}, bf16[1,272,128]{2,1,0:T(8,128)(2,1)S(1)}, u32[]{:S(2)}, u32[]{:S(2)}) collective-permute-start(bf16[1,272,128]{2,1,0:T(8,128)(2,1)S(1)} %bitcast.6), channel_id=1, source_target_pairs={{0,5},{1,4},{2,7},{3,6},{4,1},{5,0},{6,3},{7,2},{8,13},{9,12},{10,... | collective-permute-start | bytes 208904 | tf_op jit(solution)/shard_map/ppermute | solution.py:168
  9.0 7.3 %collective-permute-start.5 = (bf16[1,272,128]{2,1,0:T(8,128)(2,1)S(1)}, bf16[1,272,128]{2,1,0:T(8,128)(2,1)S(1)}, u32[]{:S(2)}, u32[]{:S(2)}) collective-permute-start(bf16[1,272,128]{2,1,0:T(8,128)(2,1)S(1)} %collective-permute-done.3.refs_1_), channel_id=1, source_target_pairs={{0,3},{1,2},{2,1},{3,0},{4,7},{5,6},{6,5},{7,4},{8,11},{9,10},{10,... | collective-permute-start | bytes 208904 | tf_op jit(solution)/shard_map/ppermute | solution.py:168
  11.3 5.0 %collective-permute-start.6 = (bf16[1,272,128]{2,1,0:T(8,128)(2,1)S(1)}, bf16[1,272,128]{2,1,0:T(8,128)(2,1)S(1)}, u32[]{:S(2)}, u32[]{:S(2)}) collective-permute-start(bf16[1,272,128]{2,1,0:T(8,128)(2,1)S(1)} %collective-permute-done.3.refs_1_), channel_id=1, source_target_pairs={{0,7},{1,6},{2,5},{3,4},{4,3},{5,2},{6,1},{7,0},{8,15},{9,14},{10,... | collective-permute-start | bytes 208904 | tf_op jit(solution)/shard_map/ppermute | solution.py:168
  12.8 4.0 %collective-permute-start.2 = (bf16[2,272,128]{2,1,0:T(8,128)(2,1)S(1)}, bf16[2,272,128]{2,1,0:T(8,128)(2,1)S(1)}, u32[]{:S(2)}, u32[]{:S(2)}) collective-permute-start(bf16[2,272,128]{2,1,0:T(8,128)(2,1)S(1)} %pad_maximum_fusion.1), channel_id=1, source_target_pairs={{0,1},{1,0},{2,3},{3,2},{4,5},{5,4},{6,7},{7,6},{8,9},{9,8},{10,11... | collective-permute-start | bytes 417800 | tf_op jit(solution)/shard_map/ppermute | solution.py:168
  13.0 6.0 %collective-permute-start.8 = (bf16[1,272,128]{2,1,0:T(8,128)(2,1)S(1)}, bf16[1,272,128]{2,1,0:T(8,128)(2,1)S(1)}, u32[]{:S(2)}, u32[]{:S(2)}) collective-permute-start(bf16[1,272,128]{2,1,0:T(8,128)(2,1)S(1)} %collective-permute-done.3.refs_1_), channel_id=1, source_target_pairs={{0,5},{1,4},{2,7},{3,6},{4,1},{5,0},{6,3},{7,2},{8,13},{9,12},{10,... | collective-permute-start | bytes 208904 | tf_op jit(solution)/shard_map/ppermute | solution.py:168
  16.4 1.5 %collective-permute-start.7 = (bf16[2,272,128]{2,1,0:T(8,128)(2,1)S(1)}, bf16[2,272,128]{2,1,0:T(8,128)(2,1)S(1)}, u32[]{:S(2)}, u32[]{:S(2)}) collective-permute-start(bf16[2,272,128]{2,1,0:T(8,128)(2,1)S(1)} %pad_maximum_fusion.2), channel_id=1, source_target_pairs={{0,1},{1,0},{2,3},{3,2},{4,5},{5,4},{6,7},{7,6},{8,9},{9,8},{10,11... | collective-permute-start | bytes 417800 | tf_op jit(solution)/shard_map/ppermute | solution.py:168
  19.0 1.6 %collective-permute-start.9 = (bf16[4,272,128]{2,1,0:T(8,128)(2,1)S(1)}, bf16[4,272,128]{2,1,0:T(8,128)(2,1)S(1)}, u32[]{:S(2)}, u32[]{:S(2)}) collective-permute-start(bf16[4,272,128]{2,1,0:T(8,128)(2,1)S(1)} %pad_maximum_fusion), channel_id=1, source_target_pairs={{0,1},{1,0},{2,3},{3,2},{4,5},{5,4},{6,7},{7,6},{8,9},{9,8},{10,11... | collective-permute-start | bytes 835592 | tf_op jit(solution)/shard_map/ppermute | solution.py:168
  19.3 3.1 %collective-permute-start.10 = (f32[8,1,384]{2,1,0:T(1,128)S(1)}, f32[8,1,384]{2,1,0:T(1,128)S(1)}, u32[]{:S(2)}, u32[]{:S(2)}) collective-permute-start(f32[8,1,384]{2,1,0:T(1,128)S(1)} %score.6), channel_id=1, source_target_pairs={{0,3},{1,2},{2,1},{3,0},{4,7},{5,6},{6,5},{7,4},{8,11},{9,10},{10,... | collective-permute-start | bytes 36872 | tf_op jit(solution)/shard_map/ppermute | solution.py:168
  22.5 3.1 %collective-permute-start.11 = (f32[4,1,384]{2,1,0:T(1,128)S(1)}, f32[4,1,384]{2,1,0:T(1,128)S(1)}, u32[]{:S(2)}, u32[]{:S(2)}) collective-permute-start(f32[4,1,384]{2,1,0:T(1,128)S(1)} %slice.37), channel_id=1, source_target_pairs={{0,5},{1,4},{2,7},{3,6},{4,1},{5,0},{6,3},{7,2},{8,13},{9,12},{10,... | collective-permute-start | bytes 18440 | tf_op jit(solution)/shard_map/ppermute | solution.py:168
  25.6 4.1 %collective-permute-start.12 = (f32[2,1,384]{2,1,0:T(1,128)S(1)}, f32[2,1,384]{2,1,0:T(1,128)S(1)}, u32[]{:S(2)}, u32[]{:S(2)}) collective-permute-start(f32[2,1,384]{2,1,0:T(1,128)S(1)} %slice.39), channel_id=1, source_target_pairs={{0,9},{1,8},{2,11},{3,10},{4,13},{5,12},{6,15},{7,14},{8,1},{9,0},... | collective-permute-start | bytes 9224 | tf_op jit(solution)/shard_map/ppermute | solution.py:168
  29.7 1.2 %collective-permute-start.13 = (f32[1,1,384]{2,1,0:T(1,128)S(1)}, f32[1,1,384]{2,1,0:T(1,128)S(1)}, u32[]{:S(2)}, u32[]{:S(2)}) collective-permute-start(f32[1,1,384]{2,1,0:T(1,128)S(1)} %get-tuple-element.22), channel_id=1, source_target_pairs={{0,1},{1,0},{2,3},{3,2},{4,5},{5,4},{6,7},{7,6},{8,9},{9,8},{10,11... | collective-permute-start | bytes 4616 | tf_op jit(solution)/shard_map/ppermute | solution.py:168

commit v7 on v6

--- a/solution.py
+++ b/solution.py
@@ -215,7 +215,7 @@
         return tuple(tuple((0, at) for _, at in job) for job in jobs(first, *keys))
 
     xa, xb = (3, d), (f ^ 3, f ^ d)
-    early = (0, f, g, 3, d)
+    early = (f, g, 3, d)
     near, beyond = score([piece[k] for k in early], jobs(*early))
     beyond, piece[xb[0]], piece[xb[1]] = lax.optimization_barrier((beyond, piece[xb[0]], piece[xb[1]]))
     ca, cb = across(xa), across(xb)
@@ -227,8 +227,10 @@
     got = swap(beyond, 3)
     own = (0, f, g, f ^ g)
     cc = across(own)
-    alone = (f ^ g,)
-    [near] = score([piece[k] for k in alone] + [cc], only(*alone, tuple(k ^ 1 for k in own)), near)
+    alone = (0, f ^ g,)
+    [near] = score([piece[k] for k in alone], only(*alone), near)
+    near, cc = lax.optimization_barrier((near, cc))
+    [near] = score([cc], only(tuple(k ^ 1 for k in own)), near)
     near = jnp.maximum(near, got)
     for k in (g, f):
         half = near.shape[0] // 2

time: 31.7 us -> 31.7 us (level)
  waiting for transfers between devices: 6.05 us -> 5.59 us
  Pallas kernels: 7.31 us -> 7.65 us
    ppermute x14, waiting for transfers between devices: 6.05 us -> 5.59 us  [swap(): return lax.ppermute(x, 'shard', [(i, i ^ k) for i in range(shards)])]
    pallas_call x4 -> x5, Pallas kernels: 5.34 us -> 5.68 us  [score(): pl.pallas_call(functools.partial(score_kernel, slots, qt, cand, jobs, out...]
  transfers between devices with their start and end apart: 14 -> 14, of which waited for: 6 -> 6; matrix products, arithmetic and copies ran while one was open for 0% -> 0% of each run, Pallas kernels for 17% -> 18%
where the time goes in v7:
time: 31.7 us; the launch traced here: 31.6 us
  starting transfers between devices  17.5 us (55%)
  Pallas kernels  7.65 us (24%)
  waiting for transfers between devices  5.59 us (18%)
  between operations  0.73 us (2%)
    ppermute x14, starting transfers between devices, swap(): return lax.ppermute(x, 'shard', [(i, i ^ k) for i in range(shards)])  17.5 us
    pallas_call x5, Pallas kernels, score(): pl.pallas_call(functools.partial(score_kernel, slots, qt, cand, jobs, out...  5.68 us
    ppermute x14, waiting for transfers between devices, swap(): return lax.ppermute(x, 'shard', [(i, i ^ k) for i in range(shards)])  5.59 us
    pallas_call x1, Pallas kernels, body(): pl.pallas_call(functools.partial(pack_kernel, slots), out_shape=pltpu.VME...  1.28 us
    pallas_call x1, Pallas kernels, body(): pl.pallas_call(last_kernel, out_shape=(jax.ShapeDtypeStruct((q_dev, qt),...  0.69 us
  transfers between devices with their start and end apart: 14, of which 6 were waited for; matrix products, arithmetic and copies ran while one was open for 0% of the time, Pallas kernels for 18%

profile of v7, /device:TPU:0, one launch (start us, length us, event | category | flops | bytes accessed | tf_op | source)
XLA Modules:
  0.0 31.6 jit_solution(18364432408248285453)
XLA Ops:
  0.7 1.3 %pack.1 = bf16[272,128]{1,0:T(8,128)(2,1)S(1)} custom-call(bf16[256,128]{1,0:T(8,128)(2,1)} %bitcast.9, s32[8,16]{1,0:T(8,128)} %bitcast.10, s32[8,16]{1,0:T(8,128)} %row_ref.1), custom_call_target="tpu_custom_call" | custom-call | flops 10000000000 | bytes 1000 | tf_op jit(solution)/shard_map/pack/pallas_call | solution.py:150
  1.9 3.5 %collective-permute-start.3 = (bf16[1,272,128]{2,1,0:T(8,128)(2,1)S(1)}, bf16[1,272,128]{2,1,0:T(8,128)(2,1)S(1)}, u32[]{:S(2)}, u32[]{:S(2)}) collective-permute-start(bf16[1,272,128]{2,1,0:T(8,128)(2,1)S(1)} %bitcast.3), channel_id=1, source_target_pairs={{0,9},{1,8},{2,11},{3,10},{4,13},{5,12},{6,15},{7,14},{8,1},{9,0},... | collective-permute-start | bytes 208904 | tf_op jit(solution)/shard_map/ppermute | solution.py:168
  5.5 2.8 %collective-permute-start.1 = (bf16[1,272,128]{2,1,0:T(8,128)(2,1)S(1)}, bf16[1,272,128]{2,1,0:T(8,128)(2,1)S(1)}, u32[]{:S(2)}, u32[]{:S(2)}) collective-permute-start(bf16[1,272,128]{2,1,0:T(8,128)(2,1)S(1)} %bitcast.4), channel_id=1, source_target_pairs={{0,7},{1,6},{2,5},{3,4},{4,3},{5,2},{6,1},{7,0},{8,15},{9,14},{10,... | collective-permute-start | bytes 208904 | tf_op jit(solution)/shard_map/ppermute | solution.py:168
  8.3 0.7 %collective-permute-start.4 = (bf16[1,272,128]{2,1,0:T(8,128)(2,1)S(1)}, bf16[1,272,128]{2,1,0:T(8,128)(2,1)S(1)}, u32[]{:S(2)}, u32[]{:S(2)}) collective-permute-start(bf16[1,272,128]{2,1,0:T(8,128)(2,1)S(1)} %bitcast.6), channel_id=1, source_target_pairs={{0,5},{1,4},{2,7},{3,6},{4,1},{5,0},{6,3},{7,2},{8,13},{9,12},{10,... | collective-permute-start | bytes 208904 | tf_op jit(solution)/shard_map/ppermute | solution.py:168
  9.0 2.4 %collective-permute-start.5 = (bf16[1,272,128]{2,1,0:T(8,128)(2,1)S(1)}, bf16[1,272,128]{2,1,0:T(8,128)(2,1)S(1)}, u32[]{:S(2)}, u32[]{:S(2)}) collective-permute-start(bf16[1,272,128]{2,1,0:T(8,128)(2,1)S(1)} %collective-permute-done.3.refs_0_), channel_id=1, source_target_pairs={{0,3},{1,2},{2,1},{3,0},{4,7},{5,6},{6,5},{7,4},{8,11},{9,10},{10,... | collective-permute-start | bytes 208904 | tf_op jit(solution)/shard_map/ppermute | solution.py:168
  11.3 0.9 %collective-permute-start.6 = (bf16[1,272,128]{2,1,0:T(8,128)(2,1)S(1)}, bf16[1,272,128]{2,1,0:T(8,128)(2,1)S(1)}, u32[]{:S(2)}, u32[]{:S(2)}) collective-permute-start(bf16[1,272,128]{2,1,0:T(8,128)(2,1)S(1)} %collective-permute-done.3.refs_0_), channel_id=1, source_target_pairs={{0,7},{1,6},{2,5},{3,4},{4,3},{5,2},{6,1},{7,0},{8,15},{9,14},{10,... | collective-permute-start | bytes 208904 | tf_op jit(solution)/shard_map/ppermute | solution.py:168
  12.2 0.5 %collective-permute-done.refs_2_ = bf16[1,272,128]{2,1,0:T(8,128)(2,1)S(1)} collective-permute-done((bf16[1,272,128]{2,1,0:T(8,128)(2,1)S(1)}, bf16[1,272,128]{2,1,0:T(8,128)(2,1)S(1)}, u32[]{:S(2)}, u32[]{:S(2)}) %collective-permute-start) | collective-permute-done | bytes 69664 | tf_op jit(solution)/shard_map/ppermute | solution.py:168
  13.0 1.7 %collective-permute-start.8 = (bf16[1,272,128]{2,1,0:T(8,128)(2,1)S(1)}, bf16[1,272,128]{2,1,0:T(8,128)(2,1)S(1)}, u32[]{:S(2)}, u32[]{:S(2)}) collective-permute-start(bf16[1,272,128]{2,1,0:T(8,128)(2,1)S(1)} %collective-permute-done.3.refs_0_), channel_id=1, source_target_pairs={{0,5},{1,4},{2,7},{3,6},{4,1},{5,0},{6,3},{7,2},{8,13},{9,12},{10,... | collective-permute-start | bytes 208904 | tf_op jit(solution)/shard_map/ppermute | solution.py:168
  14.7 1.4 %score.5 = (f32[8,1,384]{2,1,0:T(1,128)S(1)}, f32[8,1,384]{2,1,0:T(1,128)S(1)}) custom-call(bf16[1,272,128]{2,1,0:T(8,128)(2,1)S(1)} %collective-permute-done.3.refs_0_, bf16[1,272,128]{2,1,0:T(8,128)(2,1)S(1)} %collective-permute-done.4.refs_1_, bf16[1,272,128]{2,1,0:T(8,128)(2,1)S(1)} %collective-permute-done.refs_2_, ...), custom_call_target="tpu_custom_call" | custom-call | flops 402653184 | bytes 4194304 | tf_op jit(solution)/shard_map/score/pallas_call | solution.py:174
  16.1 0.3 collective-permute-done.6.refs_2_
  16.4 0.4 %collective-permute-start.7 = (bf16[2,272,128]{2,1,0:T(8,128)(2,1)S(1)}, bf16[2,272,128]{2,1,0:T(8,128)(2,1)S(1)}, u32[]{:S(2)}, u32[]{:S(2)}) collective-permute-start(bf16[2,272,128]{2,1,0:T(8,128)(2,1)S(1)} %pad_maximum_fusion.2), channel_id=1, source_target_pairs={{0,1},{1,0},{2,3},{3,2},{4,5},{5,4},{6,7},{7,6},{8,9},{9,8},{10,11... | collective-permute-start | bytes 417800 | tf_op jit(solution)/shard_map/ppermute | solution.py:168
  16.8 1.1 %score.6.refs_5_ = f32[8,1,384]{2,1,0:T(1,128)S(1)} custom-call(bf16[1,272,128]{2,1,0:T(8,128)(2,1)S(1)} %get-tuple-element.24.refs_0_, bf16[1,272,128]{2,1,0:T(8,128)(2,1)S(1)} %collective-permute-done.5.refs_1_, bf16[1,272,128]{2,1,0:T(8,128)(2,1)S(1)} %collective-permute-done.6.refs_2_, ...), custom_call_target="tpu_custom_call", output_to_operand_aliasing={{}: (6, {})} | custom-call | flops 301989888 | bytes 3145728 | tf_op jit(solution)/shard_map/score/pallas_call | solution.py:174
  17.9 1.1 %score.7 = f32[8,1,384]{2,1,0:T(1,128)S(1)} custom-call(bf16[1,272,128]{2,1,0:T(8,128)(2,1)S(1)} %get-tuple-element.25.refs_0_, bf16[2,272,128]{2,1,0:T(8,128)(2,1)S(1)} %collective-permute-done.7.refs_1_, bf16[512,128]{1,0:T(8,128)(2,1)S(1)} %copy-done.1, bf16[128,128,128]{2,1,0:T(8,128)(2,1)S(1)} %copy-done, ...), custom_call_target="tpu_custom_call", output_to_operand_aliasing={{}: (5, {})} | custom-call | flops 301989888 | bytes 3145728 | tf_op jit(solution)/shard_map/score/pallas_call | solution.py:174
  19.0 0.3 %collective-permute-start.9 = (bf16[4,272,128]{2,1,0:T(8,128)(2,1)S(1)}, bf16[4,272,128]{2,1,0:T(8,128)(2,1)S(1)}, u32[]{:S(2)}, u32[]{:S(2)}) collective-permute-start(bf16[4,272,128]{2,1,0:T(8,128)(2,1)S(1)} %pad_maximum_fusion), channel_id=1, source_target_pairs={{0,1},{1,0},{2,3},{3,2},{4,5},{5,4},{6,7},{7,6},{8,9},{9,8},{10,11... | collective-permute-start | bytes 835592 | tf_op jit(solution)/shard_map/ppermute | solution.py:168
  19.3 0.7 %collective-permute-start.10 = (f32[8,1,384]{2,1,0:T(1,128)S(1)}, f32[8,1,384]{2,1,0:T(1,128)S(1)}, u32[]{:S(2)}, u32[]{:S(2)}) collective-permute-start(f32[8,1,384]{2,1,0:T(1,128)S(1)} %score.7), channel_id=1, source_target_pairs={{0,3},{1,2},{2,1},{3,0},{4,7},{5,6},{6,5},{7,4},{8,11},{9,10},{10,... | collective-permute-start | bytes 36872 | tf_op jit(solution)/shard_map/ppermute | solution.py:168
  20.1 0.8 %score.8.refs_4_ = f32[8,1,384]{2,1,0:T(1,128)S(1)} custom-call(bf16[1,272,128]{2,1,0:T(8,128)(2,1)S(1)} %bitcast.8, bf16[1,272,128]{2,1,0:T(8,128)(2,1)S(1)} %collective-permute-done.8.refs_1_, bf16[512,128]{1,0:T(8,128)(2,1)S(1)} %copy-done.1, bf16[128,128,128]{2,1,0:T(8,128)(2,1)S(1)} %copy-done, ...), custom_call_target="tpu_custom_call", output_to_operand_aliasing={{}: (5, {})} | custom-call | flops 201326592 | bytes 2097152 | tf_op jit(solution)/shard_map/score/pallas_call | solution.py:174
  20.9 1.4 %score.9 = f32[8,1,384]{2,1,0:T(1,128)S(1)} custom-call(bf16[4,272,128]{2,1,0:T(8,128)(2,1)S(1)} %collective-permute-done.9.refs_0_, bf16[512,128]{1,0:T(8,128)(2,1)S(1)} %copy-done.1, bf16[128,128,128]{2,1,0:T(8,128)(2,1)S(1)} %copy-done, s32[1,128]{1,0:T(1,128)S(1)} %copy-done.2, f32[8,1,384]{2,1,0:T(1,128)S(1)} %score.8.refs_4_), custom_call_target="tpu_custom_call", output_to_operand_aliasing={{}: (4, {})} | custom-call | flops 402653184 | bytes 4194304 | tf_op jit(solution)/shard_map/score/pallas_call | solution.py:174
  22.5 0.8 %collective-permute-start.11 = (f32[4,1,384]{2,1,0:T(1,128)S(1)}, f32[4,1,384]{2,1,0:T(1,128)S(1)}, u32[]{:S(2)}, u32[]{:S(2)}) collective-permute-start(f32[4,1,384]{2,1,0:T(1,128)S(1)} %slice.37), channel_id=1, source_target_pairs={{0,5},{1,4},{2,7},{3,6},{4,1},{5,0},{6,3},{7,2},{8,13},{9,12},{10,... | collective-permute-start | bytes 18440 | tf_op jit(solution)/shard_map/ppermute | solution.py:168
  23.3 2.3 %collective-permute-done.11 = f32[4,1,384]{2,1,0:T(1,128)S(1)} collective-permute-done((f32[4,1,384]{2,1,0:T(1,128)S(1)}, f32[4,1,384]{2,1,0:T(1,128)S(1)}, u32[]{:S(2)}, u32[]{:S(2)}) %collective-permute-start.11) | collective-permute-done | bytes 6176 | tf_op jit(solution)/shard_map/ppermute | solution.py:168
  25.6 2.7 %collective-permute-start.12 = (f32[2,1,384]{2,1,0:T(1,128)S(1)}, f32[2,1,384]{2,1,0:T(1,128)S(1)}, u32[]{:S(2)}, u32[]{:S(2)}) collective-permute-start(f32[2,1,384]{2,1,0:T(1,128)S(1)} %slice.39), channel_id=1, source_target_pairs={{0,9},{1,8},{2,11},{3,10},{4,13},{5,12},{6,15},{7,14},{8,1},{9,0},... | collective-permute-start | bytes 9224 | tf_op jit(solution)/shard_map/ppermute | solution.py:168
  28.4 1.3 %collective-permute-done.12 = f32[2,1,384]{2,1,0:T(1,128)S(1)} collective-permute-done((f32[2,1,384]{2,1,0:T(1,128)S(1)}, f32[2,1,384]{2,1,0:T(1,128)S(1)}, u32[]{:S(2)}, u32[]{:S(2)}) %collective-permute-start.12) | collective-permute-done | bytes 3104 | tf_op jit(solution)/shard_map/ppermute | solution.py:168
  29.7 0.3 collective-permute-start.13
  30.0 0.9 %collective-permute-done.13.b_ref = f32[1,1,384]{2,1,0:T(1,128)S(1)} collective-permute-done((f32[1,1,384]{2,1,0:T(1,128)S(1)}, f32[1,1,384]{2,1,0:T(1,128)S(1)}, u32[]{:S(2)}, u32[]{:S(2)}) %collective-permute-start.13) | collective-permute-done | bytes 1568 | tf_op jit(solution)/shard_map/ppermute | solution.py:168
  30.9 0.7 %last.1 = (f32[8,32]{1,0:T(8,128)}, f32[8,16]{1,0:T(8,128)}) custom-call(f32[1,1,384]{2,1,0:T(1,128)S(1)} %get-tuple-element.27.a_ref, f32[1,1,384]{2,1,0:T(1,128)S(1)} %collective-permute-done.13.b_ref), custom_call_target="tpu_custom_call" | custom-call | tf_op jit(solution)/shard_map/last/pallas_call | solution.py:243
  (27 shorter events, 0.6 us)
Async XLA Ops:
  0.6 14.0 %copy-start = (bf16[128,128,128]{2,1,0:T(8,128)(2,1)S(1)}, bf16[128,128,128]{2,1,0:T(8,128)(2,1)}, u32[]{:S(2)}) copy-start(bf16[128,128,128]{2,1,0:T(8,128)(2,1)} %refs_2_.5) | copy-start | bytes 12582916
  0.6 14.0 %copy-start.1 = (bf16[512,128]{1,0:T(8,128)(2,1)S(1)}, bf16[512,128]{1,0:T(8,128)(2,1)}, u32[]{:S(2)}) copy-start(bf16[512,128]{1,0:T(8,128)(2,1)} %refs_1_.1) | copy-start | bytes 393220
  0.7 14.0 %copy-start.2 = (s32[1,128]{1,0:T(1,128)S(1)}, s32[1,128]{1,0:T(1,128)}, u32[]{:S(2)}) copy-start(s32[1,128]{1,0:T(1,128)} %refs_3_.7) | copy-start | bytes 1540
  1.9 7.0 %collective-permute-start.3 = (bf16[1,272,128]{2,1,0:T(8,128)(2,1)S(1)}, bf16[1,272,128]{2,1,0:T(8,128)(2,1)S(1)}, u32[]{:S(2)}, u32[]{:S(2)}) collective-permute-start(bf16[1,272,128]{2,1,0:T(8,128)(2,1)S(1)} %bitcast.3), channel_id=1, source_target_pairs={{0,9},{1,8},{2,11},{3,10},{4,13},{5,12},{6,15},{7,14},{8,1},{9,0},... | collective-permute-start | bytes 208904 | tf_op jit(solution)/shard_map/ppermute | solution.py:168
  5.5 6.7 %collective-permute-start.1 = (bf16[1,272,128]{2,1,0:T(8,128)(2,1)S(1)}, bf16[1,272,128]{2,1,0:T(8,128)(2,1)S(1)}, u32[]{:S(2)}, u32[]{:S(2)}) collective-permute-start(bf16[1,272,128]{2,1,0:T(8,128)(2,1)S(1)} %bitcast.4), channel_id=1, source_target_pairs={{0,7},{1,6},{2,5},{3,4},{4,3},{5,2},{6,1},{7,0},{8,15},{9,14},{10,... | collective-permute-start | bytes 208904 | tf_op jit(solution)/shard_map/ppermute | solution.py:168
  8.3 4.5 %collective-permute-start = (bf16[1,272,128]{2,1,0:T(8,128)(2,1)S(1)}, bf16[1,272,128]{2,1,0:T(8,128)(2,1)S(1)}, u32[]{:S(2)}, u32[]{:S(2)}) collective-permute-start(bf16[1,272,128]{2,1,0:T(8,128)(2,1)S(1)} %bitcast.5), channel_id=1, source_target_pairs={{0,3},{1,2},{2,1},{3,0},{4,7},{5,6},{6,5},{7,4},{8,11},{9,10},{10,... | collective-permute-start | bytes 208904 | tf_op jit(solution)/shard_map/ppermute | solution.py:168
  8.3 6.4 %collective-permute-start.4 = (bf16[1,272,128]{2,1,0:T(8,128)(2,1)S(1)}, bf16[1,272,128]{2,1,0:T(8,128)(2,1)S(1)}, u32[]{:S(2)}, u32[]{:S(2)}) collective-permute-start(bf16[1,272,128]{2,1,0:T(8,128)(2,1)S(1)} %bitcast.6), channel_id=1, source_target_pairs={{0,5},{1,4},{2,7},{3,6},{4,1},{5,0},{6,3},{7,2},{8,13},{9,12},{10,... | collective-permute-start | bytes 208904 | tf_op jit(solution)/shard_map/ppermute | solution.py:168
  9.0 7.1 %collective-permute-start.5 = (bf16[1,272,128]{2,1,0:T(8,128)(2,1)S(1)}, bf16[1,272,128]{2,1,0:T(8,128)(2,1)S(1)}, u32[]{:S(2)}, u32[]{:S(2)}) collective-permute-start(bf16[1,272,128]{2,1,0:T(8,128)(2,1)S(1)} %collective-permute-done.3.refs_0_), channel_id=1, source_target_pairs={{0,3},{1,2},{2,1},{3,0},{4,7},{5,6},{6,5},{7,4},{8,11},{9,10},{10,... | collective-permute-start | bytes 208904 | tf_op jit(solution)/shard_map/ppermute | solution.py:168
  11.3 5.0 %collective-permute-start.6 = (bf16[1,272,128]{2,1,0:T(8,128)(2,1)S(1)}, bf16[1,272,128]{2,1,0:T(8,128)(2,1)S(1)}, u32[]{:S(2)}, u32[]{:S(2)}) collective-permute-start(bf16[1,272,128]{2,1,0:T(8,128)(2,1)S(1)} %collective-permute-done.3.refs_0_), channel_id=1, source_target_pairs={{0,7},{1,6},{2,5},{3,4},{4,3},{5,2},{6,1},{7,0},{8,15},{9,14},{10,... | collective-permute-start | bytes 208904 | tf_op jit(solution)/shard_map/ppermute | solution.py:168
  12.8 4.0 %collective-permute-start.2 = (bf16[2,272,128]{2,1,0:T(8,128)(2,1)S(1)}, bf16[2,272,128]{2,1,0:T(8,128)(2,1)S(1)}, u32[]{:S(2)}, u32[]{:S(2)}) collective-permute-start(bf16[2,272,128]{2,1,0:T(8,128)(2,1)S(1)} %pad_maximum_fusion.1), channel_id=1, source_target_pairs={{0,1},{1,0},{2,3},{3,2},{4,5},{5,4},{6,7},{7,6},{8,9},{9,8},{10,11... | collective-permute-start | bytes 417800 | tf_op jit(solution)/shard_map/ppermute | solution.py:168
  13.0 6.0 %collective-permute-start.8 = (bf16[1,272,128]{2,1,0:T(8,128)(2,1)S(1)}, bf16[1,272,128]{2,1,0:T(8,128)(2,1)S(1)}, u32[]{:S(2)}, u32[]{:S(2)}) collective-permute-start(bf16[1,272,128]{2,1,0:T(8,128)(2,1)S(1)} %collective-permute-done.3.refs_0_), channel_id=1, source_target_pairs={{0,5},{1,4},{2,7},{3,6},{4,1},{5,0},{6,3},{7,2},{8,13},{9,12},{10,... | collective-permute-start | bytes 208904 | tf_op jit(solution)/shard_map/ppermute | solution.py:168
  16.4 1.5 %collective-permute-start.7 = (bf16[2,272,128]{2,1,0:T(8,128)(2,1)S(1)}, bf16[2,272,128]{2,1,0:T(8,128)(2,1)S(1)}, u32[]{:S(2)}, u32[]{:S(2)}) collective-permute-start(bf16[2,272,128]{2,1,0:T(8,128)(2,1)S(1)} %pad_maximum_fusion.2), channel_id=1, source_target_pairs={{0,1},{1,0},{2,3},{3,2},{4,5},{5,4},{6,7},{7,6},{8,9},{9,8},{10,11... | collective-permute-start | bytes 417800 | tf_op jit(solution)/shard_map/ppermute | solution.py:168
  19.0 1.9 %collective-permute-start.9 = (bf16[4,272,128]{2,1,0:T(8,128)(2,1)S(1)}, bf16[4,272,128]{2,1,0:T(8,128)(2,1)S(1)}, u32[]{:S(2)}, u32[]{:S(2)}) collective-permute-start(bf16[4,272,128]{2,1,0:T(8,128)(2,1)S(1)} %pad_maximum_fusion), channel_id=1, source_target_pairs={{0,1},{1,0},{2,3},{3,2},{4,5},{5,4},{6,7},{7,6},{8,9},{9,8},{10,11... | collective-permute-start | bytes 835592 | tf_op jit(solution)/shard_map/ppermute | solution.py:168
  19.3 3.1 %collective-permute-start.10 = (f32[8,1,384]{2,1,0:T(1,128)S(1)}, f32[8,1,384]{2,1,0:T(1,128)S(1)}, u32[]{:S(2)}, u32[]{:S(2)}) collective-permute-start(f32[8,1,384]{2,1,0:T(1,128)S(1)} %score.7), channel_id=1, source_target_pairs={{0,3},{1,2},{2,1},{3,0},{4,7},{5,6},{6,5},{7,4},{8,11},{9,10},{10,... | collective-permute-start | bytes 36872 | tf_op jit(solution)/shard_map/ppermute | solution.py:168
  22.5 3.1 %collective-permute-start.11 = (f32[4,1,384]{2,1,0:T(1,128)S(1)}, f32[4,1,384]{2,1,0:T(1,128)S(1)}, u32[]{:S(2)}, u32[]{:S(2)}) collective-permute-start(f32[4,1,384]{2,1,0:T(1,128)S(1)} %slice.37), channel_id=1, source_target_pairs={{0,5},{1,4},{2,7},{3,6},{4,1},{5,0},{6,3},{7,2},{8,13},{9,12},{10,... | collective-permute-start | bytes 18440 | tf_op jit(solution)/shard_map/ppermute | solution.py:168
  25.6 4.1 %collective-permute-start.12 = (f32[2,1,384]{2,1,0:T(1,128)S(1)}, f32[2,1,384]{2,1,0:T(1,128)S(1)}, u32[]{:S(2)}, u32[]{:S(2)}) collective-permute-start(f32[2,1,384]{2,1,0:T(1,128)S(1)} %slice.39), channel_id=1, source_target_pairs={{0,9},{1,8},{2,11},{3,10},{4,13},{5,12},{6,15},{7,14},{8,1},{9,0},... | collective-permute-start | bytes 9224 | tf_op jit(solution)/shard_map/ppermute | solution.py:168
  29.7 1.2 %collective-permute-start.13 = (f32[1,1,384]{2,1,0:T(1,128)S(1)}, f32[1,1,384]{2,1,0:T(1,128)S(1)}, u32[]{:S(2)}, u32[]{:S(2)}) collective-permute-start(f32[1,1,384]{2,1,0:T(1,128)S(1)} %get-tuple-element.26), channel_id=1, source_target_pairs={{0,1},{1,0},{2,3},{3,2},{4,5},{5,4},{6,7},{7,6},{8,9},{9,8},{10,11... | collective-permute-start | bytes 4616 | tf_op jit(solution)/shard_map/ppermute | solution.py:168

commit v8 on v6

--- a/solution.py
+++ b/solution.py
@@ -40,16 +40,16 @@
     place = lax.broadcasted_iota(jnp.int32, (LANES, LANES), 0).astype(jnp.float32)
     copies[0].wait()
     copies[1].wait()
-    both = jnp.concatenate([owner_held[...], row_held[...]], axis=0).astype(jnp.float32)
-    wide = jnp.dot(both, spread, preferred_element_type=jnp.float32)
+    both = jnp.concatenate([owner_held[...], row_held[...]], axis=0).astype(jnp.float32).astype(jnp.bfloat16)
+    wide = jnp.dot(both, spread.astype(jnp.bfloat16), preferred_element_type=jnp.float32)
     owner = jnp.sum(jnp.where(own_q, wide[:q_dev], 0.0), axis=0, keepdims=True)
     row = jnp.sum(jnp.where(own_q, wide[q_dev:], 0.0), axis=0, keepdims=True)
     hit = each == owner
-    rank = jnp.dot(hit.astype(jnp.float32), earlier, preferred_element_type=jnp.float32)
+    rank = jnp.dot(hit.astype(jnp.bfloat16), earlier.astype(jnp.bfloat16), preferred_element_type=jnp.float32)
     rank = jnp.sum(jnp.where(hit, rank, 0.0), axis=0, keepdims=True)
-    rows = lax.dot_general(jnp.where(hit, row, 0.0), (place == rank).astype(jnp.float32), NT,
+    rows = lax.dot_general(jnp.where(hit, row, 0.0).astype(jnp.bfloat16), (place == rank).astype(jnp.bfloat16), NT,
                            preferred_element_type=jnp.float32)
-    numbers = lax.dot_general(jnp.where(hit, number, 0.0), (place == rank + slots).astype(jnp.float32), NT,
+    numbers = lax.dot_general(jnp.where(hit, number, 0.0).astype(jnp.bfloat16), (place == rank + slots).astype(jnp.bfloat16), NT,
                               preferred_element_type=jnp.float32)
     out_ref[tokens:] = (rows + numbers).astype(out_ref.dtype)
     copies[2].wait()
@@ -204,7 +204,7 @@
     def across(keys):
         return swap(jnp.concatenate([piece[k] for k in keys], axis=0), 1)
 
-    column = (0, 1, f, f ^ 1, g, g ^ 1, f ^ g, f ^ g ^ 1)
+    column = (0, 1, g, g ^ 1, f, f ^ 1, f ^ g, f ^ g ^ 1)
     place = {k: (0, n * m) for n, k in enumerate(column)}
     place.update({k ^ 3: (1, n * m) for n, k in enumerate(column)})
 
@@ -230,7 +230,7 @@
     alone = (f ^ g,)
     [near] = score([piece[k] for k in alone] + [cc], only(*alone, tuple(k ^ 1 for k in own)), near)
     near = jnp.maximum(near, got)
-    for k in (g, f):
+    for k in (f, g):
         half = near.shape[0] // 2
         near = jnp.maximum(near[:half], swap(near[half:], k))
     near = near.reshape(2, m, *near.shape[1:])

time: 31.7 us -> 31.7 us (level)
  no operation moved by 1% of the time
where the time goes in v8:
time: 31.7 us; the launch traced here: 31.6 us
  starting transfers between devices  17.4 us (55%)
  Pallas kernels  7.32 us (23%)
  waiting for transfers between devices  5.97 us (19%)
  between operations  0.73 us (2%)
    ppermute x14, starting transfers between devices, swap(): return lax.ppermute(x, 'shard', [(i, i ^ k) for i in range(shards)])  17.4 us
    ppermute x14, waiting for transfers between devices, swap(): return lax.ppermute(x, 'shard', [(i, i ^ k) for i in range(shards)])  5.97 us
    pallas_call x4, Pallas kernels, score(): pl.pallas_call(functools.partial(score_kernel, slots, qt, cand, jobs, out...  5.35 us
    pallas_call x1, Pallas kernels, body(): pl.pallas_call(functools.partial(pack_kernel, slots), out_shape=pltpu.VME...  1.28 us
    pallas_call x1, Pallas kernels, body(): pl.pallas_call(last_kernel, out_shape=(jax.ShapeDtypeStruct((q_dev, qt),...  0.69 us
  transfers between devices with their start and end apart: 14, of which 6 were waited for; matrix products, arithmetic and copies ran while one was open for 0% of the time, Pallas kernels for 17%

profile of v8, /device:TPU:0, one launch (start us, length us, event | category | flops | bytes accessed | tf_op | source)
XLA Modules:
  0.0 31.6 jit_solution(1560582163904960449)
XLA Ops:
  0.7 1.3 %pack.1 = bf16[272,128]{1,0:T(8,128)(2,1)S(1)} custom-call(bf16[256,128]{1,0:T(8,128)(2,1)} %bitcast.9, s32[8,16]{1,0:T(8,128)} %bitcast.10, s32[8,16]{1,0:T(8,128)} %row_ref.1), custom_call_target="tpu_custom_call" | custom-call | flops 10000000000 | bytes 1000 | tf_op jit(solution)/shard_map/pack/pallas_call | solution.py:150
  1.9 3.5 %collective-permute-start.3 = (bf16[1,272,128]{2,1,0:T(8,128)(2,1)S(1)}, bf16[1,272,128]{2,1,0:T(8,128)(2,1)S(1)}, u32[]{:S(2)}, u32[]{:S(2)}) collective-permute-start(bf16[1,272,128]{2,1,0:T(8,128)(2,1)S(1)} %bitcast.3), channel_id=1, source_target_pairs={{0,9},{1,8},{2,11},{3,10},{4,13},{5,12},{6,15},{7,14},{8,1},{9,0},... | collective-permute-start | bytes 208904 | tf_op jit(solution)/shard_map/ppermute | solution.py:168
  5.5 2.8 %collective-permute-start.1 = (bf16[1,272,128]{2,1,0:T(8,128)(2,1)S(1)}, bf16[1,272,128]{2,1,0:T(8,128)(2,1)S(1)}, u32[]{:S(2)}, u32[]{:S(2)}) collective-permute-start(bf16[1,272,128]{2,1,0:T(8,128)(2,1)S(1)} %bitcast.4), channel_id=1, source_target_pairs={{0,7},{1,6},{2,5},{3,4},{4,3},{5,2},{6,1},{7,0},{8,15},{9,14},{10,... | collective-permute-start | bytes 208904 | tf_op jit(solution)/shard_map/ppermute | solution.py:168
  8.3 0.7 %collective-permute-start.4 = (bf16[1,272,128]{2,1,0:T(8,128)(2,1)S(1)}, bf16[1,272,128]{2,1,0:T(8,128)(2,1)S(1)}, u32[]{:S(2)}, u32[]{:S(2)}) collective-permute-start(bf16[1,272,128]{2,1,0:T(8,128)(2,1)S(1)} %bitcast.6), channel_id=1, source_target_pairs={{0,5},{1,4},{2,7},{3,6},{4,1},{5,0},{6,3},{7,2},{8,13},{9,12},{10,... | collective-permute-start | bytes 208904 | tf_op jit(solution)/shard_map/ppermute | solution.py:168
  9.0 2.4 %collective-permute-start.5 = (bf16[1,272,128]{2,1,0:T(8,128)(2,1)S(1)}, bf16[1,272,128]{2,1,0:T(8,128)(2,1)S(1)}, u32[]{:S(2)}, u32[]{:S(2)}) collective-permute-start(bf16[1,272,128]{2,1,0:T(8,128)(2,1)S(1)} %collective-permute-done.3.refs_1_), channel_id=1, source_target_pairs={{0,3},{1,2},{2,1},{3,0},{4,7},{5,6},{6,5},{7,4},{8,11},{9,10},{10,... | collective-permute-start | bytes 208904 | tf_op jit(solution)/shard_map/ppermute | solution.py:168
  11.4 0.9 %collective-permute-start.6 = (bf16[1,272,128]{2,1,0:T(8,128)(2,1)S(1)}, bf16[1,272,128]{2,1,0:T(8,128)(2,1)S(1)}, u32[]{:S(2)}, u32[]{:S(2)}) collective-permute-start(bf16[1,272,128]{2,1,0:T(8,128)(2,1)S(1)} %collective-permute-done.3.refs_1_), channel_id=1, source_target_pairs={{0,7},{1,6},{2,5},{3,4},{4,3},{5,2},{6,1},{7,0},{8,15},{9,14},{10,... | collective-permute-start | bytes 208904 | tf_op jit(solution)/shard_map/ppermute | solution.py:168
  12.2 0.5 %collective-permute-done.refs_3_ = bf16[1,272,128]{2,1,0:T(8,128)(2,1)S(1)} collective-permute-done((bf16[1,272,128]{2,1,0:T(8,128)(2,1)S(1)}, bf16[1,272,128]{2,1,0:T(8,128)(2,1)S(1)}, u32[]{:S(2)}, u32[]{:S(2)}) %collective-permute-start) | collective-permute-done | bytes 69664 | tf_op jit(solution)/shard_map/ppermute | solution.py:168
  13.0 1.7 %collective-permute-start.8 = (bf16[1,272,128]{2,1,0:T(8,128)(2,1)S(1)}, bf16[1,272,128]{2,1,0:T(8,128)(2,1)S(1)}, u32[]{:S(2)}, u32[]{:S(2)}) collective-permute-start(bf16[1,272,128]{2,1,0:T(8,128)(2,1)S(1)} %collective-permute-done.3.refs_1_), channel_id=1, source_target_pairs={{0,5},{1,4},{2,7},{3,6},{4,1},{5,0},{6,3},{7,2},{8,13},{9,12},{10,... | collective-permute-start | bytes 208904 | tf_op jit(solution)/shard_map/ppermute | solution.py:168
  14.7 1.6 %score.4 = (f32[8,1,384]{2,1,0:T(1,128)S(1)}, f32[8,1,384]{2,1,0:T(1,128)S(1)}) custom-call(bf16[1,272,128]{2,1,0:T(8,128)(2,1)S(1)} %bitcast.7, bf16[1,272,128]{2,1,0:T(8,128)(2,1)S(1)} %collective-permute-done.3.refs_1_, bf16[1,272,128]{2,1,0:T(8,128)(2,1)S(1)} %collective-permute-done.4.refs_2_, bf16[1,272,128]{2,1,0:T(8,128)(2,1)S(1)} %collective-permute-done.refs_3_, ...), custom_call_target="tpu_custom_call" | custom-call | flops 503316480 | bytes 5242880 | tf_op jit(solution)/shard_map/score/pallas_call | solution.py:174
  16.4 0.4 %collective-permute-start.7 = (bf16[2,272,128]{2,1,0:T(8,128)(2,1)S(1)}, bf16[2,272,128]{2,1,0:T(8,128)(2,1)S(1)}, u32[]{:S(2)}, u32[]{:S(2)}) collective-permute-start(bf16[2,272,128]{2,1,0:T(8,128)(2,1)S(1)} %pad_maximum_fusion.2), channel_id=1, source_target_pairs={{0,1},{1,0},{2,3},{3,2},{4,5},{5,4},{6,7},{7,6},{8,9},{9,8},{10,11... | collective-permute-start | bytes 417800 | tf_op jit(solution)/shard_map/ppermute | solution.py:168
  16.8 1.1 %score.5.refs_5_ = f32[8,1,384]{2,1,0:T(1,128)S(1)} custom-call(bf16[1,272,128]{2,1,0:T(8,128)(2,1)S(1)} %get-tuple-element.20.refs_0_, bf16[1,272,128]{2,1,0:T(8,128)(2,1)S(1)} %collective-permute-done.5.refs_1_, bf16[1,272,128]{2,1,0:T(8,128)(2,1)S(1)} %collective-permute-done.6.refs_2_, ...), custom_call_target="tpu_custom_call", output_to_operand_aliasing={{}: (6, {})} | custom-call | flops 301989888 | bytes 3145728 | tf_op jit(solution)/shard_map/score/pallas_call | solution.py:174
  17.9 1.1 %score.6 = f32[8,1,384]{2,1,0:T(1,128)S(1)} custom-call(bf16[1,272,128]{2,1,0:T(8,128)(2,1)S(1)} %get-tuple-element.21.refs_0_, bf16[2,272,128]{2,1,0:T(8,128)(2,1)S(1)} %collective-permute-done.7.refs_1_, bf16[512,128]{1,0:T(8,128)(2,1)S(1)} %copy-done.1, bf16[128,128,128]{2,1,0:T(8,128)(2,1)S(1)} %copy-done, ...), custom_call_target="tpu_custom_call", output_to_operand_aliasing={{}: (5, {})} | custom-call | flops 301989888 | bytes 3145728 | tf_op jit(solution)/shard_map/score/pallas_call | solution.py:174
  19.0 0.3 %collective-permute-start.9 = (bf16[4,272,128]{2,1,0:T(8,128)(2,1)S(1)}, bf16[4,272,128]{2,1,0:T(8,128)(2,1)S(1)}, u32[]{:S(2)}, u32[]{:S(2)}) collective-permute-start(bf16[4,272,128]{2,1,0:T(8,128)(2,1)S(1)} %pad_maximum_fusion), channel_id=1, source_target_pairs={{0,1},{1,0},{2,3},{3,2},{4,5},{5,4},{6,7},{7,6},{8,9},{9,8},{10,11... | collective-permute-start | bytes 835592 | tf_op jit(solution)/shard_map/ppermute | solution.py:168
  19.3 0.7 %collective-permute-start.10 = (f32[8,1,384]{2,1,0:T(1,128)S(1)}, f32[8,1,384]{2,1,0:T(1,128)S(1)}, u32[]{:S(2)}, u32[]{:S(2)}) collective-permute-start(f32[8,1,384]{2,1,0:T(1,128)S(1)} %score.6), channel_id=1, source_target_pairs={{0,3},{1,2},{2,1},{3,0},{4,7},{5,6},{6,5},{7,4},{8,11},{9,10},{10,... | collective-permute-start | bytes 36872 | tf_op jit(solution)/shard_map/ppermute | solution.py:168
  20.1 0.6 %collective-permute-done.9.refs_1_ = bf16[4,272,128]{2,1,0:T(8,128)(2,1)S(1)} collective-permute-done((bf16[4,272,128]{2,1,0:T(8,128)(2,1)S(1)}, bf16[4,272,128]{2,1,0:T(8,128)(2,1)S(1)}, u32[]{:S(2)}, u32[]{:S(2)}) %collective-permute-start.9) | collective-permute-done | bytes 278560 | tf_op jit(solution)/shard_map/ppermute | solution.py:168
  20.6 1.6 %score.7 = f32[8,1,384]{2,1,0:T(1,128)S(1)} custom-call(bf16[1,272,128]{2,1,0:T(8,128)(2,1)S(1)} %collective-permute-done.8.refs_0_, bf16[4,272,128]{2,1,0:T(8,128)(2,1)S(1)} %collective-permute-done.9.refs_1_, bf16[512,128]{1,0:T(8,128)(2,1)S(1)} %copy-done.1, bf16[128,128,128]{2,1,0:T(8,128)(2,1)S(1)} %copy-done, ...), custom_call_target="tpu_custom_call", output_to_operand_aliasing={{}: (5, {})} | custom-call | flops 503316480 | bytes 5242880 | tf_op jit(solution)/shard_map/score/pallas_call | solution.py:174
  22.2 0.2 collective-permute-done.10
  22.5 1.6 %collective-permute-start.11 = (f32[4,1,384]{2,1,0:T(1,128)S(1)}, f32[4,1,384]{2,1,0:T(1,128)S(1)}, u32[]{:S(2)}, u32[]{:S(2)}) collective-permute-start(f32[4,1,384]{2,1,0:T(1,128)S(1)} %slice.37), channel_id=1, source_target_pairs={{0,9},{1,8},{2,11},{3,10},{4,13},{5,12},{6,15},{7,14},{8,1},{9,0},... | collective-permute-start | bytes 18440 | tf_op jit(solution)/shard_map/ppermute | solution.py:168
  24.1 2.4 %collective-permute-done.11 = f32[4,1,384]{2,1,0:T(1,128)S(1)} collective-permute-done((f32[4,1,384]{2,1,0:T(1,128)S(1)}, f32[4,1,384]{2,1,0:T(1,128)S(1)}, u32[]{:S(2)}, u32[]{:S(2)}) %collective-permute-start.11) | collective-permute-done | bytes 6176 | tf_op jit(solution)/shard_map/ppermute | solution.py:168
  26.5 1.8 %collective-permute-start.12 = (f32[2,1,384]{2,1,0:T(1,128)S(1)}, f32[2,1,384]{2,1,0:T(1,128)S(1)}, u32[]{:S(2)}, u32[]{:S(2)}) collective-permute-start(f32[2,1,384]{2,1,0:T(1,128)S(1)} %slice.39), channel_id=1, source_target_pairs={{0,5},{1,4},{2,7},{3,6},{4,1},{5,0},{6,3},{7,2},{8,13},{9,12},{10,... | collective-permute-start | bytes 9224 | tf_op jit(solution)/shard_map/ppermute | solution.py:168
  28.4 1.3 %collective-permute-done.12 = f32[2,1,384]{2,1,0:T(1,128)S(1)} collective-permute-done((f32[2,1,384]{2,1,0:T(1,128)S(1)}, f32[2,1,384]{2,1,0:T(1,128)S(1)}, u32[]{:S(2)}, u32[]{:S(2)}) %collective-permute-start.12) | collective-permute-done | bytes 3104 | tf_op jit(solution)/shard_map/ppermute | solution.py:168
  29.7 0.3 collective-permute-start.13
  30.0 0.9 %collective-permute-done.13.b_ref = f32[1,1,384]{2,1,0:T(1,128)S(1)} collective-permute-done((f32[1,1,384]{2,1,0:T(1,128)S(1)}, f32[1,1,384]{2,1,0:T(1,128)S(1)}, u32[]{:S(2)}, u32[]{:S(2)}) %collective-permute-start.13) | collective-permute-done | bytes 1568 | tf_op jit(solution)/shard_map/ppermute | solution.py:168
  30.9 0.7 %last.1 = (f32[8,32]{1,0:T(8,128)}, f32[8,16]{1,0:T(8,128)}) custom-call(f32[1,1,384]{2,1,0:T(1,128)S(1)} %get-tuple-element.23.a_ref, f32[1,1,384]{2,1,0:T(1,128)S(1)} %collective-permute-done.13.b_ref), custom_call_target="tpu_custom_call" | custom-call | tf_op jit(solution)/shard_map/last/pallas_call | solution.py:241
  (26 shorter events, 0.4 us)
Async XLA Ops:
  0.6 14.0 %copy-start = (bf16[128,128,128]{2,1,0:T(8,128)(2,1)S(1)}, bf16[128,128,128]{2,1,0:T(8,128)(2,1)}, u32[]{:S(2)}) copy-start(bf16[128,128,128]{2,1,0:T(8,128)(2,1)} %refs_3_.5) | copy-start | bytes 12582916
  0.6 14.0 %copy-start.1 = (bf16[512,128]{1,0:T(8,128)(2,1)S(1)}, bf16[512,128]{1,0:T(8,128)(2,1)}, u32[]{:S(2)}) copy-start(bf16[512,128]{1,0:T(8,128)(2,1)} %refs_2_.3) | copy-start | bytes 393220
  0.7 14.0 %copy-start.2 = (s32[1,128]{1,0:T(1,128)S(1)}, s32[1,128]{1,0:T(1,128)}, u32[]{:S(2)}) copy-start(s32[1,128]{1,0:T(1,128)} %refs_4_.5) | copy-start | bytes 1540
  1.9 7.0 %collective-permute-start.3 = (bf16[1,272,128]{2,1,0:T(8,128)(2,1)S(1)}, bf16[1,272,128]{2,1,0:T(8,128)(2,1)S(1)}, u32[]{:S(2)}, u32[]{:S(2)}) collective-permute-start(bf16[1,272,128]{2,1,0:T(8,128)(2,1)S(1)} %bitcast.3), channel_id=1, source_target_pairs={{0,9},{1,8},{2,11},{3,10},{4,13},{5,12},{6,15},{7,14},{8,1},{9,0},... | collective-permute-start | bytes 208904 | tf_op jit(solution)/shard_map/ppermute | solution.py:168
  5.5 6.7 %collective-permute-start.1 = (bf16[1,272,128]{2,1,0:T(8,128)(2,1)S(1)}, bf16[1,272,128]{2,1,0:T(8,128)(2,1)S(1)}, u32[]{:S(2)}, u32[]{:S(2)}) collective-permute-start(bf16[1,272,128]{2,1,0:T(8,128)(2,1)S(1)} %bitcast.4), channel_id=1, source_target_pairs={{0,7},{1,6},{2,5},{3,4},{4,3},{5,2},{6,1},{7,0},{8,15},{9,14},{10,... | collective-permute-start | bytes 208904 | tf_op jit(solution)/shard_map/ppermute | solution.py:168
  8.3 4.5 %collective-permute-start = (bf16[1,272,128]{2,1,0:T(8,128)(2,1)S(1)}, bf16[1,272,128]{2,1,0:T(8,128)(2,1)S(1)}, u32[]{:S(2)}, u32[]{:S(2)}) collective-permute-start(bf16[1,272,128]{2,1,0:T(8,128)(2,1)S(1)} %bitcast.5), channel_id=1, source_target_pairs={{0,3},{1,2},{2,1},{3,0},{4,7},{5,6},{6,5},{7,4},{8,11},{9,10},{10,... | collective-permute-start | bytes 208904 | tf_op jit(solution)/shard_map/ppermute | solution.py:168
  8.3 6.4 %collective-permute-start.4 = (bf16[1,272,128]{2,1,0:T(8,128)(2,1)S(1)}, bf16[1,272,128]{2,1,0:T(8,128)(2,1)S(1)}, u32[]{:S(2)}, u32[]{:S(2)}) collective-permute-start(bf16[1,272,128]{2,1,0:T(8,128)(2,1)S(1)} %bitcast.6), channel_id=1, source_target_pairs={{0,5},{1,4},{2,7},{3,6},{4,1},{5,0},{6,3},{7,2},{8,13},{9,12},{10,... | collective-permute-start | bytes 208904 | tf_op jit(solution)/shard_map/ppermute | solution.py:168
  9.0 7.3 %collective-permute-start.5 = (bf16[1,272,128]{2,1,0:T(8,128)(2,1)S(1)}, bf16[1,272,128]{2,1,0:T(8,128)(2,1)S(1)}, u32[]{:S(2)}, u32[]{:S(2)}) collective-permute-start(bf16[1,272,128]{2,1,0:T(8,128)(2,1)S(1)} %collective-permute-done.3.refs_1_), channel_id=1, source_target_pairs={{0,3},{1,2},{2,1},{3,0},{4,7},{5,6},{6,5},{7,4},{8,11},{9,10},{10,... | collective-permute-start | bytes 208904 | tf_op jit(solution)/shard_map/ppermute | solution.py:168
  11.4 5.0 %collective-permute-start.6 = (bf16[1,272,128]{2,1,0:T(8,128)(2,1)S(1)}, bf16[1,272,128]{2,1,0:T(8,128)(2,1)S(1)}, u32[]{:S(2)}, u32[]{:S(2)}) collective-permute-start(bf16[1,272,128]{2,1,0:T(8,128)(2,1)S(1)} %collective-permute-done.3.refs_1_), channel_id=1, source_target_pairs={{0,7},{1,6},{2,5},{3,4},{4,3},{5,2},{6,1},{7,0},{8,15},{9,14},{10,... | collective-permute-start | bytes 208904 | tf_op jit(solution)/shard_map/ppermute | solution.py:168
  12.8 4.0 %collective-permute-start.2 = (bf16[2,272,128]{2,1,0:T(8,128)(2,1)S(1)}, bf16[2,272,128]{2,1,0:T(8,128)(2,1)S(1)}, u32[]{:S(2)}, u32[]{:S(2)}) collective-permute-start(bf16[2,272,128]{2,1,0:T(8,128)(2,1)S(1)} %pad_maximum_fusion.1), channel_id=1, source_target_pairs={{0,1},{1,0},{2,3},{3,2},{4,5},{5,4},{6,7},{7,6},{8,9},{9,8},{10,11... | collective-permute-start | bytes 417800 | tf_op jit(solution)/shard_map/ppermute | solution.py:168
  13.0 6.0 %collective-permute-start.8 = (bf16[1,272,128]{2,1,0:T(8,128)(2,1)S(1)}, bf16[1,272,128]{2,1,0:T(8,128)(2,1)S(1)}, u32[]{:S(2)}, u32[]{:S(2)}) collective-permute-start(bf16[1,272,128]{2,1,0:T(8,128)(2,1)S(1)} %collective-permute-done.3.refs_1_), channel_id=1, source_target_pairs={{0,5},{1,4},{2,7},{3,6},{4,1},{5,0},{6,3},{7,2},{8,13},{9,12},{10,... | collective-permute-start | bytes 208904 | tf_op jit(solution)/shard_map/ppermute | solution.py:168
  16.4 1.5 %collective-permute-start.7 = (bf16[2,272,128]{2,1,0:T(8,128)(2,1)S(1)}, bf16[2,272,128]{2,1,0:T(8,128)(2,1)S(1)}, u32[]{:S(2)}, u32[]{:S(2)}) collective-permute-start(bf16[2,272,128]{2,1,0:T(8,128)(2,1)S(1)} %pad_maximum_fusion.2), channel_id=1, source_target_pairs={{0,1},{1,0},{2,3},{3,2},{4,5},{5,4},{6,7},{7,6},{8,9},{9,8},{10,11... | collective-permute-start | bytes 417800 | tf_op jit(solution)/shard_map/ppermute | solution.py:168
  19.0 1.6 %collective-permute-start.9 = (bf16[4,272,128]{2,1,0:T(8,128)(2,1)S(1)}, bf16[4,272,128]{2,1,0:T(8,128)(2,1)S(1)}, u32[]{:S(2)}, u32[]{:S(2)}) collective-permute-start(bf16[4,272,128]{2,1,0:T(8,128)(2,1)S(1)} %pad_maximum_fusion), channel_id=1, source_target_pairs={{0,1},{1,0},{2,3},{3,2},{4,5},{5,4},{6,7},{7,6},{8,9},{9,8},{10,11... | collective-permute-start | bytes 835592 | tf_op jit(solution)/shard_map/ppermute | solution.py:168
  19.3 3.1 %collective-permute-start.10 = (f32[8,1,384]{2,1,0:T(1,128)S(1)}, f32[8,1,384]{2,1,0:T(1,128)S(1)}, u32[]{:S(2)}, u32[]{:S(2)}) collective-permute-start(f32[8,1,384]{2,1,0:T(1,128)S(1)} %score.6), channel_id=1, source_target_pairs={{0,3},{1,2},{2,1},{3,0},{4,7},{5,6},{6,5},{7,4},{8,11},{9,10},{10,... | collective-permute-start | bytes 36872 | tf_op jit(solution)/shard_map/ppermute | solution.py:168
  22.5 4.0 %collective-permute-start.11 = (f32[4,1,384]{2,1,0:T(1,128)S(1)}, f32[4,1,384]{2,1,0:T(1,128)S(1)}, u32[]{:S(2)}, u32[]{:S(2)}) collective-permute-start(f32[4,1,384]{2,1,0:T(1,128)S(1)} %slice.37), channel_id=1, source_target_pairs={{0,9},{1,8},{2,11},{3,10},{4,13},{5,12},{6,15},{7,14},{8,1},{9,0},... | collective-permute-start | bytes 18440 | tf_op jit(solution)/shard_map/ppermute | solution.py:168
  26.5 3.2 %collective-permute-start.12 = (f32[2,1,384]{2,1,0:T(1,128)S(1)}, f32[2,1,384]{2,1,0:T(1,128)S(1)}, u32[]{:S(2)}, u32[]{:S(2)}) collective-permute-start(f32[2,1,384]{2,1,0:T(1,128)S(1)} %slice.39), channel_id=1, source_target_pairs={{0,5},{1,4},{2,7},{3,6},{4,1},{5,0},{6,3},{7,2},{8,13},{9,12},{10,... | collective-permute-start | bytes 9224 | tf_op jit(solution)/shard_map/ppermute | solution.py:168
  29.7 1.2 %collective-permute-start.13 = (f32[1,1,384]{2,1,0:T(1,128)S(1)}, f32[1,1,384]{2,1,0:T(1,128)S(1)}, u32[]{:S(2)}, u32[]{:S(2)}) collective-permute-start(f32[1,1,384]{2,1,0:T(1,128)S(1)} %get-tuple-element.22), channel_id=1, source_target_pairs={{0,1},{1,0},{2,3},{3,2},{4,5},{5,4},{6,7},{7,6},{8,9},{9,8},{10,11... | collective-permute-start | bytes 4616 | tf_op jit(solution)/shard_map/ppermute | solution.py:168
